TPU v7x, 32 devices: a whole 2x2x4 slice. The times are simulated.
32 devices in a mesh: dp: 16 (over z, x, core), ctx: 2 (over y).
Axes of the slice: x: 2, y: 2, z: 4, core: 2. Of those that a mesh axis runs over, the one named last changes fastest.
Arguments:
- tokens: bfloat16 [16384, 1024], P(('dp', 'ctx')), may hold values from -6 to 6
- lengths: int32 [16, 7], P('dp'), may hold values from 1 to 640, as said below
- w_qkv: bfloat16 [1024, 3072], P(('dp', 'ctx')), may hold values from -0.1875 to 0.1875
- w_out: bfloat16 [1024, 1024], P(('dp', 'ctx')), may hold values from -0.1875 to 0.1875
- w_up: bfloat16 [1024, 4096], P(('dp', 'ctx')), may hold values from -0.1875 to 0.1875
- w_down: bfloat16 [4096, 1024], P(('dp', 'ctx')), may hold values from -0.09375 to 0.09375
- gains: bfloat16 [1024, 4], P(('dp', 'ctx')), may hold values from 0.25 to 1.75
- d_out: bfloat16 [16384, 1024], P(('dp', 'ctx')), may hold values from -6 to 6
Outputs:
- output: bfloat16 [16384, 1024], P(('dp', 'ctx'))
- d_tokens: bfloat16 [16384, 1024], P(('dp', 'ctx'))
- grad_qkv: float32 [1024, 3072], P(('dp', 'ctx'))
- grad_out: float32 [1024, 1024], P(('dp', 'ctx'))
- grad_up: float32 [1024, 4096], P(('dp', 'ctx'))
- grad_down: float32 [4096, 1024], P(('dp', 'ctx'))
- grad_gains: float32 [1024, 4], P(('dp', 'ctx'))
Inputs may be any that keep to these rules, and one draw needn't show every extreme that they name: Each row holds 7 positive numbers that sum to 1024: the lengths of 6 documents packed from the row's start, then the length of the padding tail, whose slots hold no token.
All inputs are finite; a program needn't handle non-finite values.
Results may differ from a plain program's by a relative error of at most 0.018.
Values may be sent and summed in bfloat16 or wider, within the bound.
A program may use at most 256 MiB of HBM per device.

v0:
```python
import math

import jax
import jax.numpy as jnp
from jax import lax
from jax.sharding import PartitionSpec as P

HEADS = 16
DOCS = 7


epsilon = 1e-05
masked_score = -1e30


def layer_norm(values, gain_vec):
    center = values - jnp.mean(values, axis=-1, keepdims=True)
    spread = jnp.mean(center * center, axis=-1, keepdims=True)
    return center * lax.rsqrt(spread + epsilon) * gain_vec


def norm_back(values, gain_vec, upstream):
    unused, pullback = jax.vjp(layer_norm, values, gain_vec)
    return pullback(upstream)


def rotate(values, cosine_table, sine_table, direction):
    half_dim = values.shape[-1] // 2
    first_half = values[..., :half_dim]
    second_half = values[..., half_dim:]
    return jnp.concatenate(
        [
            first_half * cosine_table - direction * second_half * sine_table,
            second_half * cosine_table + direction * first_half * sine_table,
        ],
        axis=-1,
    )


def doc_layout(lengths, row_len):
    doc_ends = jnp.cumsum(lengths, axis=-1)
    places = jnp.arange(row_len, dtype=jnp.int32)
    passed = places[None, :, None] >= doc_ends[:, None, :]
    segment = jnp.sum(passed.astype(jnp.int32), axis=-1)
    starts = jnp.sum(jnp.where(passed, lengths[:, None, :], 0), axis=-1)
    position = places[None, :] - starts
    is_valid = places[None, :] < doc_ends[:, DOCS - 2][:, None]
    return (segment[0], position[0], is_valid[0])


def allowed_keys(own_seg, own_place, seg_full, first_key, block_rows):
    key_place = first_key + jnp.arange(block_rows, dtype=jnp.int32)
    key_seg = lax.dynamic_slice_in_dim(seg_full, first_key, block_rows)
    return (own_seg[:, None] == key_seg[None, :]) & (key_place[None, :] <= own_place[:, None])


def make_fold(queries, own_seg, own_place, seg_full, score_scale):

    def fold_piece(fold_state, piece, start):
        key_piece, value_piece = piece
        piece_rows = key_piece.shape[0]
        block_rows = math.gcd(piece_rows, 256)
        block_count = piece_rows // block_rows
        key_blocks = key_piece.reshape((block_count, block_rows) + key_piece.shape[1:])
        value_blocks = value_piece.reshape((block_count, block_rows) + value_piece.shape[1:])

        def step_block(carried, block_items):
            row_max, row_sum, weighted = carried
            key_block, value_block, block_id = block_items
            allowed = allowed_keys(own_seg, own_place, seg_full, block_id * block_rows, block_rows)
            scores = (
                jnp.einsum("qhd,khd->hqk", queries, key_block, preferred_element_type=jnp.float32)
                * score_scale
            )
            scores = jnp.where(allowed[None], scores, masked_score)
            new_max = jnp.maximum(row_max, jnp.max(scores, axis=-1))
            factor = jnp.exp(row_max - new_max)
            shifted = jnp.where(allowed[None], jnp.exp(scores - new_max[..., None]), 0.0)
            row_sum = row_sum * factor + jnp.sum(shifted, axis=-1)
            weighted = weighted * factor[..., None] + jnp.einsum(
                "hqk,khd->hqd",
                shifted.astype(jnp.bfloat16),
                value_block,
                preferred_element_type=jnp.float32,
            )
            return ((new_max, row_sum, weighted), None)

        block_ids = jnp.arange(block_count, dtype=jnp.int32)
        fold_state, unused = lax.scan(step_block, fold_state, (key_blocks, value_blocks, block_ids))
        return fold_state

    return fold_piece


def per_device(tokens, lengths, w_qkv, w_out, w_up, w_down, gains, d_out):
    tok_rows, model_width = tokens.shape
    row_len = tok_rows * lax.axis_size("ctx")
    head_count = HEADS
    head_dim = model_width // head_count
    score_scale = head_dim ** (-0.5)
    head_shape = (tok_rows, head_count, head_dim)
    seg_full, pos_full, valid_full = doc_layout(lengths, row_len)
    offset = lax.axis_index("ctx") * tok_rows
    own_seg = lax.dynamic_slice_in_dim(seg_full, offset, tok_rows)
    own_pos = lax.dynamic_slice_in_dim(pos_full, offset, tok_rows)
    own_valid = lax.dynamic_slice_in_dim(valid_full.astype(jnp.float32), offset, tok_rows)
    own_place = offset + jnp.arange(tok_rows, dtype=jnp.int32)
    freq_index = jnp.arange(head_dim // 2, dtype=jnp.float32)
    angles = own_pos.astype(jnp.float32)[:, None] * 10000.0 ** (-2.0 * freq_index / head_dim)
    cosine_table = jnp.cos(angles)[:, None, :]
    sine_table = jnp.sin(angles)[:, None, :]
    qkv_full, out_full, up_full, down_full, gain_full = (
        lax.all_gather(w_qkv, ("dp", "ctx"), axis=0, tiled=True),
        lax.all_gather(w_out, ("dp", "ctx"), axis=0, tiled=True),
        lax.all_gather(w_up, ("dp", "ctx"), axis=0, tiled=True),
        lax.all_gather(w_down, ("dp", "ctx"), axis=0, tiled=True),
        lax.all_gather(gains, ("dp", "ctx"), axis=0, tiled=True),
    )
    gain_f = gain_full.astype(jnp.float32)
    stream = tokens.astype(jnp.float32)
    normed = layer_norm(stream, gain_f[:, 0]).astype(jnp.bfloat16)
    qkv_raw = jnp.dot(normed, qkv_full, preferred_element_type=jnp.float32)
    queries = rotate(
        qkv_raw[:, :model_width].reshape(head_shape), cosine_table, sine_table, 1.0
    ).astype(jnp.bfloat16)
    key_heads = rotate(
        qkv_raw[:, model_width : 2 * model_width].reshape(head_shape), cosine_table, sine_table, 1.0
    ).astype(jnp.bfloat16)
    value_heads = qkv_raw[:, 2 * model_width :].reshape(head_shape).astype(jnp.bfloat16)
    start_state = (
        jnp.full((head_count, tok_rows), masked_score, jnp.float32),
        jnp.zeros((head_count, tok_rows), jnp.float32),
        jnp.zeros((head_count, tok_rows, head_dim), jnp.float32),
    )
    fold_piece = make_fold(queries, own_seg, own_place, seg_full, score_scale)
    row_max, row_sum, weighted = fold_piece(
        start_state,
        (
            lax.all_gather(key_heads, "ctx", axis=0, tiled=True),
            lax.all_gather(value_heads, "ctx", axis=0, tiled=True),
        ),
        jnp.int32(0),
    )
    attended = jnp.transpose(weighted / row_sum[..., None], (1, 0, 2))
    attended_b = attended.reshape(tok_rows, model_width).astype(jnp.bfloat16)
    attn_raw = jnp.dot(attended_b, out_full, preferred_element_type=jnp.float32)
    hidden = stream + layer_norm(attn_raw, gain_f[:, 1])
    mlp_in = layer_norm(hidden, gain_f[:, 2]).astype(jnp.bfloat16)
    up_proj = jnp.dot(mlp_in, up_full, preferred_element_type=jnp.float32)
    activated = jax.nn.gelu(up_proj).astype(jnp.bfloat16)
    mlp_raw = jnp.dot(activated, down_full, preferred_element_type=jnp.float32)
    result = hidden + layer_norm(mlp_raw, gain_f[:, 3])
    output = (result * own_valid[:, None]).astype(jnp.bfloat16)
    qkv_back, out_back, up_back, down_back = (
        lax.all_gather(w_qkv, ("dp", "ctx"), axis=0, tiled=True),
        lax.all_gather(w_out, ("dp", "ctx"), axis=0, tiled=True),
        lax.all_gather(w_up, ("dp", "ctx"), axis=0, tiled=True),
        lax.all_gather(w_down, ("dp", "ctx"), axis=0, tiled=True),
    )
    upstream = d_out.astype(jnp.float32) * own_valid[:, None]
    d_mlp, d_gain_four = norm_back(mlp_raw, gain_f[:, 3], upstream)
    d_mlp_b = d_mlp.astype(jnp.bfloat16)
    grad_down = jnp.einsum("tf,td->fd", activated, d_mlp_b, preferred_element_type=jnp.float32)
    d_activated = jnp.einsum("td,fd->tf", d_mlp_b, down_back, preferred_element_type=jnp.float32)
    unused, gelu_pull = jax.vjp(jax.nn.gelu, up_proj)
    d_up_b = gelu_pull(d_activated)[0].astype(jnp.bfloat16)
    grad_up = jnp.einsum("td,tf->df", mlp_in, d_up_b, preferred_element_type=jnp.float32)
    d_mlp_in = jnp.einsum("tf,df->td", d_up_b, up_back, preferred_element_type=jnp.float32)
    d_hidden_part, d_gain_three = norm_back(hidden, gain_f[:, 2], d_mlp_in)
    d_hidden = upstream + d_hidden_part
    d_attn, d_gain_two = norm_back(attn_raw, gain_f[:, 1], d_hidden)
    d_attn_b = d_attn.astype(jnp.bfloat16)
    grad_out = jnp.einsum("td,te->de", attended_b, d_attn_b, preferred_element_type=jnp.float32)
    d_attended = (
        jnp.einsum("te,de->td", d_attn_b, out_back, preferred_element_type=jnp.float32)
        .astype(jnp.bfloat16)
        .reshape(head_shape)
    )
    row_dot = jnp.einsum("qhd,qhd->hq", d_attended.astype(jnp.float32), attended)
    key_all, value_all = (
        lax.all_gather(key_heads, "ctx", axis=0, tiled=True),
        lax.all_gather(value_heads, "ctx", axis=0, tiled=True),
    )
    block_rows = math.gcd(row_len, 256)
    block_count = row_len // block_rows
    key_blocks = key_all.reshape((block_count, block_rows) + key_all.shape[1:])
    value_blocks = value_all.reshape((block_count, block_rows) + value_all.shape[1:])

    def back_block(d_queries, block_items):
        key_block, value_block, block_id = block_items
        allowed = allowed_keys(own_seg, own_place, seg_full, block_id * block_rows, block_rows)
        scores = (
            jnp.einsum("qhd,khd->hqk", queries, key_block, preferred_element_type=jnp.float32)
            * score_scale
        )
        attn_prob = jnp.where(
            allowed[None], jnp.exp(scores - row_max[..., None]) / row_sum[..., None], 0.0
        )
        d_prob = jnp.einsum(
            "qhd,khd->hqk", d_attended, value_block, preferred_element_type=jnp.float32
        )
        d_scores = (attn_prob * (d_prob - row_dot[..., None])).astype(jnp.bfloat16)
        d_queries = (
            d_queries
            + jnp.einsum("hqk,khd->qhd", d_scores, key_block, preferred_element_type=jnp.float32)
            * score_scale
        )
        d_keys = (
            jnp.einsum("hqk,qhd->khd", d_scores, queries, preferred_element_type=jnp.float32)
            * score_scale
        )
        d_values = jnp.einsum(
            "hqk,qhd->khd",
            attn_prob.astype(jnp.bfloat16),
            d_attended,
            preferred_element_type=jnp.float32,
        )
        return (d_queries, (d_keys, d_values))

    block_ids = jnp.arange(block_count, dtype=jnp.int32)
    d_queries, (d_keys_all, d_values_all) = lax.scan(
        back_block, jnp.zeros(head_shape, jnp.float32), (key_blocks, value_blocks, block_ids)
    )
    kv_terms = jnp.concatenate(
        [d_keys_all.reshape(row_len, model_width), d_values_all.reshape(row_len, model_width)],
        axis=-1,
    )
    kv_grad = lax.psum_scatter(
        kv_terms.astype(jnp.bfloat16), "ctx", scatter_dimension=0, tiled=True
    ).astype(jnp.float32)
    d_keys = kv_grad[:, :model_width].reshape(head_shape)
    d_qkv = jnp.concatenate(
        [
            rotate(d_queries, cosine_table, sine_table, -1.0).reshape(tok_rows, model_width),
            rotate(d_keys, cosine_table, sine_table, -1.0).reshape(tok_rows, model_width),
            kv_grad[:, model_width:],
        ],
        axis=-1,
    ).astype(jnp.bfloat16)
    grad_qkv = jnp.einsum("td,te->de", normed, d_qkv, preferred_element_type=jnp.float32)
    d_normed = jnp.einsum("te,de->td", d_qkv, qkv_back, preferred_element_type=jnp.float32)
    d_stream_part, d_gain_one = norm_back(stream, gain_f[:, 0], d_normed)
    d_tokens = (d_hidden + d_stream_part).astype(jnp.bfloat16)
    grad_gains = jnp.stack([d_gain_one, d_gain_two, d_gain_three, d_gain_four], axis=-1)
    shard_qkv, shard_out, shard_up, shard_down, shard_gains = (
        lax.psum_scatter(grad_qkv, ("dp", "ctx"), scatter_dimension=0, tiled=True),
        lax.psum_scatter(grad_out, ("dp", "ctx"), scatter_dimension=0, tiled=True),
        lax.psum_scatter(grad_up, ("dp", "ctx"), scatter_dimension=0, tiled=True),
        lax.psum_scatter(grad_down, ("dp", "ctx"), scatter_dimension=0, tiled=True),
        lax.psum_scatter(grad_gains, ("dp", "ctx"), scatter_dimension=0, tiled=True),
    )
    return (output, d_tokens, shard_qkv, shard_out, shard_up, shard_down, shard_gains)


def solution(mesh):
    return jax.shard_map(
        per_device,
        mesh=mesh,
        in_specs=(
            P(("dp", "ctx"), None),
            P("dp", None),
            P(("dp", "ctx"), None),
            P(("dp", "ctx"), None),
            P(("dp", "ctx"), None),
            P(("dp", "ctx"), None),
            P(("dp", "ctx"), None),
            P(("dp", "ctx"), None),
        ),
        out_specs=(
            P(("dp", "ctx"), None),
            P(("dp", "ctx"), None),
            P(("dp", "ctx"), None),
            P(("dp", "ctx"), None),
            P(("dp", "ctx"), None),
            P(("dp", "ctx"), None),
            P(("dp", "ctx"), None),
        ),
        check_vma=False,
    )
```

profile of v0, /device:TPU:0, one launch (start us, length us, event | category | flops | bytes accessed | tf_op | source)
XLA Modules:
  0.0 1762.6 jit_solution(18077323365157604960)
XLA Ops:
  8.0 70.3 %all-gather = bf16[32,32,4]{1,2,0:T(4,128)(2,1)S(1)} all-gather(bf16[1,32,4]{1,2,0:T(4,128)(2,1)} %bitcast.206), channel_id=1, replica_groups=mesh['dp'=16,'ctx'=2] {'dp','ctx'}, dimensions={0}, use_global_device_ids=true | all-gather | bytes 8448 | tf_op jit(solution)/shard_map/all_gather | solution.py:117
  83.5 5.8 fusion.79
  108.1 24.9 %all-gather.10.cloned.1.call-done = bf16[1024,16,64]{0,2,1:T(8,128)(2,1)} async-done(((bf16[512,16,64]{0,2,1:T(8,128)(2,1)}), bf16[1024,16,64]{0,2,1:T(8,128)(2,1)}) %all-gather.10.cloned.1.call-update) | async-done | bytes 2097168 | tf_op jit(solution)/shard_map/all_gather | solution.py:139
  134.9 33.4 %all-gather.12.cloned.1.call-done = bf16[1024,16,64]{0,2,1:T(8,128)(2,1)} async-done(((bf16[512,16,64]{0,2,1:T(8,128)(2,1)}), bf16[1024,16,64]{0,2,1:T(8,128)(2,1)}) %all-gather.12.cloned.1.call-update) | async-done | bytes 2097168 | tf_op jit(solution)/shard_map/all_gather | solution.py:140
  171.5 67.5 %while.30 = (s32[]{:T(128)}, f32[16,512]{1,0:T(8,128)S(1)}, f32[16,512]{1,0:T(8,128)S(1)}, f32[16,512,64]{1,2,0:T(8,128)}, s32[512]{0:T(512)S(1)}, /*index=5*/s3...) while((s32[]{:T(128)}, f32[16,512]{1,0:T(8,128)S(1)}, ...), condition=%wide.region_8.9_spmd.clone, body=%wide.region_5.8_spmd.clone.sunk | while | flops 566141696 | bytes 66072316 | solution.py:89
  249.5 57.6 %all-gather.16.cloned.1.call-done = bf16[1024,4096]{1,0:T(8,128)(2,1)} async-done(((bf16[32,4096]{1,0:T(8,128)(2,1)}), bf16[1024,4096]{1,0:T(8,128)(2,1)}) %all-gather.16.cloned.1.call-update) | async-done | bytes 8388624 | tf_op jit(solution)/shard_map/all_gather | solution.py:115
  307.1 11.9 fusion.83
  319.0 67.1 %all-gather.18.cloned.1.call-done = bf16[4096,1024]{1,0:T(8,128)(2,1)} async-done(((bf16[128,1024]{1,0:T(8,128)(2,1)}), bf16[4096,1024]{1,0:T(8,128)(2,1)}) %all-gather.18.cloned.1.call-update) | async-done | bytes 8388624 | tf_op jit(solution)/shard_map/all_gather | solution.py:116
  386.1 10.7 fusion.93
  401.5 15.6 fusion.50
  417.2 7.2 multiply_reduce_fusion.1
  432.8 89.8 %while.31 = (s32[]{:T(128)}, f32[512,16,64]{0,2,1:T(8,128)}, bf16[4,256,16,64]{1,3,2,0:T(8,128)(2,1)}, bf16[4,256,16,64]{1,3,2,0:T(8,128)(2,1)}, bf16[4,256,16,6...) while((s32[]{:T(128)}, f32[512,16,64]{0,2,1:T(8,128)}, ...), condition=%wide.region_22.23_spmd.clone, body=%wide.region_21.22_spmd.clone.sunk | while | flops 1361183488 | bytes 134068056 | solution.py:221
  467.4 5.4 bitcast_add_fusion.2
  490.0 5.4 bitcast_add_fusion.2
  532.8 53.0 %reduce-scatter.9.cloned.1.call-done = bf16[512,2048]{0,1:T(8,128)(2,1)} async-done(((bf16[1024,2048]{0,1:T(8,128)(2,1)}), bf16[512,2048]{0,1:T(8,128)(2,1)}) %reduce-scatter.9.cloned.1.call-update) | async-done | bytes 2097168 | tf_op jit(solution)/shard_map/reduce_scatter | solution.py:228
  591.3 6.6 fusion.60
  607.9 9.4 fusion.63
  618.9 15.1 fusion.75
  635.6 10.5 fusion.82
  651.2 84.3 %reduce-scatter.19.cloned.1.call-done = f32[32,4]{1,0:T(8,128)} async-done(((f32[1024,4]{1,0:T(8,128)}), f32[32,4]{1,0:T(8,128)}) %reduce-scatter.19.cloned.1.call-update) | async-done | bytes 528
  736.9 138.9 %reduce-scatter.13.cloned.1.call-done = f32[32,1024]{1,0:T(8,128)} async-done(((f32[1024,1024]{1,0:T(8,128)}), f32[32,1024]{1,0:T(8,128)}) %reduce-scatter.13.cloned.1.call-update) | async-done | bytes 131088 | tf_op jit(solution)/shard_map/reduce_scatter | solution.py:247
  875.8 158.7 %reduce-scatter.11.cloned.1.call-done = f32[32,3072]{1,0:T(8,128)} async-done(((f32[1024,3072]{1,0:T(8,128)}), f32[32,3072]{1,0:T(8,128)}) %reduce-scatter.11.cloned.1.call-update) | async-done | bytes 393232 | tf_op jit(solution)/shard_map/reduce_scatter | solution.py:246
  1034.5 359.5 %reduce-scatter.17.cloned.1.call-done = f32[128,1024]{1,0:T(8,128)} async-done(((f32[4096,1024]{1,0:T(8,128)}), f32[128,1024]{1,0:T(8,128)}) %reduce-scatter.17.cloned.1.call-update) | async-done | bytes 524304 | tf_op jit(solution)/shard_map/reduce_scatter | solution.py:249
  1394.0 361.3 %reduce-scatter.15.cloned.1.call-done = f32[32,4096]{1,0:T(8,128)} async-done(((f32[1024,4096]{1,0:T(8,128)}), f32[32,4096]{1,0:T(8,128)}) %reduce-scatter.15.cloned.1.call-update) | async-done | bytes 524304 | tf_op jit(solution)/shard_map/reduce_scatter | solution.py:248
  (314 shorter events, 229.4 us)
Async XLA Ops:
  7.2 74.3 %copy-start.12 = (bf16[512,1024]{1,0:T(8,128)(2,1)S(1)}, bf16[512,1024]{1,0:T(8,128)(2,1)}, u32[]{:S(2)}) copy-start(bf16[512,1024]{1,0:T(8,128)(2,1)} %param.12) | copy-start | bytes 3145732
  7.2 76.3 %all-gather.8.cloned.1.call-start = ((), (), s32[]{:S(2)}) async-start(), calls=%async_computation.6 | async-start | bytes 6488064 | tf_op jit(solution)/shard_map/all_gather | solution.py:113
  7.9 125.1 %all-gather.10.cloned.1.call-start = ((), (), s32[]{:S(2)}) async-start(), calls=%async_computation.7 | async-start | bytes 3145728 | tf_op jit(solution)/shard_map/all_gather | solution.py:139
  82.6 341.9 %copy-start.44 = (f32[1024,1]{0,1:T(1,128)}, f32[1024,1]{0,1:T(1,128)S(1)}, u32[]{:S(2)}) copy-start(f32[1024,1]{0,1:T(1,128)S(1)} %get-tuple-element.463) | copy-start | bytes 12292
  83.5 14.8 copy-start.26
  101.5 66.8 %all-gather.12.cloned.1.call-start = ((), (), s32[]{:S(2)}) async-start(), calls=%async_computation.8 | async-start | bytes 3145728 | tf_op jit(solution)/shard_map/all_gather | solution.py:140
  104.7 138.0 %all-gather.14.cloned.1.call-start = ((), (), s32[]{:S(2)}) async-start(), calls=%async_computation.9 | async-start | bytes 2162688 | tf_op jit(solution)/shard_map/all_gather | solution.py:114
  105.3 201.8 %all-gather.16.cloned.1.call-start = ((), (), s32[]{:S(2)}) async-start(), calls=%async_computation.10 | async-start | bytes 8650752 | tf_op jit(solution)/shard_map/all_gather | solution.py:115
  105.8 280.3 %all-gather.18.cloned.1.call-start = ((), (), s32[]{:S(2)}) async-start(), calls=%async_computation.11 | async-start | bytes 8650752 | tf_op jit(solution)/shard_map/all_gather | solution.py:116
  106.4 479.4 %reduce-scatter.9.cloned.1.call-start = ((), (), s32[]{:S(2)}) async-start(), calls=%async_computation.12 | async-start | bytes 6291456 | tf_op jit(solution)/shard_map/reduce_scatter | solution.py:228
  108.0 318.3 %copy-start.29 = (f32[512]{0:T(512)}, f32[512]{0:T(512)S(1)}, u32[]{:S(2)}) copy-start(f32[512]{0:T(512)S(1)} %dynamic_slice.37) | copy-start | bytes 6148
  247.8 176.6 %copy-start.41 = (f32[512]{0:T(512)}, f32[512]{0:T(512)S(1)}, u32[]{:S(2)}) copy-start(f32[512]{0:T(512)S(1)} %broadcast_multiply_fusion.2) | copy-start | bytes 6148
  249.5 175.0 %copy-start.46 = (f32[512]{0:T(512)}, f32[512]{0:T(512)S(1)}, u32[]{:S(2)}) copy-start(f32[512]{0:T(512)S(1)} %fusion.71) | copy-start | bytes 6148
  399.5 17.7 %slice-start = ((s8[8388608]{0:T(1024)(128)(4,1)}), s8[4194304]{0:T(1024)(128)(4,1)S(1)}, s32[]{:S(2)}) async-start(s8[8388608]{0:T(1024)(128)(4,1)} %bitcast.209), calls=%async_computation.18 | async-start | bytes 8388608
  401.5 15.7 copy-start.20
  401.5 15.7 copy-start.48
  401.5 15.7 slice-start.1
  532.8 202.8 %reduce-scatter.19.cloned.1.call-start = ((), (), s32[]{:S(2)}) async-start(), calls=%async_computation.17 | async-start | bytes 540672
  590.0 7.9 copy-start.23
  591.3 7.9 copy-start.38
  601.4 274.4 %reduce-scatter.13.cloned.1.call-start = ((), (), s32[]{:S(2)}) async-start(), calls=%async_computation.14 | async-start | bytes 4325376 | tf_op jit(solution)/shard_map/reduce_scatter | solution.py:247
  606.7 427.8 %reduce-scatter.11.cloned.1.call-start = ((), (), s32[]{:S(2)}) async-start(), calls=%async_computation.13 | async-start | bytes 12976128 | tf_op jit(solution)/shard_map/reduce_scatter | solution.py:246
  617.3 776.6 %reduce-scatter.17.cloned.1.call-start = ((), (), s32[]{:S(2)}) async-start(), calls=%async_computation.16 | async-start | bytes 17301504 | tf_op jit(solution)/shard_map/reduce_scatter | solution.py:249
  634.0 1121.3 %reduce-scatter.15.cloned.1.call-start = ((), (), s32[]{:S(2)}) async-start(), calls=%async_computation.15 | async-start | bytes 17301504 | tf_op jit(solution)/shard_map/reduce_scatter | solution.py:248
  (52 other events, 177.1 us)
Sparse Core Ops, SparseCore 0:
  10.9 72.2 all-gather.7
  101.6 31.3 all-gather.9
  135.1 33.1 all-gather.11
  171.2 56.4 all-gather.13
  230.7 76.3 all-gather.15
  310.1 75.9 all-gather.17
  532.9 52.9 reduce-scatter.8
  601.5 133.9 reduce-scatter.18
  738.4 137.3 reduce-scatter.12
  882.2 152.2 reduce-scatter.10
  1037.5 356.4 reduce-scatter.16
  1396.8 358.4 reduce-scatter.14
where the time goes:
time: 1770 us; the launch traced here: 1760 us
  waiting for transfers between devices  1340 us (76%)
  matrix products  211 us (12%)
  blocking collectives  70.3 us (4%)
  local copies, waits for them, and re-layouts  68 us (4%)
  other arithmetic  50.3 us (3%)
    reduce_scatter x1, waiting for transfers between devices, per_device(): lax.psum_scatter(grad_up, ('dp', 'ctx'), scatter_dimension=0, tiled=True)  361 us
    reduce_scatter x1, waiting for transfers between devices, per_device(): lax.psum_scatter(grad_down, ('dp', 'ctx'), scatter_dimension=0, tiled=True)  359 us
    reduce_scatter x1, waiting for transfers between devices, per_device(): lax.psum_scatter(grad_qkv, ('dp', 'ctx'), scatter_dimension=0, tiled=True)  159 us
    reduce_scatter x1, waiting for transfers between devices, per_device(): lax.psum_scatter(grad_out, ('dp', 'ctx'), scatter_dimension=0, tiled=True)  139 us
    unnamed x13, waiting for transfers between devices  86.7 us
    all_gather x1, blocking collectives, per_device(): lax.all_gather(gains, ('dp', 'ctx'), axis=0, tiled=True)  70.3 us
    all_gather x1, waiting for transfers between devices, per_device(): lax.all_gather(w_down, ('dp', 'ctx'), axis=0, tiled=True)  67.1 us
    all_gather x1, waiting for transfers between devices, per_device(): lax.all_gather(w_up, ('dp', 'ctx'), axis=0, tiled=True)  57.6 us
  transfers between devices with their start and end apart: 12, of which 10 were waited for; matrix products, arithmetic and copies ran while one was open for 8% of the time, Pallas kernels for 0%

commit v1 on v0

--- a/solution.py
+++ b/solution.py
@@ -4,6 +4,460 @@
 import jax.numpy as jnp
 from jax import lax
 from jax.sharding import PartitionSpec as P
+
+import functools
+from jax.experimental import pallas as pl
+from jax.experimental.pallas import tpu as pltpu
+
+MESH = pl.DeviceIdType.MESH
+
+
+class Place:
+    def __init__(self, dp_size):
+        dp = lax.axis_index("dp")
+        self.Z = dp_size // 4
+        self.z = lax.div(dp, 4)
+        self.x = lax.rem(lax.div(dp, 2), 2)
+        self.c = lax.rem(dp, 2)
+        self.y = lax.axis_index("ctx")
+        c, x, y = self.c, self.x, self.y
+        self.i2 = y * (1 - c) + x * c
+        self.i3 = x * (1 - c) + y * c
+        self.sib = self.device(self.z, x, 1 - c, y)
+        self.p2 = self.device(self.z, x * (1 - c) + (1 - x) * c, c, (1 - y) * (1 - c) + y * c)
+        self.p3 = self.device(self.z, (1 - x) * (1 - c) + x * c, c, y * (1 - c) + (1 - y) * c)
+
+    def device(self, z, x, c, y):
+        return ((z * 2 + x) * 2 + c, y)
+
+    def at_z(self, z):
+        return self.device(z, self.x, self.c, self.y)
+
+    def block(self, z, a2, a3):
+        c = self.c
+        return (z * 2 + a3 * (1 - c) + a2 * c) * 2 + a2 * (1 - c) + a3 * c
+
+    def row_block(self, z, a2, a3, core):
+        c = self.c
+        xx = a3 * (1 - c) + a2 * c
+        yy = a2 * (1 - c) + a3 * c
+        return ((z * 2 + xx) * 2 + core) * 2 + yy
+
+    def barrier(self):
+        bar = pltpu.get_barrier_semaphore()
+        for device in (self.sib, self.p2, self.p3):
+            pl.semaphore_signal(bar, 1, device_id=device, device_id_type=MESH)
+        for k in range(1, self.Z):
+            pl.semaphore_signal(
+                bar, 1, device_id=self.at_z(lax.rem(self.z + k, self.Z)), device_id_type=MESH
+            )
+        pl.semaphore_wait(bar, 3 + self.Z - 1)
+
+
+class Gather:
+    def __init__(self, place, shard, full, send, recv, by_z):
+        self.g, self.shard, self.full = place, shard, full
+        self.send, self.recv = send, recv
+        self.rows = shard.shape[0]
+        self.by_z = by_z
+        Z = place.Z
+        self.n_z = 0
+        self.n_p2 = 2 * (Z - 1)
+        self.n_p3 = self.n_p2 + Z
+        self.n_sib = self.n_p3 + 2 * Z
+        self.n_own = self.n_sib + 4 * Z
+        self.count = self.n_own + 1
+
+    @staticmethod
+    def sems(Z):
+        return 2 * (Z - 1) + Z + 2 * Z + 4 * Z + 1
+
+    def at(self, index):
+        return self.full.at[pl.ds(pl.multiple_of(index * self.rows, self.rows), self.rows)]
+
+    def copy(self, index, number, device, src=None):
+        return pltpu.make_async_remote_copy(
+            src_ref=self.at(index) if src is None else src,
+            dst_ref=self.at(index),
+            send_sem=self.send.at[number],
+            recv_sem=self.recv.at[number],
+            device_id=device,
+            device_id_type=MESH,
+        )
+
+    def own_copy(self):
+        g = self.g
+        index = g.row_block(g.z, g.i2, g.i3, g.c)
+        return pltpu.make_async_copy(self.shard, self.at(index), self.recv.at[self.n_own])
+
+    def z_copy(self, z, a2_is_other, k, src=None):
+        g = self.g
+        a2 = (1 - g.i2) if a2_is_other else g.i2
+        index = g.row_block(z, a2, g.i3, g.c)
+        to = lax.rem(g.z + k, g.Z)
+        return self.copy(index, self.n_z + (k - 1) * 2 + int(a2_is_other), g.at_z(to), src)
+
+    def p2_copy(self, z, src=None):
+        g = self.g
+        return self.copy(g.row_block(z, g.i2, g.i3, g.c), self.n_p2 + z, g.p2, src)
+
+    def p3_copy(self, z, a2, src=None):
+        g = self.g
+        return self.copy(g.row_block(z, a2, g.i3, g.c), self.n_p3 + z * 2 + a2, g.p3, src)
+
+    def sib_copy(self, z, a2, a3, src=None):
+        g = self.g
+        number = self.n_sib + g.block(z, a2, a3)
+        return self.copy(g.row_block(z, a2, a3, g.c), number, g.sib, src)
+
+    def wait(self, number, index):
+        self.copy(index, number, self.g.sib).wait_recv()
+
+    def start(self):
+        g, src = self.g, self.shard
+        self.own_copy().start()
+        self.p2_copy(g.z, src).start()
+        self.p3_copy(g.z, g.i2, src).start()
+        for k in range(1, g.Z):
+            self.z_copy(g.z, False, k, src).start()
+        self.sib_copy(g.z, g.i2, g.i3, src).start()
+
+    def arrived_p2(self, z):
+        g = self.g
+        o2 = 1 - g.i2
+        self.wait(self.n_p2 + z, g.row_block(z, o2, g.i3, g.c))
+        self.p3_copy(z, o2).start()
+        self.sib_copy(z, o2, g.i3).start()
+
+    def first_p2(self):
+        g = self.g
+        self.arrived_p2(g.z)
+        if self.by_z:
+            for k in range(1, g.Z):
+                self.z_copy(g.z, True, k).start()
+
+    def arrived_z(self, k):
+        g = self.g
+        z = lax.rem(g.z - k + g.Z, g.Z)
+        for other in ((False, True) if self.by_z else (False,)):
+            a2 = (1 - g.i2) if other else g.i2
+            self.wait(self.n_z + (k - 1) * 2 + int(other), g.row_block(z, a2, g.i3, g.c))
+            if not self.by_z:
+                self.p2_copy(z).start()
+            self.p3_copy(z, a2).start()
+            self.sib_copy(z, a2, g.i3).start()
+
+    def later_p2(self, k):
+        if not self.by_z:
+            self.arrived_p2(lax.rem(self.g.z + k, self.g.Z))
+
+    def arrived_p3(self, k):
+        g = self.g
+        z = lax.rem(g.z + k, g.Z)
+        for a2 in (0, 1):
+            self.wait(self.n_p3 + z * 2 + a2, g.row_block(z, a2, 1 - g.i3, g.c))
+            self.sib_copy(z, a2, 1 - g.i3).start()
+
+    def arrived_sib(self, z):
+        g = self.g
+        for xx in (0, 1):
+            for yy in (0, 1):
+                number = self.n_sib + (z * 2 + xx) * 2 + yy
+                self.wait(number, ((z * 2 + xx) * 2 + 1 - g.c) * 2 + yy)
+
+    def own_here(self):
+        self.own_copy().wait()
+
+    def sent(self):
+        g, src = self.g, self.shard
+        self.p2_copy(g.z, src).wait_send()
+        self.p3_copy(g.z, g.i2, src).wait_send()
+        self.sib_copy(g.z, g.i2, g.i3, src).wait_send()
+        for k in range(1, g.Z):
+            self.z_copy(g.z, False, k, src).wait_send()
+            if self.by_z:
+                self.z_copy(g.z, True, k).wait_send()
+            z = lax.rem(g.z + k, g.Z)
+            if not self.by_z:
+                self.p2_copy(z).wait_send()
+            self.p3_copy(z, g.i2).wait_send()
+            self.sib_copy(z, g.i2, g.i3).wait_send()
+        for k in range(g.Z):
+            z = lax.rem(g.z + k, g.Z)
+            self.p3_copy(z, 1 - g.i2).wait_send()
+            self.sib_copy(z, 1 - g.i2, g.i3).wait_send()
+            for a2 in (0, 1):
+                self.sib_copy(z, a2, 1 - g.i3).wait_send()
+
+
+def gather_kernel(dp_size, by_z, n, *refs):
+    shards, fulls = refs[:n], refs[n : 2 * n]
+    sends, recvs = refs[2 * n : 3 * n], refs[3 * n : 4 * n]
+    g = Place(dp_size)
+    g.barrier()
+    ms = [
+        Gather(g, shards[i], fulls[i], sends[i], recvs[i], by_z[i]) for i in range(n)
+    ]
+    for m in ms:
+        m.start()
+    for m in ms:
+        m.first_p2()
+        for k in range(1, g.Z):
+            m.arrived_z(k)
+        for k in range(1, g.Z):
+            m.later_p2(k)
+        for k in range(g.Z):
+            m.arrived_p3(k)
+    for m in ms:
+        for z in range(g.Z):
+            m.arrived_sib(z)
+        m.own_here()
+    for m in ms:
+        m.sent()
+
+
+def gather_all(shards, by_z):
+    dp_size = lax.axis_size("dp")
+    devices = dp_size * lax.axis_size("ctx")
+    n = len(shards)
+    any_spec = pl.BlockSpec(memory_space=pl.ANY)
+    return pl.pallas_call(
+        functools.partial(gather_kernel, dp_size, by_z, n),
+        out_shape=[jax.ShapeDtypeStruct((s.shape[0] * devices, s.shape[1]), s.dtype) for s in shards],
+        in_specs=[any_spec] * n,
+        out_specs=[any_spec] * n,
+        scratch_shapes=[pltpu.SemaphoreType.DMA((Gather.sems(dp_size // 4),))] * (2 * n),
+        compiler_params=pltpu.CompilerParams(
+            collective_id=0, has_side_effects=True, vmem_limit_bytes=16 * 2**20
+        ),
+    )(*shards)
+
+
+class Scatter:
+    def __init__(self, place, part, rec3, rec2, recz, out, send, recv, by_z):
+        self.g = place
+        self.part, self.rec3, self.rec2, self.recz, self.out = part, rec3, rec2, recz, out
+        self.send, self.recv, self.by_z = send, recv, by_z
+        Z = place.Z
+        self.n_p3, self.n_z, self.n_p2 = 0, 2 * Z, 2 * Z + 2 * (Z - 1)
+
+    @staticmethod
+    def sems(Z):
+        return 2 * Z + 2 * (Z - 1) + Z
+
+    def copy(self, src, dst, number, device):
+        return pltpu.make_async_remote_copy(
+            src_ref=src,
+            dst_ref=dst,
+            send_sem=self.send.at[number],
+            recv_sem=self.recv.at[number],
+            device_id=device,
+            device_id_type=MESH,
+        )
+
+    def p3_copy(self, z, a2):
+        g = self.g
+        slot = z * 2 + a2
+        return self.copy(
+            self.part.at[g.block(z, a2, 1 - g.i3)], self.rec3.at[slot], self.n_p3 + slot, g.p3
+        )
+
+    def z_copy(self, k, a2):
+        g = self.g
+        z = lax.rem(g.z + k, g.Z)
+        if self.by_z:
+            slot = (k - 1) * 2 + a2
+        else:
+            slot = k - 1
+        return self.copy(
+            self.part.at[g.block(z, a2, g.i3)], self.recz.at[slot], self.n_z + slot, g.at_z(z)
+        )
+
+    def p2_copy(self, z):
+        g = self.g
+        slot = 0 if self.by_z else z
+        return self.copy(
+            self.part.at[g.block(z, 1 - g.i2, g.i3)], self.rec2.at[slot], self.n_p2 + slot, g.p2
+        )
+
+    def start(self, z, a2):
+        self.p3_copy(z, a2).start()
+
+    def add3(self, k, a2):
+        g = self.g
+        z = lax.rem(g.z + k, g.Z)
+        self.p3_copy(z, a2).wait_recv()
+        block = g.block(z, a2, g.i3)
+        total = self.part[block].astype(jnp.float32) + self.rec3[z * 2 + a2].astype(jnp.float32)
+        self.part[block] = total.astype(jnp.bfloat16)
+        if self.by_z and k > 0:
+            self.z_copy(k, a2).start()
+
+    def stage3(self, k):
+        g = self.g
+        if self.by_z:
+            for a2 in (0, 1):
+                self.add3(k, a2)
+        else:
+            self.add3(k, 1 - g.i2)
+            self.p2_copy(lax.rem(g.z + k, g.Z)).start()
+            self.add3(k, g.i2)
+
+    def stage2(self, k):
+        g = self.g
+        z = lax.rem(g.z + k, g.Z)
+        self.p2_copy(z).wait_recv()
+        block = g.block(z, g.i2, g.i3)
+        total = self.part[block].astype(jnp.float32) + self.rec2[z].astype(jnp.float32)
+        if k > 0:
+            self.part[block] = total.astype(jnp.bfloat16)
+            self.z_copy(k, g.i2).start()
+        else:
+            self.out[...] = total
+
+    def last_z(self):
+        g = self.g
+        for k in range(1, g.Z):
+            self.z_copy(k, g.i2).wait_recv()
+            self.out[...] += self.recz[k - 1].astype(jnp.float32)
+
+    def sum_z(self):
+        g = self.g
+        block = g.block(g.z, 1 - g.i2, g.i3)
+        total = self.part[block].astype(jnp.float32)
+        for k in range(1, g.Z):
+            self.z_copy(k, 1 - g.i2).wait_recv()
+            total += self.recz[(k - 1) * 2 + 1 - g.i2].astype(jnp.float32)
+        self.part[block] = total.astype(jnp.bfloat16)
+        self.p2_copy(g.z).start()
+        total = self.part[g.block(g.z, g.i2, g.i3)].astype(jnp.float32)
+        for k in range(1, g.Z):
+            self.z_copy(k, g.i2).wait_recv()
+            total += self.recz[(k - 1) * 2 + g.i2].astype(jnp.float32)
+        self.out[...] = total
+
+    def last_p2(self):
+        self.p2_copy(self.g.z).wait_recv()
+        self.out[...] += self.rec2[0].astype(jnp.float32)
+
+    def sent(self):
+        g = self.g
+        for z in range(g.Z):
+            for a2 in (0, 1):
+                self.p3_copy(z, a2).wait_send()
+        for k in range(1, g.Z):
+            if self.by_z:
+                self.z_copy(k, 0).wait_send()
+                self.z_copy(k, 1).wait_send()
+            else:
+                self.z_copy(k, g.i2).wait_send()
+        if self.by_z:
+            self.p2_copy(g.z).wait_send()
+        else:
+            for z in range(g.Z):
+                self.p2_copy(z).wait_send()
+
+
+def scatter_kernel(dp_size, by_z, n, *refs):
+    grads, outs = refs[:n], refs[n : 2 * n]
+    scr = refs[2 * n :]
+    g = Place(dp_size)
+    Z = g.Z
+    g.barrier()
+    ms = []
+    sibs = []
+    for i in range(n):
+        part, rsib, rec3, rec2, recz, send, recv, ssend, srecv, slocal = scr[10 * i : 10 * i + 10]
+        ms.append(Scatter(g, part, rec3, rec2, recz, outs[i], send, recv, by_z[i]))
+        sibs.append((grads[i], part, rsib, ssend, srecv, slocal))
+
+    def sib_copy(s, q):
+        grad, part, rsib, ssend, srecv, slocal = s
+        return pltpu.make_async_remote_copy(
+            src_ref=grad.at[2 * q + 1 - g.c],
+            dst_ref=rsib.at[q],
+            send_sem=ssend.at[q],
+            recv_sem=srecv.at[q],
+            device_id=g.sib,
+            device_id_type=MESH,
+        )
+
+    def loc_copy(s, q):
+        grad, part, rsib, ssend, srecv, slocal = s
+        return pltpu.make_async_copy(grad.at[2 * q + g.c], part.at[pl.ds(2 * q, 2)], slocal.at[q])
+
+    for s in sibs:
+        for q in range(2 * Z):
+            sib_copy(s, q).start()
+            loc_copy(s, q).start()
+    for s, m in zip(sibs, ms):
+        for q in range(2 * Z):
+            sib_copy(s, q).wait_recv()
+            loc_copy(s, q).wait()
+            for j in (0, 1):
+                part, rsib = s[1], s[2]
+                part[2 * q + j] = (
+                    part[2 * q + j].astype(jnp.float32) + rsib[q, j].astype(jnp.float32)
+                ).astype(jnp.bfloat16)
+        for z in range(Z):
+            for a2 in (0, 1):
+                m.start(z, a2)
+    for m in ms:
+        for k in range(1, Z):
+            m.stage3(k)
+        m.stage3(0)
+    for m in ms:
+        if not m.by_z:
+            for k in range(1, Z):
+                m.stage2(k)
+            m.stage2(0)
+    for m in ms:
+        if m.by_z:
+            m.sum_z()
+    for m in ms:
+        if m.by_z:
+            m.last_p2()
+        else:
+            m.last_z()
+    for s, m in zip(sibs, ms):
+        m.sent()
+        for q in range(2 * Z):
+            sib_copy(s, q).wait_send()
+
+
+def scatter_all(grads, by_z):
+    dp_size = lax.axis_size("dp")
+    Z = dp_size // 4
+    n = len(grads)
+    scratch, outs, views = [], [], []
+    for grad, z_first in zip(grads, by_z):
+        rows, cols = grad.shape[0] // (8 * Z), grad.shape[1]
+        bf = jnp.bfloat16
+        scratch += [
+            pltpu.VMEM((4 * Z, rows, cols), bf),
+            pltpu.VMEM((2 * Z, 2, rows, cols), bf),
+            pltpu.VMEM((2 * Z, rows, cols), bf),
+            pltpu.VMEM((1 if z_first else Z, rows, cols), bf),
+            pltpu.VMEM(((2 if z_first else 1) * (Z - 1), rows, cols), bf),
+            pltpu.SemaphoreType.DMA((Scatter.sems(Z),)),
+            pltpu.SemaphoreType.DMA((Scatter.sems(Z),)),
+            pltpu.SemaphoreType.DMA((2 * Z,)),
+            pltpu.SemaphoreType.DMA((2 * Z,)),
+            pltpu.SemaphoreType.DMA((2 * Z,)),
+        ]
+        outs.append(jax.ShapeDtypeStruct((rows, cols), jnp.float32))
+        views.append(grad.reshape(4 * Z, 2, rows, cols))
+    return pl.pallas_call(
+        functools.partial(scatter_kernel, dp_size, by_z, n),
+        out_shape=outs,
+        in_specs=[pl.BlockSpec(memory_space=pl.ANY)] * n,
+        out_specs=[pl.BlockSpec(memory_space=pltpu.VMEM)] * n,
+        scratch_shapes=scratch,
+        compiler_params=pltpu.CompilerParams(
+            collective_id=1, has_side_effects=True, vmem_limit_bytes=60 * 2**20
+        ),
+    )(*views)
+
 
 HEADS = 16
 DOCS = 7
@@ -109,13 +563,11 @@
     angles = own_pos.astype(jnp.float32)[:, None] * 10000.0 ** (-2.0 * freq_index / head_dim)
     cosine_table = jnp.cos(angles)[:, None, :]
     sine_table = jnp.sin(angles)[:, None, :]
-    qkv_full, out_full, up_full, down_full, gain_full = (
-        lax.all_gather(w_qkv, ("dp", "ctx"), axis=0, tiled=True),
-        lax.all_gather(w_out, ("dp", "ctx"), axis=0, tiled=True),
-        lax.all_gather(w_up, ("dp", "ctx"), axis=0, tiled=True),
-        lax.all_gather(w_down, ("dp", "ctx"), axis=0, tiled=True),
-        lax.all_gather(gains, ("dp", "ctx"), axis=0, tiled=True),
-    )
+    gains_wide = jnp.pad(gains, ((0, 0), (0, 128 - gains.shape[1])))
+    gain_full, qkv_full, out_full, up_full, down_full = gather_all(
+        (gains_wide, w_qkv, w_out, w_up, w_down), (False, True, True, False, False)
+    )
+    gain_full = gain_full[:, : gains.shape[1]]
     gain_f = gain_full.astype(jnp.float32)
     stream = tokens.astype(jnp.float32)
     normed = layer_norm(stream, gain_f[:, 0]).astype(jnp.bfloat16)
@@ -151,12 +603,7 @@
     mlp_raw = jnp.dot(activated, down_full, preferred_element_type=jnp.float32)
     result = hidden + layer_norm(mlp_raw, gain_f[:, 3])
     output = (result * own_valid[:, None]).astype(jnp.bfloat16)
-    qkv_back, out_back, up_back, down_back = (
-        lax.all_gather(w_qkv, ("dp", "ctx"), axis=0, tiled=True),
-        lax.all_gather(w_out, ("dp", "ctx"), axis=0, tiled=True),
-        lax.all_gather(w_up, ("dp", "ctx"), axis=0, tiled=True),
-        lax.all_gather(w_down, ("dp", "ctx"), axis=0, tiled=True),
-    )
+    qkv_back, out_back, up_back, down_back = (qkv_full, out_full, up_full, down_full)
     upstream = d_out.astype(jnp.float32) * own_valid[:, None]
     d_mlp, d_gain_four = norm_back(mlp_raw, gain_f[:, 3], upstream)
     d_mlp_b = d_mlp.astype(jnp.bfloat16)
@@ -242,13 +689,12 @@
     d_stream_part, d_gain_one = norm_back(stream, gain_f[:, 0], d_normed)
     d_tokens = (d_hidden + d_stream_part).astype(jnp.bfloat16)
     grad_gains = jnp.stack([d_gain_one, d_gain_two, d_gain_three, d_gain_four], axis=-1)
-    shard_qkv, shard_out, shard_up, shard_down, shard_gains = (
-        lax.psum_scatter(grad_qkv, ("dp", "ctx"), scatter_dimension=0, tiled=True),
-        lax.psum_scatter(grad_out, ("dp", "ctx"), scatter_dimension=0, tiled=True),
-        lax.psum_scatter(grad_up, ("dp", "ctx"), scatter_dimension=0, tiled=True),
-        lax.psum_scatter(grad_down, ("dp", "ctx"), scatter_dimension=0, tiled=True),
-        lax.psum_scatter(grad_gains, ("dp", "ctx"), scatter_dimension=0, tiled=True),
-    )
+    grad_gains = jnp.pad(grad_gains, ((0, 0), (0, 128 - gains.shape[1])))
+    shard_down, shard_up, shard_out, shard_qkv, shard_gains = scatter_all(
+        [v.astype(jnp.bfloat16) for v in (grad_down, grad_up, grad_out, grad_qkv, grad_gains)],
+        (False, False, True, True, False),
+    )
+    shard_gains = shard_gains[:, : gains.shape[1]]
     return (output, d_tokens, shard_qkv, shard_out, shard_up, shard_down, shard_gains)
 
 

time: 1770 us -> 797 us (0.45)
  waiting for transfers between devices: 1340 us -> 90.1 us
  Pallas kernels: 0 us -> 354 us
  blocking collectives: 70.3 us -> 0 us
  matrix products: 211 us -> 189 us
    reduce_scatter x4 -> x0, waiting for transfers between devices: 1020 us -> none  [the longest x1 361 us: per_device(): lax.psum_scatter(grad_up, ('dp', 'ctx'), scatter_dimension=0, tiled=True)]
    pallas_call x0 -> x2, Pallas kernels: none -> 354 us  [the longest x1 180 us: gather_all(): pl.pallas_call(functools.partial(gather_kernel, dp_size, by_z, n), out_sh...]
    all_gather x4 -> x0, waiting for transfers between devices: 125 us -> none  [the longest x1 67.1 us: per_device(): lax.all_gather(w_down, ('dp', 'ctx'), axis=0, tiled=True)]
    unnamed x13 -> x3, waiting for transfers between devices: 86.7 us -> 0.05 us
    all_gather x1 -> x0, blocking collectives: 70.3 us -> none  [per_device(): lax.all_gather(gains, ('dp', 'ctx'), axis=0, tiled=True)]
    reduce_scatter x1, waiting for transfers between devices: 53 us -> 33.2 us  [per_device(): lax.psum_scatter(kv_terms.astype(jnp.bfloat16), 'ctx', scatter_dimension=...]
  transfers between devices with their start and end apart: 12 -> 3, of which waited for: 10 -> 3; matrix products, arithmetic and copies ran while one was open for 8% -> 4% of each run, Pallas kernels for 0% -> 0%
where the time goes in v1:
time: 797 us; the launch traced here: 786 us
  Pallas kernels  354 us (44%)
  matrix products  189 us (24%)
  waiting for transfers between devices  90.1 us (11%)
  local copies, waits for them, and re-layouts  81.5 us (10%)
  other arithmetic  49.9 us (6%)
  between operations  14.9 us (2%)
    pallas_call x1, Pallas kernels, gather_all(): pl.pallas_call(functools.partial(gather_kernel, dp_size, by_z, n), out_sh...  180 us
    pallas_call x1, Pallas kernels, scatter_all(): pl.pallas_call(functools.partial(scatter_kernel, dp_size, by_z, n), out_s...  175 us
    reduce_scatter x1, waiting for transfers between devices, per_device(): lax.psum_scatter(kv_terms.astype(jnp.bfloat16), 'ctx', scatter_dimension=...  33.2 us
    all_gather x1, waiting for transfers between devices, per_device(): lax.all_gather(value_heads, 'ctx', axis=0, tiled=True)  32 us
    unnamed x127, local copies, waits for them, and re-layouts  28.4 us
    all_gather x1, waiting for transfers between devices, per_device(): lax.all_gather(key_heads, 'ctx', axis=0, tiled=True)  24.9 us
    dot_general x4, matrix products, step_block(): jnp.einsum('qhd,khd->hqk', queries, key_block, preferred_element_type=jnp...  23.2 us
    dot_general x4, matrix products, back_block(): jnp.einsum('hqk,khd->qhd', d_scores, key_block, preferred_element_type=jn...  20.6 us
  transfers between devices with their start and end apart: 3, of which 3 were waited for; matrix products, arithmetic and copies ran while one was open for 4% of the time, Pallas kernels for 0%

profile of v1, /device:TPU:0, one launch (start us, length us, event | category | flops | bytes accessed | tf_op | source)
XLA Modules:
  0.0 785.6 jit_solution(8584939153547256494)
XLA Ops:
  11.7 179.5 %shard_map.135 = (bf16[1024,128]{1,0:T(8,128)(2,1)S(1)}, bf16[1024,3072]{1,0:T(8,128)(2,1)S(1)}, bf16[1024,1024]{1,0:T(8,128)(2,1)S(1)}, bf16[1024,4096]{1,0:T(8,128)(2,1)S(1)}, bf16[4096,1024]{1,0:T(8,128)(2,1)S(1)}) custom-call(bf16[32,128]{1,0:T(8,128)(2,1)S(1)} %pad.9.refs_0_, bf16[32,3072]{1,0:T(8,128)(2,1)S(1)} %copy-done.2, ...), custom_call_target="tpu_custom_call" | custom-call | tf_op jit(solution)/shard_map/pallas_call | solution.py:224
  225.5 24.9 %all-gather.3.cloned.1.call-done = bf16[1024,16,64]{0,2,1:T(8,128)(2,1)} async-done(((bf16[512,16,64]{0,2,1:T(8,128)(2,1)}), bf16[1024,16,64]{0,2,1:T(8,128)(2,1)}) %all-gather.3.cloned.1.call-update) | async-done | bytes 2097168 | tf_op jit(solution)/shard_map/all_gather | solution.py:591
  253.6 32.0 %all-gather.5.cloned.1.call-done = bf16[1024,16,64]{0,2,1:T(8,128)(2,1)} async-done(((bf16[512,16,64]{0,2,1:T(8,128)(2,1)}), bf16[1024,16,64]{0,2,1:T(8,128)(2,1)}) %all-gather.5.cloned.1.call-update) | async-done | bytes 2097168 | tf_op jit(solution)/shard_map/all_gather | solution.py:592
  288.9 71.6 %while.30 = (s32[]{:T(128)}, f32[16,512]{1,0:T(8,128)S(1)}, f32[16,512]{1,0:T(8,128)S(1)}, f32[16,512,64]{1,2,0:T(8,128)}, s32[512]{0:T(512)S(1)}, /*index=5*/s3...) while((s32[]{:T(128)}, f32[16,512]{1,0:T(8,128)S(1)}, ...), condition=%wide.region_8.9_spmd.clone, body=%wide.region_5.8_spmd.clone.sunk | while | flops 566141696 | bytes 66072824 | solution.py:543
  290.4 5.8 fusion.131
  308.1 5.8 fusion.131
  319.7 4.8 fusion.134
  326.1 5.8 fusion.131
  337.7 4.8 fusion.134
  344.0 5.8 fusion.131
  355.7 4.8 fusion.134
  368.5 7.0 fusion.79
  375.4 8.4 %fusion.88 = (f32[512]{0:T(512)S(1)}, f32[512,1024]{1,0:T(8,128)S(1)}) fusion(bf16[4096,1024]{1,0:T(8,128)(2,1)S(1)} %bitcast.164, f32[512,4096]{1,0:T(8,128)} %fusion.79), kind=kOutput, calls=%fused_computation.174 | convolution fusion | flops 4314365440 | bytes 18876416 | tf_op jit(solution)/shard_map/dot_general | solution.py:603
  389.2 13.5 %fusion.50 = bf16[512,4096]{1,0:T(8,128)(2,1)} fusion(f32[512,4096]{1,0:T(8,128)} %fusion.79, bf16[4096,1024]{1,0:T(8,128)(2,1)S(1)} %bitcast.164, f32[512,1024]{1,0:T(8,128)} %get-tuple-element.433, f32[512]{0:T(512)S(1)} %negate_multiply_fusion.3), kind=kOutput, calls=%fused_computation.59 | convolution fusion | flops 4337958912 | bytes 23070720 | tf_op jit(solution)/shard_map/td,fd->tf/dot_general | solution.py:611
  402.7 7.9 %multiply_reduce_fusion.1 = (bf16[1024]{0:T(1024)(128)(2,1)S(1)}, f32[512]{0:T(512)S(1)}, f32[512,1024]{1,0:T(8,128)S(1)}) fusion(f32[512,1024]{1,0:T(8,128)} %copy-done.18, f32[512]{0:T(512)S(1)} %fusion.70, f32[512]{0:T(512)S(1)} %broadcast_multiply_fusion.2, f32[1024]{0:T(1024)S(1)} %get-tuple-element.369, bf16[512,4096]{1,0:T(8,128)(2,1)} %fusion.50, ...), kind=kOutput, calls=%fused_computation.90 | convolution fusion | flops 4298635776 | bytes 16789504 | tf_op jit(solution)/shard_map/tf,df->td/dot_general | solution.py:615
  420.3 90.3 %while.31 = (s32[]{:T(128)}, f32[512,16,64]{0,2,1:T(8,128)}, bf16[4,256,16,64]{1,3,2,0:T(8,128)(2,1)}, bf16[4,256,16,64]{1,3,2,0:T(8,128)(2,1)}, bf16[4,256,16,6...) while((s32[]{:T(128)}, f32[512,16,64]{0,2,1:T(8,128)}, ...), condition=%wide.region_22.23_spmd.clone, body=%wide.region_21.22_spmd.clone.sunk | while | flops 1361183488 | bytes 134068056 | solution.py:668
  455.4 5.3 bitcast_add_fusion.2
  478.1 5.3 bitcast_add_fusion.2
  500.8 5.3 bitcast_add_fusion.2
  526.5 7.4 convolution_convert_fusion
  533.9 8.2 %convolution_convert_fusion.1 = bf16[4096,1024]{1,0:T(8,128)(2,1)} fusion(f32[512,1024]{1,0:T(8,128)S(1)} %copy-done.31, f32[512]{0:T(512)S(1)} %negate_multiply_fusion.3, f32[512,4096]{1,0:T(8,128)S(1)} %bitcast.197), kind=kOutput, calls=%fused_computation.62 | convolution fusion | flops 4319084544 | bytes 18876416 | tf_op jit(solution)/shard_map/tf,td->fd/dot_general | solution.py:610
  542.1 33.2 %reduce-scatter.2.cloned.1.call-done = bf16[512,2048]{0,1:T(8,128)(2,1)} async-done(((bf16[1024,2048]{0,1:T(8,128)(2,1)}), bf16[512,2048]{0,1:T(8,128)(2,1)}) %reduce-scatter.2.cloned.1.call-update) | async-done | bytes 2097168 | tf_op jit(solution)/shard_map/reduce_scatter | solution.py:675
  584.7 9.1 %convolution_convert_fusion.2 = bf16[1024,3072]{1,0:T(8,128)(2,1)} fusion(bf16[512,1024]{0,1:T(8,128)(2,1)S(1)} %get-tuple-element.450, bf16[512,1024]{0,1:T(8,128)(2,1)S(1)} %bitcast.190, bf16[512,1024]{0,1:T(8,128)(2,1)S(1)} %bitcast.188, bf16[512,1024]{1,0:T(8,128)(2,1)S(1)} %copy-done.26, f32[1024]{0:T(1024)S(1)} %copy-done.43, f32[512]{0:T(512)S(1)} %copy-done.51, ...), kind=kOutput, calls=%fused_computation.63 | convolution fusion | flops 3236429824 | bytes 10493952 | tf_op jit(solution)/shard_map/td,te->de/dot_general | solution.py:687
  595.9 174.9 %shard_map.136 = (f32[128,1024]{1,0:T(8,128)}, f32[32,4096]{1,0:T(8,128)}, f32[32,1024]{1,0:T(8,128)}, f32[32,3072]{1,0:T(8,128)}, f32[32,128]{1,0:T(8,128)}) custom-call(bf16[16,2,128,1024]{3,2,1,0:T(8,128)(2,1)} %bitcast.171, bf16[16,2,32,4096]{3,2,1,0:T(8,128)(2,1)} %bitcast.170, bf16[16,2,32,1024]{3,2,1,0:T(8,128)(2,1)} %bitcast.183, ...), custom_call_target="tpu_custom_call" | custom-call | tf_op jit(solution)/shard_map/pallas_call | solution.py:450
  (323 shorter events, 205.4 us)
Async XLA Ops:
  7.2 243.2 %all-gather.3.cloned.1.call-start = ((), (), s32[]{:S(2)}) async-start(), calls=%async_computation.1 | async-start | bytes 3145728 | tf_op jit(solution)/shard_map/all_gather | solution.py:591
  11.7 187.1 %copy-start.24 = (bf16[512,1024]{1,0:T(8,128)(2,1)S(1)}, bf16[512,1024]{1,0:T(8,128)(2,1)}, u32[]{:S(2)}) copy-start(bf16[512,1024]{1,0:T(8,128)(2,1)} %param.12) | copy-start | bytes 3145732
  219.2 66.4 %all-gather.5.cloned.1.call-start = ((), (), s32[]{:S(2)}) async-start(), calls=%async_computation.2 | async-start | bytes 3145728 | tf_op jit(solution)/shard_map/all_gather | solution.py:592
  222.4 353.0 %reduce-scatter.2.cloned.1.call-start = ((), (), s32[]{:S(2)}) async-start(), calls=%async_computation.3 | async-start | bytes 6291456 | tf_op jit(solution)/shard_map/reduce_scatter | solution.py:675
  224.1 189.9 %copy-start.40 = (f32[512]{0:T(512)}, f32[512]{0:T(512)S(1)}, u32[]{:S(2)}) copy-start(f32[512]{0:T(512)S(1)} %dynamic_slice.37) | copy-start | bytes 6148
  331.9 5.8 copy-start.8
  360.5 7.7 slice-start
  367.2 8.2 %slice-start.2 = ((s8[8388608]{0:T(1024)(128)(4,1)}), s8[4194304]{0:T(1024)(128)(4,1)S(1)}, s32[]{:S(2)}) async-start(s8[8388608]{0:T(1024)(128)(4,1)} %bitcast.163), calls=%async_computation.6 | async-start | bytes 8388608
  367.8 18.6 %copy-start.18 = (f32[512,1024]{1,0:T(8,128)}, f32[512,1024]{1,0:T(8,128)S(1)}, u32[]{:S(2)}) copy-start(f32[512,1024]{1,0:T(8,128)S(1)} %get-tuple-element.435) | copy-start | bytes 6291460
  368.5 7.0 slice-start.3
  402.7 7.9 %copy-start.19 = (f32[512,1024]{1,0:T(8,128)S(1)}, f32[512,1024]{1,0:T(8,128)}, u32[]{:S(2)}) copy-start(f32[512,1024]{1,0:T(8,128)} %copy-done.18) | copy-start | bytes 6291460
  433.4 6.9 copy-start.10
  455.4 7.5 copy-start.10
  478.1 7.5 copy-start.10
  500.8 7.6 copy-start.10
  522.1 11.8 %slice-start.6 = ((s8[8388608]{0:T(1024)(128)(4,1)}), s8[4194304]{0:T(1024)(128)(4,1)S(1)}, s32[]{:S(2)}) async-start(s8[8388608]{0:T(1024)(128)(4,1)} %bitcast.196), calls=%async_computation.10 | async-start | bytes 8388608
  526.5 7.4 copy-start.31
  526.5 7.4 slice-start.7
  584.7 9.1 %copy-start.27 = (f32[512,1024]{1,0:T(8,128)}, f32[512,1024]{1,0:T(8,128)S(1)}, u32[]{:S(2)}) copy-start(f32[512,1024]{1,0:T(8,128)S(1)} %get-tuple-element.464) | copy-start | bytes 6291460
  584.7 9.1 %copy-start.49 = (f32[512]{0:T(512)S(1)}, f32[512]{0:T(512)}, u32[]{:S(2)}) copy-start(f32[512]{0:T(512)} %copy-done.48) | copy-start | bytes 6148
  595.9 176.3 %copy-start.17 = (f32[512,1024]{1,0:T(8,128)S(1)}, f32[512,1024]{1,0:T(8,128)}, u32[]{:S(2)}) copy-start(f32[512,1024]{1,0:T(8,128)} %copy-done.16) | copy-start | bytes 6291460
  595.9 176.3 %copy-start.23 = (bf16[512,1024]{1,0:T(8,128)(2,1)S(1)}, bf16[512,1024]{1,0:T(8,128)(2,1)}, u32[]{:S(2)}) copy-start(bf16[512,1024]{1,0:T(8,128)(2,1)} %param.19) | copy-start | bytes 3145732
  595.9 176.3 %copy-start.41 = (f32[512]{0:T(512)S(1)}, f32[512]{0:T(512)}, u32[]{:S(2)}) copy-start(f32[512]{0:T(512)} %copy-done.40) | copy-start | bytes 6148
  595.9 176.3 %copy-start.45 = (f32[512]{0:T(512)S(1)}, f32[512]{0:T(512)}, u32[]{:S(2)}) copy-start(f32[512]{0:T(512)} %copy-done.44) | copy-start | bytes 6148
  (54 other events, 164.8 us)
Sparse Core Ops, SparseCore 0:
  219.3 31.0 all-gather.2
  252.5 33.0 all-gather.4
  521.0 54.2 reduce-scatter.1

commit v2 on v1

--- a/solution.py
+++ b/solution.py
@@ -2,6 +2,7 @@
 
 import jax
 import jax.numpy as jnp
+import numpy as np
 from jax import lax
 from jax.sharding import PartitionSpec as P
 
@@ -467,6 +468,473 @@
 masked_score = -1e30
 
 
+def loop(count):
+    def run(body):
+        def step(i, carry):
+            body(i)
+            return carry
+
+        lax.fori_loop(0, count, step, 0)
+
+    return run
+
+
+def dot(a, b):
+    return jnp.dot(a, b, preferred_element_type=jnp.float32)
+
+
+def dot_nt(a, b):
+    return lax.dot_general(a, b, (((1,), (1,)), ((), ())), preferred_element_type=jnp.float32)
+
+
+def normed(v):
+    center = v - jnp.mean(v, axis=-1, keepdims=True)
+    r = lax.rsqrt(jnp.mean(center * center, axis=-1, keepdims=True) + epsilon)
+    return center * r, r
+
+
+def norm_pull(v, gain, e):
+    z, r = normed(v)
+    f = e * gain
+    dv = r * (
+        f
+        - jnp.mean(f, axis=-1, keepdims=True)
+        - z * jnp.mean(f * z, axis=-1, keepdims=True)
+    )
+    return dv, e * z
+
+
+def turn(u, cosine, sine, half):
+    lane = lax.broadcasted_iota(jnp.int32, u.shape, 1)
+    swapped = jnp.where(
+        lax.rem(lane, 2 * half) < half,
+        pltpu.roll(u, u.shape[1] - half, 1),
+        pltpu.roll(u, half, 1),
+    )
+    return u * cosine + swapped * sine
+
+
+def turn_tables(row_len, head_dim):
+    half = head_dim // 2
+    inverse = 10000.0 ** (-2.0 * np.arange(half) / head_dim)
+    angles = np.arange(row_len)[:, None] * inverse[None, :]
+    cosine = np.tile(np.cos(angles), (1, 4))
+    sine = np.tile(np.concatenate([-np.sin(angles), np.sin(angles)], axis=1), (1, 2))
+    return cosine.astype(np.float32), sine.astype(np.float32)
+
+
+def doc_ends(lens):
+    ends = [lens[0, 0]]
+    for d in range(1, DOCS):
+        ends.append(ends[-1] + lens[0, d])
+    return ends
+
+
+def fill_bias(bias, lens, first, rows):
+    ends = doc_ends(lens)
+    block = 128
+
+    @loop(bias.shape[0] // block)
+    def _(i):
+        shape = (block, rows)
+        place = first + lax.broadcasted_iota(jnp.int32, shape, 1)
+        key = i * block + lax.broadcasted_iota(jnp.int32, shape, 0)
+        start = jnp.zeros(shape, jnp.int32)
+        for d in range(DOCS):
+            start = jnp.where(place >= ends[d], ends[d], start)
+        fine = (key >= start) & (key <= place)
+        bias[pl.ds(i * block, block), :] = jnp.where(fine, 0.0, masked_score)
+
+
+def split_heads(v, axis=1):
+    spot = lax.broadcasted_iota(jnp.int32, v.shape, axis)
+    first = spot < v.shape[axis] // 2
+    zero = jnp.zeros_like(v)
+    return jnp.where(first, v, zero), jnp.where(first, zero, v)
+
+
+class Tiles:
+    def __init__(self, source, buffer, sems):
+        self.source, self.buffer, self.sems = source, buffer, sems
+
+    def copy(self, t):
+        slot = lax.rem(t, 2)
+        return pltpu.make_async_copy(self.source(t), self.buffer.at[slot], self.sems.at[slot])
+
+    def first(self, t=0):
+        self.copy(jnp.int32(t)).start()
+
+    def get(self, t, end):
+        @pl.when(t + 1 < end)
+        def _():
+            self.copy(t + 1).start()
+
+        self.copy(t).wait()
+        return self.buffer[lax.rem(t, 2)]
+
+
+def forward_kernel(dp_size, head_dim, *refs):
+    (tok, lens, gs, wq, wo, wu, wd, cosine, sine) = refs[:9]
+    (out, wq_f, wo_f, wu_f, wd_f, gain_o, q_o, k_o, v_o, ob_o, lse_o) = refs[9:20]
+    (araw_o, h_o, mraw_o, bt_o, gt_o, gp_o, at_o, atx_o) = refs[20:28]
+    (g_full, gain, tokx, a, ax, at, atx, q, k, v, vt, bias, ob, lse) = refs[28:42]
+    (araw, h, mraw, b, bt, act, actt, gp, wbuf, dbuf) = refs[42:52]
+    sems = refs[52:62]
+    wsem, dsem, xsem, osem = refs[62:66]
+    g = Place(dp_size)
+    y = g.y
+    rows, width = tok.shape
+    half = head_dim // 2
+    pairs = width // 128
+    scale = head_dim ** (-0.5)
+    gg, gq, go, gu, gd = [
+        Gather(g, s, f, sems[2 * i], sems[2 * i + 1], False)
+        for i, (s, f) in enumerate(
+            ((gs, g_full), (wq, wq_f), (wo, wo_f), (wu, wu_f), (wd, wd_f))
+        )
+    ]
+    Z = g.Z
+    saves = []
+
+    def save(src, dst):
+        copy = pltpu.make_async_copy(src, dst, osem.at[len(saves)])
+        copy.start()
+        saves.append(copy)
+
+    tok_copy = pltpu.make_async_remote_copy(
+        src_ref=tok,
+        dst_ref=tokx,
+        send_sem=xsem.at[0],
+        recv_sem=xsem.at[1],
+        device_id=g.device(g.z, g.x, g.c, 1 - y),
+        device_id_type=MESH,
+    )
+    g.barrier()
+    gg.start()
+    gq.start()
+
+    @pl.when(y == 0)
+    def _():
+        tok_copy.start()
+
+    go.start()
+    fill_bias(bias, lens, y * rows, rows)
+    for k_ in range(1, Z):
+        gg.arrived_z(k_)
+    for k_ in range(Z):
+        gg.later_p2(k_)
+    for k_ in range(Z):
+        gg.arrived_p3(k_)
+    for k_ in range(1, Z):
+        gq.arrived_z(k_)
+    gu.start()
+    for z in range(Z):
+        gg.arrived_sib(z)
+    gg.own_here()
+    turned = jnp.transpose(g_full[...].astype(jnp.float32))
+    gain[...] = turned[:8]
+    save(gain, gain_o)
+
+    def first_norm(src, dst, dst_t):
+        @loop(rows // 128)
+        def _(i):
+            spot = pl.ds(i * 128, 128)
+            z, _r = normed(src[spot, :].astype(jnp.float32))
+            value = z * gain[0:1, :]
+            dst[spot, :] = value.astype(jnp.bfloat16)
+            dst_t[:, spot] = jnp.transpose(value).astype(jnp.bfloat16)
+
+    first_norm(tok, a, at)
+    save(at, at_o)
+    for k_ in range(Z):
+        gq.later_p2(k_)
+
+    @pl.when(y == 1)
+    def _():
+        tok_copy.wait_recv()
+        first_norm(tokx, ax, atx)
+
+    save(atx, atx_o)
+    for k_ in range(Z):
+        gq.arrived_p3(k_)
+    for k_ in range(1, Z):
+        go.arrived_z(k_)
+    for k_ in range(Z):
+        go.later_p2(k_)
+    for z in range(Z):
+        gq.arrived_sib(z)
+    gq.own_here()
+
+    tiles = Tiles(lambda t: wq_f.at[:, pl.ds(pl.multiple_of(t * 256, 256), 256)], wbuf, wsem)
+    per = width // 256
+    first = pl.multiple_of(y * rows, rows)
+
+    def turned_pair(u, start):
+        return turn(u, cosine[pl.ds(start, rows), :], sine[pl.ds(start, rows), :], half)
+
+    tiles.first()
+
+    @loop(per)
+    def _(t):
+        u = dot(a[...], tiles.get(t, 3 * per))
+        for j in (0, 1):
+            part = turned_pair(u[:, j * 128 : j * 128 + 128], first) * scale
+            q[2 * t + j] = part.astype(jnp.bfloat16)
+
+    for k_ in range(Z):
+        go.arrived_p3(k_)
+    for k_ in range(1, Z):
+        gu.arrived_z(k_)
+    gd.start()
+
+    def keys(w, t, src, start):
+        u = dot(src[...], w)
+        for j in (0, 1):
+            part = turned_pair(u[:, j * 128 : j * 128 + 128], start)
+            k[2 * t + j, pl.ds(start, rows), :] = part.astype(jnp.bfloat16)
+
+    @loop(per)
+    def _(t):
+        w = tiles.get(t + per, 3 * per)
+        keys(w, t, a, first)
+
+        @pl.when(y == 1)
+        def _():
+            keys(w, t, ax, 0)
+
+    for k_ in range(Z):
+        gu.later_p2(k_)
+
+    def values(w, t, src, start):
+        u = dot(src[...], w)
+        ut = jnp.transpose(u).astype(jnp.bfloat16)
+        for j in (0, 1):
+            cols = slice(j * 128, j * 128 + 128)
+            v[2 * t + j, pl.ds(start, rows), :] = u[:, cols].astype(jnp.bfloat16)
+            vt[2 * t + j, :, pl.ds(start, rows)] = ut[cols]
+
+    @loop(per)
+    def _(t):
+        w = tiles.get(t + 2 * per, 3 * per)
+        values(w, t, a, first)
+
+        @pl.when(y == 1)
+        def _():
+            values(w, t, ax, 0)
+
+    save(q, q_o)
+    save(k, k_o)
+    save(v, v_o)
+
+    def attend(p, block, count):
+        spot = slice(block * 256, block * 256 + 256)
+        heads = split_heads(q[p, spot, :])
+        kk = k[p, :count, :]
+        vv = vt[p, :, :count]
+        parts = []
+        for i in (0, 1):
+            s = dot_nt(kk, heads[i]) + bias[:count, spot]
+            m = jnp.max(s, axis=0, keepdims=True)
+            e = jnp.exp(s - m)
+            total = jnp.sum(e, axis=0, keepdims=True)
+            lse[p, i : i + 1, spot] = m + jnp.log(total)
+            parts.append(dot(vv, e.astype(jnp.bfloat16)) * (1.0 / total))
+        upper = lax.broadcasted_iota(jnp.int32, parts[0].shape, 0) < head_dim
+        ob[p, :, spot] = jnp.where(upper, parts[0], parts[1]).astype(jnp.bfloat16)
+
+    events = [lambda: None] * pairs
+    events[0] = lambda: [gu.arrived_p3(k_) for k_ in range(Z // 2)]
+    events[1] = lambda: [gu.arrived_p3(k_) for k_ in range(Z // 2, Z)]
+    events[2] = lambda: [gd.arrived_z(k_) for k_ in range(1, Z)]
+    events[4] = lambda: [gd.later_p2(k_) for k_ in range(Z)]
+    events[7] = lambda: [gd.arrived_p3(k_) for k_ in range(Z)]
+
+    blocks = rows // 256
+
+    @loop(pairs)
+    def _(p):
+        for half_row in (0, 1):
+
+            @pl.when(y == half_row)
+            def _():
+                for block in range(blocks):
+                    attend(p, block, (half_row * blocks + block + 1) * 256)
+
+        for i in range(pairs):
+
+            @pl.when(p == i)
+            def _():
+                events[i]()
+
+    save(ob, ob_o)
+    save(lse, lse_o)
+
+    for z in range(Z):
+        go.arrived_sib(z)
+    go.own_here()
+    obf = jnp.transpose(ob[...].reshape(width, rows))
+    a[...] = obf
+    tiles = Tiles(lambda t: wo_f.at[:, pl.ds(pl.multiple_of(t * 256, 256), 256)], wbuf, wsem)
+    tiles.first()
+
+    @loop(per)
+    def _(t):
+        w = tiles.get(t, per)
+        araw[:, pl.ds(pl.multiple_of(t * 256, 256), 256)] = dot(a[...], w)
+
+    save(araw, araw_o)
+
+    @loop(rows // 128)
+    def _(i):
+        spot = pl.ds(i * 128, 128)
+        z, _r = normed(araw[spot, :])
+        hidden = tok[spot, :].astype(jnp.float32) + z * gain[1:2, :]
+        h[spot, :] = hidden
+        z, _r = normed(hidden)
+        value = z * gain[2:3, :]
+        b[spot, :] = value.astype(jnp.bfloat16)
+        bt[:, spot] = jnp.transpose(value).astype(jnp.bfloat16)
+
+    save(h, h_o)
+    save(bt, bt_o)
+
+    for z in range(Z):
+        gu.arrived_sib(z)
+    gu.own_here()
+    tiles = Tiles(lambda t: wu_f.at[:, pl.ds(pl.multiple_of(t * 256, 256), 256)], wbuf, wsem)
+    ups = act.shape[0]
+    tiles.first()
+    c0 = math.sqrt(2.0 / math.pi)
+
+    @loop(ups)
+    def _(t):
+        u = dot(b[...], tiles.get(t, ups))
+        square = u * u
+        th = jnp.tanh(c0 * (u + 0.044715 * (square * u)))
+        value = 0.5 * u * (1.0 + th)
+        slope = 0.5 * (1.0 + th) + (0.5 * c0) * u * (1.0 - th * th) * (
+            1.0 + (3 * 0.044715) * square
+        )
+        act[t] = value.astype(jnp.bfloat16)
+        actt[t] = jnp.transpose(value).astype(jnp.bfloat16)
+        gp[t] = slope.astype(jnp.bfloat16)
+
+    save(actt, gt_o)
+    save(gp, gp_o)
+
+    for z in range(Z):
+        gd.arrived_sib(z)
+    gd.own_here()
+    tiles = Tiles(lambda t: wd_f.at[pl.ds(pl.multiple_of(t * 256, 256), 256), :], dbuf, dsem)
+    tiles.first()
+    mraw[...] = jnp.zeros_like(mraw)
+
+    @loop(ups)
+    def _(t):
+        mraw[...] += dot(act[t], tiles.get(t, ups))
+
+    save(mraw, mraw_o)
+    ends = doc_ends(lens)
+
+    @loop(rows // 128)
+    def _(i):
+        spot = pl.ds(i * 128, 128)
+        z, _r = normed(mraw[spot, :])
+        result = h[spot, :] + z * gain[3:4, :]
+        place = y * rows + i * 128 + lax.broadcasted_iota(jnp.int32, result.shape, 0)
+        result = jnp.where(place < ends[DOCS - 2], result, 0.0)
+        out[spot, :] = result.astype(jnp.bfloat16)
+
+    for copy in saves:
+        copy.wait()
+
+    @pl.when(y == 0)
+    def _():
+        tok_copy.wait_send()
+
+    for m in (gg, gq, go, gu, gd):
+        m.sent()
+
+
+def forward(tokens, lengths, gains_wide, w_qkv, w_out, w_up, w_down, tables):
+    dp_size = lax.axis_size("dp")
+    devices = dp_size * lax.axis_size("ctx")
+    rows, width = tokens.shape
+    row_len = rows * lax.axis_size("ctx")
+    head_dim = width // HEADS
+    pairs = width // 128
+    ups = w_up.shape[1] // 256
+    bf, f32 = jnp.bfloat16, jnp.float32
+    any_spec = pl.BlockSpec(memory_space=pl.ANY)
+    vm = pl.BlockSpec(memory_space=pltpu.VMEM)
+    shape = jax.ShapeDtypeStruct
+
+    def whole(w):
+        return shape((w.shape[0] * devices, w.shape[1]), bf)
+
+    outs = [
+        shape((rows, width), bf),
+        whole(w_qkv),
+        whole(w_out),
+        whole(w_up),
+        whole(w_down),
+        shape((8, width), f32),
+        shape((pairs, rows, 128), bf),
+        shape((pairs, row_len, 128), bf),
+        shape((pairs, row_len, 128), bf),
+        shape((pairs, 128, rows), bf),
+        shape((pairs, 2, rows), f32),
+        shape((rows, width), f32),
+        shape((rows, width), f32),
+        shape((rows, width), f32),
+        shape((width, rows), bf),
+        shape((ups, 256, rows), bf),
+        shape((ups, rows, 256), bf),
+        shape((width, rows), bf),
+        shape((width, rows), bf),
+    ]
+    scratch = [
+        pltpu.VMEM((width, 128), bf),
+        pltpu.VMEM((8, width), f32),
+        pltpu.VMEM((rows, width), bf),
+        pltpu.VMEM((rows, width), bf),
+        pltpu.VMEM((rows, width), bf),
+        pltpu.VMEM((width, rows), bf),
+        pltpu.VMEM((width, rows), bf),
+        pltpu.VMEM((pairs, rows, 128), bf),
+        pltpu.VMEM((pairs, row_len, 128), bf),
+        pltpu.VMEM((pairs, row_len, 128), bf),
+        pltpu.VMEM((pairs, 128, row_len), bf),
+        pltpu.VMEM((row_len, rows), f32),
+        pltpu.VMEM((pairs, 128, rows), bf),
+        pltpu.VMEM((pairs, 2, rows), f32),
+        pltpu.VMEM((rows, width), f32),
+        pltpu.VMEM((rows, width), f32),
+        pltpu.VMEM((rows, width), f32),
+        pltpu.VMEM((rows, width), bf),
+        pltpu.VMEM((width, rows), bf),
+        pltpu.VMEM((ups, rows, 256), bf),
+        pltpu.VMEM((ups, 256, rows), bf),
+        pltpu.VMEM((ups, rows, 256), bf),
+        pltpu.VMEM((2, width, 256), bf),
+        pltpu.VMEM((2, 256, width), bf),
+    ]
+    scratch += [pltpu.SemaphoreType.DMA((Gather.sems(dp_size // 4),))] * 10
+    scratch += [pltpu.SemaphoreType.DMA((2,))] * 3 + [pltpu.SemaphoreType.DMA((16,))]
+    return pl.pallas_call(
+        functools.partial(forward_kernel, dp_size, head_dim),
+        out_shape=outs,
+        in_specs=[vm, pl.BlockSpec(memory_space=pltpu.SMEM), vm]
+        + [any_spec] * 4
+        + [vm, vm],
+        out_specs=[vm] + [any_spec] * (len(outs) - 1),
+        scratch_shapes=scratch,
+        compiler_params=pltpu.CompilerParams(
+            collective_id=0, has_side_effects=True, vmem_limit_bytes=60 * 2**20
+        ),
+    )(tokens, lengths, gains_wide, w_qkv, w_out, w_up, w_down, *tables)
+
+
 def layer_norm(values, gain_vec):
     center = values - jnp.mean(values, axis=-1, keepdims=True)
     spread = jnp.mean(center * center, axis=-1, keepdims=True)
@@ -698,9 +1166,140 @@
     return (output, d_tokens, shard_qkv, shard_out, shard_up, shard_down, shard_gains)
 
 
+def fused_device(tokens, lengths, w_qkv, w_out, w_up, w_down, gains, d_out):
+    tok_rows, model_width = tokens.shape
+    row_len = tok_rows * lax.axis_size("ctx")
+    head_count = HEADS
+    head_dim = model_width // head_count
+    score_scale = head_dim ** (-0.5)
+    head_shape = (tok_rows, head_count, head_dim)
+    seg_full, pos_full, valid_full = doc_layout(lengths, row_len)
+    offset = lax.axis_index("ctx") * tok_rows
+    own_seg = lax.dynamic_slice_in_dim(seg_full, offset, tok_rows)
+    own_valid = lax.dynamic_slice_in_dim(valid_full.astype(jnp.float32), offset, tok_rows)
+    own_place = offset + jnp.arange(tok_rows, dtype=jnp.int32)
+    gains_wide = jnp.pad(gains, ((0, 0), (0, 128 - gains.shape[1])))
+    cos_np, sin_np = turn_tables(row_len, head_dim)
+    tables = (jnp.asarray(cos_np), jnp.asarray(sin_np))
+    (output, qkv_back, out_back, up_back, down_back, gain_rows, qs, ks, vs, obs, lse, attn_raw, hidden,
+     mlp_raw, bts, gts, gps, ats, atx) = forward(
+        tokens, lengths, gains_wide, w_qkv, w_out, w_up, w_down, tables)
+    gain_f = gain_rows[:4].T
+    stream = tokens.astype(jnp.float32)
+    def unpair(v):
+        return jnp.transpose(v, (1, 0, 2)).reshape(v.shape[1], head_count, head_dim)
+    seen = (jnp.arange(row_len) < offset + tok_rows)[:, None, None]
+    queries = unpair(qs)
+    key_all, value_all = jnp.where(seen, unpair(ks), 0), jnp.where(seen, unpair(vs), 0)
+    attended_b = obs.reshape(model_width, tok_rows).T
+    attended = attended_b.astype(jnp.float32).reshape(head_shape)
+    row_max = lse.reshape(head_count, tok_rows)
+    row_sum = jnp.ones_like(row_max)
+    mlp_in = bts.T
+    normed_x = ats.T
+    activated = jnp.transpose(gts, (2, 0, 1)).reshape(tok_rows, -1)
+    gp = jnp.transpose(gps, (1, 0, 2)).reshape(tok_rows, -1).astype(jnp.float32)
+    upstream = d_out.astype(jnp.float32) * own_valid[:, None]
+    d_mlp, d_gain_four = norm_back(mlp_raw, gain_f[:, 3], upstream)
+    d_mlp_b = d_mlp.astype(jnp.bfloat16)
+    grad_down = jnp.einsum("tf,td->fd", activated, d_mlp_b, preferred_element_type=jnp.float32)
+    d_activated = jnp.einsum("td,fd->tf", d_mlp_b, down_back, preferred_element_type=jnp.float32)
+    d_up_b = (d_activated * gp).astype(jnp.bfloat16)
+    grad_up = jnp.einsum("td,tf->df", mlp_in, d_up_b, preferred_element_type=jnp.float32)
+    d_mlp_in = jnp.einsum("tf,df->td", d_up_b, up_back, preferred_element_type=jnp.float32)
+    d_hidden_part, d_gain_three = norm_back(hidden, gain_f[:, 2], d_mlp_in)
+    d_hidden = upstream + d_hidden_part
+    d_attn, d_gain_two = norm_back(attn_raw, gain_f[:, 1], d_hidden)
+    d_attn_b = d_attn.astype(jnp.bfloat16)
+    grad_out = jnp.einsum("td,te->de", attended_b, d_attn_b, preferred_element_type=jnp.float32)
+    d_attended = (
+        jnp.einsum("te,de->td", d_attn_b, out_back, preferred_element_type=jnp.float32)
+        .astype(jnp.bfloat16)
+        .reshape(head_shape)
+    )
+    row_dot = jnp.einsum("qhd,qhd->hq", d_attended.astype(jnp.float32), attended)
+    block_rows = math.gcd(row_len, 256)
+    block_count = row_len // block_rows
+    key_blocks = key_all.reshape((block_count, block_rows) + key_all.shape[1:])
+    value_blocks = value_all.reshape((block_count, block_rows) + value_all.shape[1:])
+
+    def back_block(d_queries, block_items):
+        key_block, value_block, block_id = block_items
+        allowed = allowed_keys(own_seg, own_place, seg_full, block_id * block_rows, block_rows)
+        scores = (
+            jnp.einsum("qhd,khd->hqk", queries, key_block, preferred_element_type=jnp.float32)
+        )
+        attn_prob = jnp.where(
+            allowed[None], jnp.exp(scores - row_max[..., None]) / row_sum[..., None], 0.0
+        )
+        d_prob = jnp.einsum(
+            "qhd,khd->hqk", d_attended, value_block, preferred_element_type=jnp.float32
+        )
+        d_scores = (attn_prob * (d_prob - row_dot[..., None])).astype(jnp.bfloat16)
+        d_queries = (
+            d_queries
+            + jnp.einsum("hqk,khd->qhd", d_scores, key_block, preferred_element_type=jnp.float32)
+            * score_scale
+        )
+        d_keys = (
+            jnp.einsum("hqk,qhd->khd", d_scores, queries, preferred_element_type=jnp.float32)
+        )
+        d_values = jnp.einsum(
+            "hqk,qhd->khd",
+            attn_prob.astype(jnp.bfloat16),
+            d_attended,
+            preferred_element_type=jnp.float32,
+        )
+        return (d_queries, (d_keys, d_values))
+
+    block_ids = jnp.arange(block_count, dtype=jnp.int32)
+    d_queries, (d_keys_all, d_values_all) = lax.scan(
+        back_block, jnp.zeros(head_shape, jnp.float32), (key_blocks, value_blocks, block_ids)
+    )
+    kv_terms = jnp.concatenate(
+        [d_keys_all.reshape(row_len, model_width), d_values_all.reshape(row_len, model_width)],
+        axis=-1,
+    )
+    kv_grad = lax.psum_scatter(
+        kv_terms.astype(jnp.bfloat16), "ctx", scatter_dimension=0, tiled=True
+    ).astype(jnp.float32)
+    place = offset + jnp.arange(tok_rows)
+    inv = 10000.0 ** (-2.0 * np.arange(head_dim // 2) / head_dim)
+    angles = place.astype(jnp.float32)[:, None] * jnp.asarray(inv, jnp.float32)
+    cosine_table = jnp.cos(angles)[:, None, :]
+    sine_table = jnp.sin(angles)[:, None, :]
+    d_keys = kv_grad[:, :model_width].reshape(head_shape)
+    d_qkv = jnp.concatenate(
+        [
+            rotate(d_queries, cosine_table, sine_table, -1.0).reshape(tok_rows, model_width),
+            rotate(d_keys, cosine_table, sine_table, -1.0).reshape(tok_rows, model_width),
+            kv_grad[:, model_width:],
+        ],
+        axis=-1,
+    ).astype(jnp.bfloat16)
+    grad_qkv = jnp.einsum("td,te->de", normed_x, d_qkv, preferred_element_type=jnp.float32)
+    d_normed = jnp.einsum("te,de->td", d_qkv, qkv_back, preferred_element_type=jnp.float32)
+    d_stream_part, d_gain_one = norm_back(stream, gain_f[:, 0], d_normed)
+    d_tokens = (d_hidden + d_stream_part).astype(jnp.bfloat16)
+    grad_gains = jnp.stack([d_gain_one, d_gain_two, d_gain_three, d_gain_four], axis=-1)
+    grad_gains = jnp.pad(grad_gains, ((0, 0), (0, 128 - gains.shape[1])))
+    shard_down, shard_up, shard_out, shard_qkv, shard_gains = scatter_all(
+        [v.astype(jnp.bfloat16) for v in (grad_down, grad_up, grad_out, grad_qkv, grad_gains)],
+        (False,) * 5,
+    )
+    shard_gains = shard_gains[:, : gains.shape[1]]
+    return (output, d_tokens, shard_qkv, shard_out, shard_up, shard_down, shard_gains)
+
+
+def layer(mesh):
+    if mesh.shape["dp"] == 16 and mesh.shape["ctx"] == 2:
+        return fused_device
+    return per_device
+
+
 def solution(mesh):
     return jax.shard_map(
-        per_device,
+        layer(mesh),
         mesh=mesh,
         in_specs=(
             P(("dp", "ctx"), None),

time: 797 us -> 665 us (0.83)
  matrix products: 189 us -> 116 us
  waiting for transfers between devices: 90.1 us -> 30.7 us
  Pallas kernels: 354 us -> 367 us
  other arithmetic: 49.9 us -> 38.2 us
    dot_general x20 -> x8, matrix products: 118 us -> 54.6 us  [the longest x1 13 us: fused_device(): jnp.einsum('td,fd->tf', d_mlp_b, down_back, preferred_element_type=jnp.fl...]
    all_gather x2 -> x0, waiting for transfers between devices: 56.9 us -> none  [the longest x1 32 us: per_device(): lax.all_gather(value_heads, 'ctx', axis=0, tiled=True)]
    convert_element_type x1 -> x3, local copies, waits for them, and re-layouts: 0.54 us -> 19.5 us  [the longest x2 18.2 us: fused_device(): gp = jnp.transpose(gps, (1, 0, 2)).reshape(tok_rows, -1).astype(jnp.float32)]
    reduce_sum x5 -> x1, other arithmetic: 18.6 us -> 0.1 us  [doc_layout(): segment = jnp.sum(passed.astype(jnp.int32), axis=-1)]
    slice x7 -> x2, local copies, waits for them, and re-layouts: 14.4 us -> 2.43 us  [the longest x1 1.83 us: fused_device(): d_keys = kv_grad[:, :model_width].reshape(head_shape)]
    unnamed x127 -> x72, local copies, waits for them, and re-layouts: 28.4 us -> 17.6 us
    transpose x0 -> x4, local copies, waits for them, and re-layouts: none -> 9.31 us  [the longest x3 9.31 us: unpair(): return jnp.transpose(v, (1, 0, 2)).reshape(v.shape[1], head_count, head_dim)]
    pallas_call x1, Pallas kernels: 180 us -> 188 us  [forward(): pl.pallas_call(functools.partial(forward_kernel, dp_size, head_dim), out_...]
  transfers between devices with their start and end apart: 3 -> 1, of which waited for: 3 -> 1; matrix products, arithmetic and copies ran while one was open for 4% -> 3% of each run, Pallas kernels for 0% -> 0%
where the time goes in v2:
time: 665 us; the launch traced here: 655 us
  Pallas kernels  367 us (55%)
  matrix products  116 us (17%)
  local copies, waits for them, and re-layouts  85 us (13%)
  other arithmetic  38.2 us (6%)
  waiting for transfers between devices  30.7 us (5%)
  between operations  15 us (2%)
    pallas_call x1, Pallas kernels, forward(): pl.pallas_call(functools.partial(forward_kernel, dp_size, head_dim), out_...  188 us
    pallas_call x1, Pallas kernels, scatter_all(): pl.pallas_call(functools.partial(scatter_kernel, dp_size, by_z, n), out_s...  179 us
    reduce_scatter x1, waiting for transfers between devices, fused_device(): lax.psum_scatter(kv_terms.astype(jnp.bfloat16), 'ctx', scatter_dimension=...  30.7 us
    dot_general x4, matrix products, back_block(): jnp.einsum('qhd,khd->hqk', d_attended, value_block, preferred_element_typ...  20.3 us
    convert_element_type x2, local copies, waits for them, and re-layouts, fused_device(): gp = jnp.transpose(gps, (1, 0, 2)).reshape(tok_rows, -1).astype(jnp.float32)  18.2 us
    unnamed x72, local copies, waits for them, and re-layouts  17.6 us
    while x40, local copies, waits for them, and re-layouts  17.2 us
    dot_general x4, matrix products, back_block(): jnp.einsum('hqk,khd->qhd', d_scores, key_block, preferred_element_type=jn...  13.6 us
  transfers between devices with their start and end apart: 1, of which 1 were waited for; matrix products, arithmetic and copies ran while one was open for 3% of the time, Pallas kernels for 0%

profile of v2, /device:TPU:0, one launch (start us, length us, event | category | flops | bytes accessed | tf_op | source)
XLA Modules:
  0.0 655.0 jit_solution(8009763157983440)
XLA Ops:
  9.5 187.5 %shard_map.162 = (bf16[512,1024]{1,0:T(8,128)(2,1)}, bf16[1024,3072]{1,0:T(8,128)(2,1)}, bf16[1024,1024]{1,0:T(8,128)(2,1)}, bf16[1024,4096]{1,0:T(8,128)(2,1)},...) custom-call(bf16[512,1024]{1,0:T(8,128)(2,1)} %refs_0_.1, ...), custom_call_target="tpu_custom_call" | custom-call | tf_op jit(solution)/shard_map/pallas_call | solution.py:924
  204.6 3.4 multiply_reduce_fusion
  211.0 4.1 convert_bitcast_fusion
  215.1 9.3 %copy.44 = f32[512,16,256]{0,2,1:T(8,128)} copy(f32[512,16,256]{2,0,1:T(8,128)} %convert_bitcast_fusion) | data formatting | bytes 16777216 | tf_op jit(solution)/shard_map/convert_element_type | solution.py:1201
  224.3 8.9 %copy.45 = f32[512,4096]{1,0:T(8,128)} copy(f32[512,4096]{0,1:T(8,128)} %bitcast.159) | data formatting | bytes 16777216 | tf_op jit(solution)/shard_map/convert_element_type | solution.py:1201
  237.0 13.0 %multiply_convert_fusion = bf16[512,4096]{1,0:T(8,128)(2,1)} fusion(f32[512,4096]{1,0:T(8,128)} %copy.45, bf16[4096,1024]{1,0:T(8,128)(2,1)} %get-tuple-element.107, f32[512,1024]{1,0:T(8,128)} %get-tuple-element.284, f32[512]{0:T(512)S(1)} %negate_multiply_fusion.3), kind=kOutput, calls=%fused_computation.29 | convolution fusion | flops 4300210176 | bytes 23070720 | tf_op jit(solution)/shard_map/td,fd->tf/dot_general | solution.py:1206
  250.0 9.0 %multiply_reduce_fusion.1 = (bf16[1024]{0:T(1024)(128)(2,1)S(1)}, f32[512]{0:T(512)S(1)}, f32[512,1024]{1,0:T(8,128)S(1)}) fusion(f32[512,1024]{1,0:T(8,128)S(1)} %copy-done.11, f32[512]{0:T(512)S(1)} %fusion.42, f32[512]{0:T(512)S(1)} %broadcast_multiply_fusion.2, f32[1024]{0:T(1024)S(1)} %bitcast.187, bf16[512,4096]{1,0:T(8,128)(2,1)} %multiply_convert_fusion, ...), kind=kOutput, calls=%fused_computation.52 | convolution fusion | flops 4298635776 | bytes 16789504 | tf_op jit(solution)/shard_map/tf,df->td/dot_general | solution.py:1209
  266.8 3.9 copy.46
  270.7 4.5 reshape.368
  275.2 3.9 copy.48
  279.1 4.5 reshape.370
  283.6 3.8 broadcast_select_fusion
  294.5 84.9 %while.16 = (s32[]{:T(128)}, f32[512,16,64]{0,2,1:T(8,128)S(1)}, bf16[4,256,16,64]{1,3,2,0:T(8,128)(2,1)}, bf16[4,256,16,64]{1,3,2,0:T(8,128)(2,1)}, bf16[4,256,...) while((s32[]{:T(128)}, f32[512,16,64]{0,2,1:T(8,128)S(1)}, ...), condition=%wide.wide.region_15.16_spmd.clone, body=%wide.wide.region_14.15_spmd.clone.sunk | while | flops 1360921344 | bytes 142587792 | solution.py:1256
  301.9 5.1 fusion.108
  323.1 5.1 fusion.108
  344.3 5.1 fusion.108
  365.4 5.1 fusion.108
  390.8 5.2 convolution_convert_fusion.3
  396.0 6.7 %convolution_convert_fusion = bf16[1024,4096]{1,0:T(8,128)(2,1)} fusion(bf16[1024,512]{1,0:T(8,128)(2,1)S(1)} %copy-done.31, bf16[512,4096]{1,0:T(8,128)(2,1)S(1)} %copy-done.32), kind=kOutput, calls=%fused_computation.30 | convolution fusion | flops 4299161600 | bytes 13631488 | tf_op jit(solution)/shard_map/td,tf->df/dot_general | solution.py:1208
  402.7 7.3 %convolution_convert_fusion.1 = bf16[4096,1024]{1,0:T(8,128)(2,1)} fusion(bf16[512,4096]{0,1:T(8,128)(2,1)S(1)} %bitcast.192, f32[512,1024]{1,0:T(8,128)S(1)} %copy-done.16, f32[512]{0:T(512)S(1)} %negate_multiply_fusion.3), kind=kOutput, calls=%fused_computation.31 | convolution fusion | flops 4300210176 | bytes 14682112 | tf_op jit(solution)/shard_map/tf,td->fd/dot_general | solution.py:1205
  410.1 30.7 %reduce-scatter.2.cloned.1.call-done = bf16[512,2048]{0,1:T(8,128)(2,1)} async-done(((bf16[1024,2048]{0,1:T(8,128)(2,1)}), bf16[512,2048]{0,1:T(8,128)(2,1)}) %reduce-scatter.2.cloned.1.call-update) | async-done | bytes 2097168 | tf_op jit(solution)/shard_map/reduce_scatter | solution.py:1263
  444.9 4.0 fusion.31
  451.3 8.0 %convolution_convert_fusion.2 = bf16[1024,3072]{1,0:T(8,128)(2,1)} fusion(bf16[1024,512]{1,0:T(8,128)(2,1)} %get-tuple-element.124, bf16[512,1024]{0,1:T(8,128)(2,1)} %copy-done.20, bf16[512,1024]{0,1:T(8,128)(2,1)} %bitcast.178, bf16[512,1024]{0,1:T(8,128)(2,1)S(1)} %bitcast.176), kind=kOutput, calls=%fused_computation.32 | convolution fusion | flops 3233808384 | bytes 10485760 | tf_op jit(solution)/shard_map/td,te->de/dot_general | solution.py:1280
  459.3 179.4 %shard_map.163 = (f32[128,1024]{1,0:T(8,128)}, f32[32,4096]{1,0:T(8,128)}, f32[32,1024]{1,0:T(8,128)}, f32[32,3072]{1,0:T(8,128)}, f32[32,128]{1,0:T(8,128)}) custom-call(bf16[16,2,128,1024]{3,2,1,0:T(8,128)(2,1)} %bitcast.161, bf16[16,2,32,4096]{3,2,1,0:T(8,128)(2,1)} %bitcast.160, bf16[16,2,32,1024]{3,2,1,0:T(8,128)(2,1)} %bitcast.168, ...), custom_call_target="tpu_custom_call" | custom-call | tf_op jit(solution)/shard_map/pallas_call | solution.py:451
  (213 shorter events, 119.3 us)
Async XLA Ops:
  7.2 433.7 %reduce-scatter.2.cloned.1.call-start = ((), (), s32[]{:S(2)}) async-start(), calls=%async_computation.1 | async-start | bytes 6291456 | tf_op jit(solution)/shard_map/reduce_scatter | solution.py:1263
  197.0 93.9 %copy-start.26 = (f32[8,2,512]{2,1,0:T(2,128)}, f32[8,2,512]{2,1,0:T(2,128)S(1)}, u32[]{:S(2)}) copy-start(f32[8,2,512]{2,1,0:T(2,128)S(1)} %get-tuple-element.462) | copy-start | bytes 98308
  198.8 3.8 copy-start.27
  198.8 5.8 copy-start.9
  237.0 13.1 %copy-start.11 = (f32[512,1024]{1,0:T(8,128)S(1)}, f32[512,1024]{1,0:T(8,128)}, u32[]{:S(2)}) copy-start(f32[512,1024]{1,0:T(8,128)} %get-tuple-element.110) | copy-start | bytes 6291460
  296.2 5.7 copy-start.3
  306.9 3.6 copy-start
  307.0 6.1 copy-start.2
  317.4 5.7 copy-start.3
  328.1 3.6 copy-start
  328.1 6.1 copy-start.2
  338.6 5.7 copy-start.3
  349.3 3.6 copy-start
  349.3 6.1 copy-start.2
  359.8 5.7 copy-start.3
  370.5 3.6 copy-start
  370.5 6.1 copy-start.2
  390.8 5.2 copy-start.31
  390.8 5.2 copy-start.32
  396.0 6.7 %copy-start.16 = (f32[512,1024]{1,0:T(8,128)S(1)}, f32[512,1024]{1,0:T(8,128)}, u32[]{:S(2)}) copy-start(f32[512,1024]{1,0:T(8,128)} %get-tuple-element.284) | copy-start | bytes 6291460
  396.0 6.7 %copy-start.29 = (bf16[16,256,512]{2,1,0:T(8,128)(2,1)S(1)}, bf16[16,256,512]{2,1,0:T(8,128)(2,1)}, u32[]{:S(2)}) copy-start(bf16[16,256,512]{2,1,0:T(8,128)(2,1)} %get-tuple-element.122) | copy-start | bytes 12582916
  443.8 5.0 copy-start.19
  459.2 180.8 %copy-start.6 = (f32[512,1024]{1,0:T(8,128)S(1)}, f32[512,1024]{1,0:T(8,128)}, u32[]{:S(2)}) copy-start(f32[512,1024]{1,0:T(8,128)} %copy-done.5) | copy-start | bytes 6291460
  459.2 180.8 %copy-start.10 = (bf16[512,1024]{1,0:T(8,128)(2,1)S(1)}, bf16[512,1024]{1,0:T(8,128)(2,1)}, u32[]{:S(2)}) copy-start(bf16[512,1024]{1,0:T(8,128)(2,1)} %param.20) | copy-start | bytes 3145732
  (27 other events, 64.3 us)
Sparse Core Ops, SparseCore 0:
  389.2 51.5 reduce-scatter.1

commit v3 on v2

--- a/solution.py
+++ b/solution.py
@@ -554,20 +554,25 @@
 
 
 class Tiles:
-    def __init__(self, source, buffer, sems):
-        self.source, self.buffer, self.sems = source, buffer, sems
+    def __init__(self, source, buffer, sems, ready=None):
+        self.source, self.buffer, self.sems, self.ready = source, buffer, sems, ready
 
     def copy(self, t):
         slot = lax.rem(t, 2)
         return pltpu.make_async_copy(self.source(t), self.buffer.at[slot], self.sems.at[slot])
 
+    def start(self, t):
+        if self.ready is not None:
+            self.ready(t)
+        self.copy(t).start()
+
     def first(self, t=0):
-        self.copy(jnp.int32(t)).start()
+        self.start(jnp.int32(t))
 
     def get(self, t, end):
         @pl.when(t + 1 < end)
         def _():
-            self.copy(t + 1).start()
+            self.start(t + 1)
 
         self.copy(t).wait()
         return self.buffer[lax.rem(t, 2)]
@@ -933,6 +938,639 @@
             collective_id=0, has_side_effects=True, vmem_limit_bytes=60 * 2**20
         ),
     )(tokens, lengths, gains_wide, w_qkv, w_out, w_up, w_down, *tables)
+
+
+class Share:
+    def __init__(self, place, part, first, landing, unit, n, send, recv, write):
+        self.g, self.part, self.first = place, part, first
+        self.rec3, self.rec2, self.recz = landing
+        self.unit, self.n, self.send, self.recv, self.write = unit, n, send, recv, write
+        self.kind = part.dtype
+        self.n_z, self.n_p2 = 2 * place.Z, 3 * place.Z - 1
+
+    @staticmethod
+    def sems(Z):
+        return 4 * Z - 1
+
+    def slots(self, block):
+        return self.part.at[pl.ds(self.first, self.n), block]
+
+    def copy(self, block, landing, slot, number, device):
+        return pltpu.make_async_remote_copy(
+            src_ref=self.slots(block),
+            dst_ref=landing.at[pl.ds(self.unit, self.n), slot],
+            send_sem=self.send.at[number],
+            recv_sem=self.recv.at[number],
+            device_id=device,
+            device_id_type=MESH,
+        )
+
+    def p3_copy(self, z, a2):
+        g = self.g
+        slot = z * 2 + a2
+        return self.copy(g.block(z, a2, 1 - g.i3), self.rec3, slot, slot, g.p3)
+
+    def p2_copy(self, z):
+        g = self.g
+        return self.copy(g.block(z, 1 - g.i2, g.i3), self.rec2, z, self.n_p2 + z, g.p2)
+
+    def z_copy(self, k):
+        g = self.g
+        z = lax.rem(g.z + k, g.Z)
+        return self.copy(
+            g.block(z, g.i2, g.i3), self.recz, k - 1, self.n_z + k - 1, g.at_z(z)
+        )
+
+    def value(self, ref, *index):
+        return ref[(pl.ds(self.unit, self.n),) + index].astype(jnp.float32)
+
+    def own(self, block):
+        return self.part[pl.ds(self.first, self.n), block].astype(jnp.float32)
+
+    def start(self, z):
+        for a2 in (0, 1):
+            self.p3_copy(z, a2).start()
+
+    def start_all(self):
+        g = self.g
+        for k in range(1, g.Z + 1):
+            self.start(lax.rem(g.z + k, g.Z))
+
+    def add3(self, z, a2):
+        g = self.g
+        self.p3_copy(z, a2).wait_recv()
+        block = g.block(z, a2, g.i3)
+        total = self.own(block) + self.value(self.rec3, z * 2 + a2)
+        self.part[pl.ds(self.first, self.n), block] = total.astype(self.kind)
+
+    def stage3(self, *ks):
+        g = self.g
+        for k in ks:
+            z = lax.rem(g.z + k, g.Z)
+            self.add3(z, 1 - g.i2)
+            self.p2_copy(z).start()
+            self.add3(z, g.i2)
+
+    def stage2(self, *ks):
+        g = self.g
+        for k in ks:
+            z = lax.rem(g.z + k, g.Z)
+            self.p2_copy(z).wait_recv()
+            block = g.block(z, g.i2, g.i3)
+            total = self.own(block) + self.value(self.rec2, z)
+            self.part[pl.ds(self.first, self.n), block] = total.astype(self.kind)
+            self.z_copy(k).start()
+
+    def last(self):
+        g = self.g
+        self.p2_copy(g.z).wait_recv()
+        total = self.own(g.block(g.z, g.i2, g.i3)) + self.value(self.rec2, g.z)
+        for k in range(1, g.Z):
+            self.z_copy(k).wait_recv()
+            total += self.value(self.recz, k - 1)
+        self.write(total)
+
+    def sent(self):
+        g = self.g
+        for z in range(g.Z):
+            for a2 in (0, 1):
+                self.p3_copy(z, a2).wait_send()
+            self.p2_copy(z).wait_send()
+        for k in range(1, g.Z):
+            self.z_copy(k).wait_send()
+
+
+def backward_kernel(dp_size, head_dim, *refs):
+    (tok, dout, lens, gain, cosine, sine, wq, wo, wu, wd) = refs[:10]
+    (q_i, k_i, v_i, ob_i, lse_i, araw_i, h_i, mraw_i, bt_i, gt_i, gp_i, at_i, atx_i) = refs[10:23]
+    (dtok, out_q, out_o, out_u, out_d, out_g) = refs[23:29]
+    (gts, dus, dzs) = refs[29:32]
+    (part, rec3, rec2, recz, gpart, grec3, grec2, grecz) = refs[32:40]
+    (f1, f2, acc, dm, dms, da, das, dz, bt, bts, obts, ats, atx, atxs) = refs[40:54]
+    (q, ob, lse, do, bias, dk, dv, dg, dgs, dgt, dnx, dnxs, tile) = refs[54:67]
+    (kbuf, vbuf, wbuf, dbuf, gbuf, gsbuf, gpbuf, sbuf) = refs[67:75]
+    tsems = refs[75:84]
+    usend, urecv, gsend, grecv, zsend, zrecv, osend, orecv, lsem = refs[84:93]
+    dnsem = refs[93]
+    gsems, rsems = refs[94:100], refs[100:106]
+    at, xbuf = bt, gpbuf
+    g = Place(dp_size)
+    Z, y, c = g.Z, g.y, g.c
+    rows, width = tok.shape
+    half = head_dim // 2
+    pairs = width // 128
+    scale = head_dim ** (-0.5)
+    ups = gp_i.shape[0]
+    per = width // 256
+    bf, f32 = jnp.bfloat16, jnp.float32
+    first = pl.multiple_of(y * rows, rows)
+
+    def to_sib(src, dst, send, recv):
+        return pltpu.make_async_remote_copy(
+            src_ref=src,
+            dst_ref=dst,
+            send_sem=send,
+            recv_sem=recv,
+            device_id=g.sib,
+            device_id_type=MESH,
+        )
+
+    def load(src, dst, i):
+        return pltpu.make_async_copy(src, dst, lsem.at[i])
+
+    loads = [
+        load(mraw_i, f1, 0),
+        load(h_i, f2, 1),
+        load(bt_i.at[:, c], bt, 2),
+        load(atx_i.at[:, c], atx, 5),
+        load(q_i, q, 6),
+        load(ob_i, ob, 7),
+        load(lse_i, lse, 8),
+    ]
+    araw_load = load(araw_i, f1, 9)
+    at_load = load(at_i.at[:, c], at, 4)
+    gt_sends = [
+        to_sib(gt_i.at[i, 1 - c], gts.at[i], gsend.at[i], grecv.at[i]) for i in range(2 * Z)
+    ]
+    bt_send = to_sib(bt_i.at[:, 1 - c], bts, osend.at[0], orecv.at[0])
+    ob_send = to_sib(ob_i.at[:, 1 - c], obts, osend.at[1], orecv.at[1])
+    at_send = to_sib(at_i.at[:, 1 - c], ats, osend.at[2], orecv.at[2])
+    atx_send = to_sib(atx_i.at[:, 1 - c], atxs, osend.at[3], orecv.at[3])
+    dm_send = to_sib(dm, dms, osend.at[4], orecv.at[4])
+    da_send = to_sib(da, das, osend.at[5], orecv.at[5])
+    dg_send = to_sib(dg, dgs, osend.at[6], orecv.at[6])
+    dnx_send = pltpu.make_async_remote_copy(
+        src_ref=dnx,
+        dst_ref=dnxs,
+        send_sem=dnsem.at[0],
+        recv_sem=dnsem.at[1],
+        device_id=g.device(g.z, g.x, c, 1 - y),
+        device_id_type=MESH,
+    )
+
+    def du_send(t):
+        return to_sib(dz.at[t], dus.at[t], usend.at[t], urecv.at[t])
+
+    def dz_send(t):
+        return to_sib(dz.at[t], dzs.at[t], zsend.at[t], zrecv.at[t])
+
+    landing = (rec3, rec2, recz)
+
+    def write_d(total):
+        out_d[...] = total.reshape(out_d.shape)
+
+    def write_into(out, column):
+        def write(total):
+            for i in range(total.shape[0]):
+                out[:, column + i * width : column + (i + 1) * width] = total[i]
+
+        return write
+
+    def write_g(total):
+        out_g[...] = total[0]
+
+    s_d = Share(g, part, 0, landing, 0, 4, gsems[0], rsems[0], write_d)
+    s_u = [
+        Share(g, part, 4 + 2 * i, landing, 4 + 2 * i, 2, gsems[1 + i], rsems[1 + i],
+              write_into(out_u, 2 * i * width))
+        for i in (0, 1)
+    ]
+    s_o = Share(g, part, 8, landing, 8, 1, gsems[3], rsems[3], write_into(out_o, 0))
+    s_q = Share(g, part, 0, landing, 9, 3, gsems[4], rsems[4], write_into(out_q, 0))
+    s_g = Share(g, gpart, 0, (grec3, grec2, grecz), 0, 1, gsems[5], rsems[5], write_g)
+
+    for copy in loads[:2]:
+        copy.start()
+    g.barrier()
+    for copy in gt_sends:
+        copy.start()
+    bt_send.start()
+    ob_send.start()
+    at_send.start()
+
+    @pl.when(y == 1)
+    def _():
+        atx_send.start()
+
+    for copy in loads[2:]:
+        copy.start()
+    dg[...] = jnp.zeros_like(dg)
+    ends = doc_ends(lens)
+
+    def upstream(i):
+        e = dout[pl.ds(i * 128, 128), :].astype(f32)
+        place = y * rows + i * 128 + lax.broadcasted_iota(jnp.int32, e.shape, 0)
+        return jnp.where(place < ends[DOCS - 2], e, 0.0)
+
+    def gain_sum(index, term):
+        dg[index : index + 1, :] += jnp.sum(term, axis=0, keepdims=True)
+
+    loads[0].wait()
+
+    @loop(rows // 128)
+    def _(i):
+        spot = pl.ds(i * 128, 128)
+        dv_, term = norm_pull(f1[spot, :], gain[3:4, :], upstream(i))
+        dm[spot, :] = dv_.astype(bf)
+        gain_sum(3, term)
+
+    dm_send.start()
+    araw_load.start()
+
+    def tile_of(j):
+        return lax.rem(g.z + 1 + lax.div(j, 2), Z) * 2 + lax.rem(j, 2)
+
+    def gt_ready(j):
+        i = tile_of(j)
+        to_sib(gt_i.at[i, 1 - c], gts.at[i], gsend.at[i], grecv.at[i]).wait_recv()
+
+    own_g = Tiles(lambda j: gt_i.at[tile_of(j), c], gbuf, tsems[0])
+    sib_g = Tiles(lambda j: gts.at[tile_of(j)], gsbuf, tsems[1], gt_ready)
+    own_g.first()
+    sib_g.first()
+    dm_send.wait_recv()
+
+    @loop(2 * Z)
+    def _(j):
+        i = tile_of(j)
+        total = dot(own_g.get(j, 2 * Z), dm[...]) + dot(sib_g.get(j, 2 * Z), dms[...])
+        total = total.astype(bf).reshape(2, 4, total.shape[0] // 8, width)
+        for a in (0, 1):
+            for e in range(4):
+                part[e, 2 * i + a] = total[a, e]
+
+        @pl.when(lax.rem(j, 2) == 1)
+        def _():
+            s_d.start(lax.div(i, 2))
+
+    downs = Tiles(lambda t: wd.at[pl.ds(pl.multiple_of(t * 256, 256), 256), :], dbuf, tsems[2])
+    upw = Tiles(lambda t: wu.at[:, pl.ds(pl.multiple_of(t * 256, 256), 256)], wbuf, tsems[3])
+    slopes = Tiles(lambda t: gp_i.at[t], gpbuf, tsems[4])
+    for tiles in (downs, upw, slopes):
+        tiles.first()
+    acc[...] = jnp.zeros_like(acc)
+
+    def run_at(t, events):
+        for i, event in events.items():
+
+            @pl.when(t == i)
+            def _():
+                event()
+
+    @loop(ups)
+    def _(t):
+        du = dot_nt(dm[...], downs.get(t, ups)) * slopes.get(t, ups).astype(f32)
+        du = du.astype(bf)
+        dz[t] = du
+        du_send(t).start()
+        acc[...] += dot_nt(du, upw.get(t, ups))
+        run_at(t, {7: lambda: s_d.stage3(1), 14: lambda: s_d.stage3(2)})
+
+    def du_ready(t):
+        du_send(t).wait_recv()
+
+    loads[2].wait()
+    bt_send.wait_recv()
+    sib_du = Tiles(lambda t: dus.at[t], sbuf, tsems[5], du_ready)
+    sib_du.first()
+    for i in (0, 1):
+
+        @loop(ups // 2)
+        def _(t2):
+            t = t2 + i * (ups // 2)
+            total = dot(bt[...].reshape(-1, rows), dz[t])
+            total += dot(bts[...].reshape(-1, rows), sib_du.get(t, ups))
+            total = total.astype(bf).reshape(4 * Z, -1, 256)
+            column = pl.ds(pl.multiple_of(lax.rem(t, per) * 256, 256), 256)
+            part[4 + lax.div(t, per), :, :, column] = total
+
+        s_u[i].start_all()
+        s_d.stage3(3 if i == 0 else 0)
+
+    at_load.start()
+
+    loads[1].wait()
+    araw_load.wait()
+
+    @loop(rows // 128)
+    def _(i):
+        spot = pl.ds(i * 128, 128)
+        dv_, term = norm_pull(f2[spot, :], gain[2:3, :], acc[spot, :])
+        gain_sum(2, term)
+        dh = upstream(i) + dv_
+        f2[spot, :] = dh
+        dv_, term = norm_pull(f1[spot, :], gain[1:2, :], dh)
+        gain_sum(1, term)
+        da[spot, :] = dv_.astype(bf)
+
+    da_send.start()
+    s_d.stage2(1)
+    outs = Tiles(lambda t: wo.at[pl.ds(pl.multiple_of(t * 256, 256), 256), :], dbuf, tsems[2])
+    outs.first()
+
+    @loop(per)
+    def _(t):
+        u = dot_nt(da[...], outs.get(t, per)).astype(bf)
+        do[2 * t] = u[:, :128]
+        do[2 * t + 1] = u[:, 128:]
+
+    loads[5].wait()
+    ob_send.wait_recv()
+    da_send.wait_recv()
+
+    @loop(per)
+    def _(t):
+        column = pl.ds(pl.multiple_of(t * 256, 256), 256)
+        total = dot(ob[:, c].reshape(-1, rows), da[:, column])
+        total += dot(obts[...].reshape(-1, rows), das[:, column])
+        part[8, :, :, column] = total.astype(bf).reshape(4 * Z, -1, 256)
+
+    s_o.start_all()
+    s_d.stage2(2, 3)
+    for t in range(ups):
+        du_send(t).wait_send()
+
+    fill_bias(bias, lens, y * rows, rows)
+    loads[4].wait()
+    loads[6].wait()
+    keys = Tiles(lambda p: k_i.at[p], kbuf, tsems[6])
+    values = Tiles(lambda p: v_i.at[p], vbuf, tsems[7])
+    keys.first()
+    values.first()
+    blocks = rows // 256
+
+    def attend(p, block, count, fresh, kk, vv, kt):
+        spot = slice(block * 256, block * 256 + 256)
+        qs = split_heads(q[p, spot, :])
+        dos = split_heads(do[p, spot, :])
+        dot_o = jnp.transpose(do[p, spot, :].astype(f32)) * ob_pair(p, spot)
+        parts = []
+        dk_, dv_ = [], []
+        for i in (0, 1):
+            delta = jnp.sum(
+                dot_o[i * head_dim : (i + 1) * head_dim], axis=0, keepdims=True
+            )
+            s = dot_nt(kk, qs[i]) + bias[:count, spot]
+            prob = jnp.exp(s - lse[p, i : i + 1, spot])
+            ds = (prob * (dot_nt(vv, dos[i]) - delta)).astype(bf)
+            dv_.append(dot(prob.astype(bf), dos[i]))
+            dk_.append(dot(ds, qs[i]))
+            parts.append(dot(kt, ds))
+        if fresh:
+            dk[:count, :] = dk_[0] + dk_[1]
+            dv[:count, :] = dv_[0] + dv_[1]
+        else:
+            dk[:count, :] += dk_[0] + dk_[1]
+            dv[:count, :] += dv_[0] + dv_[1]
+        upper = lax.broadcasted_iota(jnp.int32, parts[0].shape, 0) < head_dim
+        dq = jnp.transpose(jnp.where(upper, parts[0], parts[1]) * scale)
+        start = pl.multiple_of(first + block * 256, 256)
+        dq = turn(dq, cosine[pl.ds(start, 256), :], -sine[pl.ds(start, 256), :], half)
+        dz[lax.div(p, 2), spot, lanes(p)] = dq.astype(bf)
+
+    def ob_pair(p, spot):
+        return ob[p, :, :, spot].astype(f32).reshape(128, -1)
+
+    def lanes(p):
+        return pl.ds(pl.multiple_of(lax.rem(p, 2) * 128, 128), 128)
+
+    def keep(p, start, base):
+        spot = pl.ds(start, rows)
+        u = turn(dk[spot, :], cosine[spot, :], -sine[spot, :], half)
+        dz[base + lax.div(p, 2), :, lanes(p)] = u.astype(bf)
+        dz[base + per + lax.div(p, 2), :, lanes(p)] = dv[spot, :].astype(bf)
+
+    events = {
+        0: lambda: s_u[0].stage3(1, 2),
+        1: lambda: (s_u[0].stage3(3, 0), s_d.last()),
+        2: lambda: s_u[1].stage3(1, 2),
+        3: lambda: s_u[0].stage2(1, 2, 3),
+        4: lambda: s_u[1].stage3(3, 0),
+        5: lambda: (s_o.stage3(1, 2, 3, 0), s_u[1].stage2(1, 2, 3)),
+        6: lambda: (s_o.stage2(1, 2, 3), s_u[0].last()),
+        7: lambda: s_u[1].last(),
+    }
+
+    @loop(pairs)
+    def _(p):
+        kk = keys.get(p, pairs)
+        vv = values.get(p, pairs)
+        kt = jnp.transpose(kk.astype(f32)).astype(bf)
+        for half_row in (0, 1):
+
+            @pl.when(y == half_row)
+            def _():
+                for block in reversed(range(blocks)):
+                    count = (half_row * blocks + block + 1) * 256
+                    attend(p, block, count, block == blocks - 1, kk[:count], vv[:count], kt[:, :count])
+
+        keep(p, first, per)
+
+        @pl.when(y == 1)
+        def _():
+            keep(p, 0, 3 * per)
+
+        @pl.when(lax.rem(p, 2) == 1)
+        def _():
+            for e in range(3):
+                dz_send(e * per + lax.div(p, 2)).start()
+
+            @pl.when(y == 1)
+            def _():
+                for e in (3, 4):
+                    dz_send(e * per + lax.div(p, 2)).start()
+
+        run_at(p, events)
+
+    s_o.last()
+
+    qkv_w = Tiles(lambda t: wq.at[:, pl.ds(pl.multiple_of(t * 256, 256), 256)], wbuf, tsems[3])
+
+    @pl.when(y == 1)
+    def _():
+        acc[...] = jnp.zeros_like(acc)
+        qkv_w.first(per)
+
+        @loop(2 * per)
+        def _(t):
+            acc[...] += dot_nt(dz[t + 3 * per], qkv_w.get(t + per, 3 * per))
+
+        dnx[...] = acc[...].astype(bf)
+        dnx_send.start()
+
+    s_d.sent()
+    loads[3].wait()
+    at_load.wait()
+    at_send.wait_recv()
+
+    @pl.when(y == 1)
+    def _():
+        atx_send.wait_recv()
+
+    def dz_ready(t):
+        dz_send(t).wait_recv()
+
+    sib_dz = Tiles(lambda t: dzs.at[t], sbuf, tsems[5], dz_ready)
+    sib_dx = Tiles(lambda t: dzs.at[t], xbuf, tsems[8], dz_ready)
+    sib_dz.first()
+
+    @pl.when(y == 1)
+    def _():
+        sib_dx.first(3 * per)
+
+    @loop(3 * per)
+    def _(t):
+        tile[...] = dot(at[...].reshape(-1, rows), dz[t])
+        tile[...] += dot(ats[...].reshape(-1, rows), sib_dz.get(t, 3 * per))
+
+        @pl.when((y == 1) & (t >= per))
+        def _():
+            tx = t + 2 * per
+            tile[...] += dot(atx[...].reshape(-1, rows), dz[tx])
+            tile[...] += dot(atxs[...].reshape(-1, rows), sib_dx.get(tx, 5 * per))
+
+        column = pl.ds(pl.multiple_of(lax.rem(t, per) * 256, 256), 256)
+        part[lax.div(t, per), :, :, column] = tile[...].astype(bf).reshape(4 * Z, -1, 256)
+
+    s_q.start_all()
+
+    acc[...] = jnp.zeros_like(acc)
+    qkv_w.first()
+
+    @loop(3 * per)
+    def _(t):
+        acc[...] += dot_nt(dz[t], qkv_w.get(t, 3 * per))
+
+    @pl.when(y == 0)
+    def _():
+        dnx_send.wait_recv()
+        acc[...] += dnxs[...].astype(f32)
+
+    @loop(rows // 128)
+    def _(i):
+        spot = pl.ds(i * 128, 128)
+        dv_, term = norm_pull(tok[spot, :].astype(f32), gain[0:1, :], acc[spot, :])
+        gain_sum(0, term)
+        dtok[spot, :] = (f2[spot, :] + dv_).astype(bf)
+
+    dg_send.start()
+    s_q.stage3(1)
+    dg_send.wait_recv()
+    wide = jnp.concatenate([dg[...] + dgs[...], jnp.zeros((120, width), f32)], axis=0)
+    dgt[...] = jnp.transpose(wide).reshape(dgt.shape)
+    gpart[0] = dgt[:, c].reshape(gpart.shape[1:])
+    s_g.start_all()
+    s_q.stage3(2, 3, 0)
+    s_g.stage3(1, 2, 3, 0)
+    s_q.stage2(1, 2, 3)
+    s_g.stage2(1, 2, 3)
+    s_q.last()
+    s_g.last()
+
+    for copy in gt_sends + [bt_send, ob_send, at_send, dm_send, da_send, dg_send]:
+        copy.wait_send()
+    for t in range(3 * per):
+        dz_send(t).wait_send()
+
+    @pl.when(y == 1)
+    def _():
+        atx_send.wait_send()
+        dnx_send.wait_send()
+        for t in range(3 * per, 5 * per):
+            dz_send(t).wait_send()
+
+    for s in (s_u[0], s_u[1], s_o, s_q, s_g):
+        s.sent()
+
+
+def backward(tokens, d_out, lengths, gain_rows, tables, weights, saved, shards):
+    dp_size = lax.axis_size("dp")
+    Z = dp_size // 4
+    rows, width = tokens.shape
+    row_len = rows * lax.axis_size("ctx")
+    head_dim = width // HEADS
+    pairs = width // 128
+    per = width // 256
+    bf, f32 = jnp.bfloat16, jnp.float32
+    ups = saved[10].shape[0]
+    any_spec = pl.BlockSpec(memory_space=pl.ANY)
+    vm = pl.BlockSpec(memory_space=pltpu.VMEM)
+    smem = pl.BlockSpec(memory_space=pltpu.SMEM)
+    shape = jax.ShapeDtypeStruct
+    block = 32
+    saved = list(saved)
+    for i in (3, 8, 11, 12):
+        saved[i] = saved[i].reshape(2 * Z, 2, width // (4 * Z), rows)
+    saved[9] = saved[9].reshape(2 * Z, 2, 256, rows)
+    outs = [
+        shape((rows, width), bf),
+        shape((shards[0].shape[0], shards[0].shape[1]), f32),
+        shape(shards[1].shape, f32),
+        shape(shards[2].shape, f32),
+        shape(shards[3].shape, f32),
+        shape((block, 128), f32),
+        shape((2 * Z, 256, rows), bf),
+        shape((ups, rows, 256), bf),
+        shape((5 * per, rows, 256), bf),
+    ]
+    core_rows = (2 * Z, width // (4 * Z), rows)
+    scratch = [
+        pltpu.VMEM((9, 4 * Z, block, width), bf),
+        pltpu.VMEM((12, 2 * Z, block, width), bf),
+        pltpu.VMEM((12, Z, block, width), bf),
+        pltpu.VMEM((12, Z - 1, block, width), bf),
+        pltpu.VMEM((1, 4 * Z, block, 128), f32),
+        pltpu.VMEM((1, 2 * Z, block, 128), f32),
+        pltpu.VMEM((1, Z, block, 128), f32),
+        pltpu.VMEM((1, Z - 1, block, 128), f32),
+        pltpu.VMEM((rows, width), f32),
+        pltpu.VMEM((rows, width), f32),
+        pltpu.VMEM((rows, width), f32),
+        pltpu.VMEM((rows, width), bf),
+        pltpu.VMEM((rows, width), bf),
+        pltpu.VMEM((rows, width), bf),
+        pltpu.VMEM((rows, width), bf),
+        pltpu.VMEM((max(ups, 5 * per), rows, 256), bf),
+    ]
+    scratch += [pltpu.VMEM(core_rows, bf)] * 6
+    scratch += [
+        pltpu.VMEM((pairs, rows, 128), bf),
+        pltpu.VMEM((2 * Z, 2, width // (4 * Z), rows), bf),
+        pltpu.VMEM((pairs, 2, rows), f32),
+        pltpu.VMEM((pairs, rows, 128), bf),
+        pltpu.VMEM((row_len, rows), f32),
+        pltpu.VMEM((row_len, 128), f32),
+        pltpu.VMEM((row_len, 128), f32),
+        pltpu.VMEM((8, width), f32),
+        pltpu.VMEM((8, width), f32),
+        pltpu.VMEM((2 * Z, 2, width // (4 * Z), 128), f32),
+        pltpu.VMEM((rows, width), bf),
+        pltpu.VMEM((rows, width), bf),
+        pltpu.VMEM((rows, 256), f32),
+        pltpu.VMEM((2, row_len, 128), bf),
+        pltpu.VMEM((2, row_len, 128), bf),
+        pltpu.VMEM((2, width, 256), bf),
+        pltpu.VMEM((2, 256, width), bf),
+        pltpu.VMEM((2, 256, rows), bf),
+        pltpu.VMEM((2, 256, rows), bf),
+        pltpu.VMEM((2, rows, 256), bf),
+        pltpu.VMEM((2, rows, 256), bf),
+    ]
+    dma = pltpu.SemaphoreType.DMA
+    scratch += [dma((2,))] * 9
+    scratch += [dma((ups,))] * 2 + [dma((2 * Z,))] * 2 + [dma((5 * per,))] * 2
+    scratch += [dma((7,))] * 2 + [dma((10,)), dma((2,))]
+    scratch += [dma((Share.sems(Z),))] * 12
+    return pl.pallas_call(
+        functools.partial(backward_kernel, dp_size, head_dim),
+        out_shape=outs,
+        in_specs=[vm, vm, smem, vm, vm, vm] + [any_spec] * 17,
+        out_specs=[vm] * 6 + [any_spec] * 3,
+        scratch_shapes=scratch,
+        compiler_params=pltpu.CompilerParams(
+            collective_id=1, has_side_effects=True, vmem_limit_bytes=63 * 2**20
+        ),
+    )(tokens, d_out, lengths, gain_rows, *tables, *weights, *saved)
 
 
 def layer_norm(values, gain_vec):
@@ -1167,128 +1805,32 @@
 
 
 def fused_device(tokens, lengths, w_qkv, w_out, w_up, w_down, gains, d_out):
-    tok_rows, model_width = tokens.shape
-    row_len = tok_rows * lax.axis_size("ctx")
-    head_count = HEADS
-    head_dim = model_width // head_count
-    score_scale = head_dim ** (-0.5)
-    head_shape = (tok_rows, head_count, head_dim)
-    seg_full, pos_full, valid_full = doc_layout(lengths, row_len)
-    offset = lax.axis_index("ctx") * tok_rows
-    own_seg = lax.dynamic_slice_in_dim(seg_full, offset, tok_rows)
-    own_valid = lax.dynamic_slice_in_dim(valid_full.astype(jnp.float32), offset, tok_rows)
-    own_place = offset + jnp.arange(tok_rows, dtype=jnp.int32)
+    rows, width = tokens.shape
+    row_len = rows * lax.axis_size("ctx")
     gains_wide = jnp.pad(gains, ((0, 0), (0, 128 - gains.shape[1])))
-    cos_np, sin_np = turn_tables(row_len, head_dim)
-    tables = (jnp.asarray(cos_np), jnp.asarray(sin_np))
-    (output, qkv_back, out_back, up_back, down_back, gain_rows, qs, ks, vs, obs, lse, attn_raw, hidden,
-     mlp_raw, bts, gts, gps, ats, atx) = forward(
-        tokens, lengths, gains_wide, w_qkv, w_out, w_up, w_down, tables)
-    gain_f = gain_rows[:4].T
-    stream = tokens.astype(jnp.float32)
-    def unpair(v):
-        return jnp.transpose(v, (1, 0, 2)).reshape(v.shape[1], head_count, head_dim)
-    seen = (jnp.arange(row_len) < offset + tok_rows)[:, None, None]
-    queries = unpair(qs)
-    key_all, value_all = jnp.where(seen, unpair(ks), 0), jnp.where(seen, unpair(vs), 0)
-    attended_b = obs.reshape(model_width, tok_rows).T
-    attended = attended_b.astype(jnp.float32).reshape(head_shape)
-    row_max = lse.reshape(head_count, tok_rows)
-    row_sum = jnp.ones_like(row_max)
-    mlp_in = bts.T
-    normed_x = ats.T
-    activated = jnp.transpose(gts, (2, 0, 1)).reshape(tok_rows, -1)
-    gp = jnp.transpose(gps, (1, 0, 2)).reshape(tok_rows, -1).astype(jnp.float32)
-    upstream = d_out.astype(jnp.float32) * own_valid[:, None]
-    d_mlp, d_gain_four = norm_back(mlp_raw, gain_f[:, 3], upstream)
-    d_mlp_b = d_mlp.astype(jnp.bfloat16)
-    grad_down = jnp.einsum("tf,td->fd", activated, d_mlp_b, preferred_element_type=jnp.float32)
-    d_activated = jnp.einsum("td,fd->tf", d_mlp_b, down_back, preferred_element_type=jnp.float32)
-    d_up_b = (d_activated * gp).astype(jnp.bfloat16)
-    grad_up = jnp.einsum("td,tf->df", mlp_in, d_up_b, preferred_element_type=jnp.float32)
-    d_mlp_in = jnp.einsum("tf,df->td", d_up_b, up_back, preferred_element_type=jnp.float32)
-    d_hidden_part, d_gain_three = norm_back(hidden, gain_f[:, 2], d_mlp_in)
-    d_hidden = upstream + d_hidden_part
-    d_attn, d_gain_two = norm_back(attn_raw, gain_f[:, 1], d_hidden)
-    d_attn_b = d_attn.astype(jnp.bfloat16)
-    grad_out = jnp.einsum("td,te->de", attended_b, d_attn_b, preferred_element_type=jnp.float32)
-    d_attended = (
-        jnp.einsum("te,de->td", d_attn_b, out_back, preferred_element_type=jnp.float32)
-        .astype(jnp.bfloat16)
-        .reshape(head_shape)
+    tables = tuple(jnp.asarray(v) for v in turn_tables(row_len, width // HEADS))
+    output, wq, wo, wu, wd, gain_rows, *saved = forward(
+        tokens, lengths, gains_wide, w_qkv, w_out, w_up, w_down, tables
     )
-    row_dot = jnp.einsum("qhd,qhd->hq", d_attended.astype(jnp.float32), attended)
-    block_rows = math.gcd(row_len, 256)
-    block_count = row_len // block_rows
-    key_blocks = key_all.reshape((block_count, block_rows) + key_all.shape[1:])
-    value_blocks = value_all.reshape((block_count, block_rows) + value_all.shape[1:])
-
-    def back_block(d_queries, block_items):
-        key_block, value_block, block_id = block_items
-        allowed = allowed_keys(own_seg, own_place, seg_full, block_id * block_rows, block_rows)
-        scores = (
-            jnp.einsum("qhd,khd->hqk", queries, key_block, preferred_element_type=jnp.float32)
-        )
-        attn_prob = jnp.where(
-            allowed[None], jnp.exp(scores - row_max[..., None]) / row_sum[..., None], 0.0
-        )
-        d_prob = jnp.einsum(
-            "qhd,khd->hqk", d_attended, value_block, preferred_element_type=jnp.float32
-        )
-        d_scores = (attn_prob * (d_prob - row_dot[..., None])).astype(jnp.bfloat16)
-        d_queries = (
-            d_queries
-            + jnp.einsum("hqk,khd->qhd", d_scores, key_block, preferred_element_type=jnp.float32)
-            * score_scale
-        )
-        d_keys = (
-            jnp.einsum("hqk,qhd->khd", d_scores, queries, preferred_element_type=jnp.float32)
-        )
-        d_values = jnp.einsum(
-            "hqk,qhd->khd",
-            attn_prob.astype(jnp.bfloat16),
-            d_attended,
-            preferred_element_type=jnp.float32,
-        )
-        return (d_queries, (d_keys, d_values))
-
-    block_ids = jnp.arange(block_count, dtype=jnp.int32)
-    d_queries, (d_keys_all, d_values_all) = lax.scan(
-        back_block, jnp.zeros(head_shape, jnp.float32), (key_blocks, value_blocks, block_ids)
+    d_tokens, grad_qkv, grad_out, grad_up, grad_down, grad_gains = backward(
+        tokens,
+        d_out,
+        lengths,
+        gain_rows,
+        tables,
+        (wq, wo, wu, wd),
+        saved,
+        (w_qkv, w_out, w_up, w_down),
+    )[:6]
+    return (
+        output,
+        d_tokens,
+        grad_qkv,
+        grad_out,
+        grad_up,
+        grad_down,
+        grad_gains[:, : gains.shape[1]],
     )
-    kv_terms = jnp.concatenate(
-        [d_keys_all.reshape(row_len, model_width), d_values_all.reshape(row_len, model_width)],
-        axis=-1,
-    )
-    kv_grad = lax.psum_scatter(
-        kv_terms.astype(jnp.bfloat16), "ctx", scatter_dimension=0, tiled=True
-    ).astype(jnp.float32)
-    place = offset + jnp.arange(tok_rows)
-    inv = 10000.0 ** (-2.0 * np.arange(head_dim // 2) / head_dim)
-    angles = place.astype(jnp.float32)[:, None] * jnp.asarray(inv, jnp.float32)
-    cosine_table = jnp.cos(angles)[:, None, :]
-    sine_table = jnp.sin(angles)[:, None, :]
-    d_keys = kv_grad[:, :model_width].reshape(head_shape)
-    d_qkv = jnp.concatenate(
-        [
-            rotate(d_queries, cosine_table, sine_table, -1.0).reshape(tok_rows, model_width),
-            rotate(d_keys, cosine_table, sine_table, -1.0).reshape(tok_rows, model_width),
-            kv_grad[:, model_width:],
-        ],
-        axis=-1,
-    ).astype(jnp.bfloat16)
-    grad_qkv = jnp.einsum("td,te->de", normed_x, d_qkv, preferred_element_type=jnp.float32)
-    d_normed = jnp.einsum("te,de->td", d_qkv, qkv_back, preferred_element_type=jnp.float32)
-    d_stream_part, d_gain_one = norm_back(stream, gain_f[:, 0], d_normed)
-    d_tokens = (d_hidden + d_stream_part).astype(jnp.bfloat16)
-    grad_gains = jnp.stack([d_gain_one, d_gain_two, d_gain_three, d_gain_four], axis=-1)
-    grad_gains = jnp.pad(grad_gains, ((0, 0), (0, 128 - gains.shape[1])))
-    shard_down, shard_up, shard_out, shard_qkv, shard_gains = scatter_all(
-        [v.astype(jnp.bfloat16) for v in (grad_down, grad_up, grad_out, grad_qkv, grad_gains)],
-        (False,) * 5,
-    )
-    shard_gains = shard_gains[:, : gains.shape[1]]
-    return (output, d_tokens, shard_qkv, shard_out, shard_up, shard_down, shard_gains)
 
 
 def layer(mesh):

time: 665 us -> 394 us (0.59)
  the two profiles are of different devices: /device:TPU:0 before, /device:TPU:1 now
where the time goes in v3:
time: 394 us; the launch traced here: 393 us
  Pallas kernels  381 us (97%)
  local copies, waits for them, and re-layouts  10.4 us (3%)
    pallas_call x1, Pallas kernels, backward(): pl.pallas_call(functools.partial(backward_kernel, dp_size, head_dim), out...  195 us
    pallas_call x1, Pallas kernels, forward(): pl.pallas_call(functools.partial(forward_kernel, dp_size, head_dim), out_...  186 us
    unnamed x16, local copies, waits for them, and re-layouts  9.78 us

profile of v3, /device:TPU:1, one launch (start us, length us, event | category | flops | bytes accessed | tf_op | source)
XLA Modules:
  0.0 392.6 jit_solution(3213475324694821872)
XLA Ops:
  0.6 0.8 copy.17
  1.4 0.6 pad.4.refs_2_
  2.0 186.2 %shard_map.153 = (bf16[512,1024]{1,0:T(8,128)(2,1)}, bf16[1024,3072]{1,0:T(8,128)(2,1)}, bf16[1024,1024]{1,0:T(8,128)(2,1)}, bf16[1024,4096]{1,0:T(8,128)(2,1)},...) custom-call(bf16[512,1024]{1,0:T(8,128)(2,1)} %refs_0_.3, ...), custom_call_target="tpu_custom_call" | custom-call | tf_op jit(solution)/shard_map/pallas_call | solution.py:929
  188.2 195.3 %shard_map.154 = (bf16[512,1024]{1,0:T(8,128)(2,1)}, f32[32,3072]{1,0:T(8,128)}, f32[32,1024]{1,0:T(8,128)}, f32[32,4096]{1,0:T(8,128)}, f32[128,1024]{1,0:T(8,1...) custom-call(bf16[512,1024]{1,0:T(8,128)(2,1)} %refs_0_.3, ...), custom_call_target="tpu_custom_call" | custom-call | tf_op jit(solution)/shard_map/pallas_call | solution.py:1564
  383.5 0.0 copy-start.2
  383.5 0.0 copy-start.3
  383.5 0.0 copy-start.1
  383.5 0.0 copy-start
  383.6 1.5 copy.18
  385.0 2.3 copy.25
  387.3 2.3 copy.26
  389.6 0.0 copy-done.2
  389.6 0.7 copy.27
  390.3 0.0 copy-done.3
  390.3 0.7 copy.28
  391.0 0.0 copy-done.1
  391.0 0.8 copy.29
  391.8 0.0 copy-done
  391.8 0.8 copy.30
Async XLA Ops:
  383.5 6.0 %copy-start.2 = (f32[32,3072]{1,0:T(8,128)S(1)}, f32[32,3072]{1,0:T(8,128)}, u32[]{:S(2)}) copy-start(f32[32,3072]{1,0:T(8,128)} %get-tuple-element.73) | copy-start | bytes 1179652
  383.5 6.8 %copy-start.3 = (f32[32,1024]{1,0:T(8,128)S(1)}, f32[32,1024]{1,0:T(8,128)}, u32[]{:S(2)}) copy-start(f32[32,1024]{1,0:T(8,128)} %get-tuple-element.74) | copy-start | bytes 393220
  383.5 7.4 %copy-start.1 = (f32[32,4096]{1,0:T(8,128)S(1)}, f32[32,4096]{1,0:T(8,128)}, u32[]{:S(2)}) copy-start(f32[32,4096]{1,0:T(8,128)} %get-tuple-element.75) | copy-start | bytes 1572868
  383.5 8.2 %copy-start = (f32[128,1024]{1,0:T(8,128)S(1)}, f32[128,1024]{1,0:T(8,128)}, u32[]{:S(2)}) copy-start(f32[128,1024]{1,0:T(8,128)} %get-tuple-element.76) | copy-start | bytes 1572868

commit v4 on v3

v4 whole, which is shorter than its diff:
```python
import functools
import math

import jax
import jax.numpy as jnp
import numpy as np
from jax import lax
from jax.experimental import pallas as pl
from jax.experimental.pallas import tpu as pltpu
from jax.sharding import PartitionSpec as P

HEADS = 16
DOCS = 7
MODES = (False, False, False, False)

epsilon = 1e-05
masked_score = -1e30


MESH = pl.DeviceIdType.MESH


def when(condition, body):
    if isinstance(condition, bool):
        if condition:
            body()
    else:
        pl.when(condition)(body)


def unless(condition, body):
    if isinstance(condition, bool):
        if not condition:
            body()
    else:
        pl.when(jnp.logical_not(condition))(body)


def pick(condition, one, other):
    if isinstance(condition, bool):
        return one if condition else other
    return jnp.where(condition, one, other)


class Place:
    def __init__(self, dp_size):
        dp = lax.axis_index("dp")
        self.Z = dp_size // 4
        self.z = lax.div(dp, 4)
        self.x = lax.rem(lax.div(dp, 2), 2)
        self.c = lax.rem(dp, 2)
        self.y = lax.axis_index("ctx")
        c, x, y = self.c, self.x, self.y
        self.i2 = y * (1 - c) + x * c
        self.i3 = x * (1 - c) + y * c
        self.sib = self.device(self.z, x, 1 - c, y)
        self.p2 = self.device(self.z, x * (1 - c) + (1 - x) * c, c, (1 - y) * (1 - c) + y * c)
        self.p3 = self.device(self.z, (1 - x) * (1 - c) + x * c, c, y * (1 - c) + (1 - y) * c)

    def device(self, z, x, c, y):
        return ((z * 2 + x) * 2 + c, y)

    def above(self, k):
        return lax.rem(self.z + k, self.Z)

    def below(self, k):
        return lax.rem(self.z - k + self.Z, self.Z)

    def at_z(self, z):
        return self.device(z, self.x, self.c, self.y)

    def block(self, z, a2, a3):
        c = self.c
        return (z * 2 + a3 * (1 - c) + a2 * c) * 2 + a2 * (1 - c) + a3 * c

    def row_block(self, z, a2, a3, core):
        c = self.c
        xx = a3 * (1 - c) + a2 * c
        yy = a2 * (1 - c) + a3 * c
        return ((z * 2 + xx) * 2 + core) * 2 + yy

    def barrier(self):
        bar = pltpu.get_barrier_semaphore()
        for device in (self.sib, self.p2, self.p3):
            pl.semaphore_signal(bar, 1, device_id=device, device_id_type=MESH)
        for k in range(1, self.Z):
            pl.semaphore_signal(
                bar, 1, device_id=self.at_z(self.above(k)), device_id_type=MESH
            )
        pl.semaphore_wait(bar, 3 + self.Z - 1)


class Gather:
    def __init__(self, place, shard, full, send, recv, by_z):
        self.g, self.shard, self.full = place, shard, full
        self.send, self.recv = send, recv
        self.rows = shard.shape[0]
        self.by_z = by_z
        Z = place.Z
        self.n_z = 0
        self.n_p2 = 2 * (Z - 1)
        self.n_p3 = self.n_p2 + Z
        self.n_sib = self.n_p3 + 2 * Z
        self.n_own = self.n_sib + 4 * Z

    @staticmethod
    def sems(Z):
        return 2 * (Z - 1) + Z + 2 * Z + 4 * Z + 1

    def at(self, index):
        return self.full.at[pl.ds(pl.multiple_of(index * self.rows, self.rows), self.rows)]

    def copy(self, index, number, device, src=None):
        return pltpu.make_async_remote_copy(
            src_ref=self.at(index) if src is None else src,
            dst_ref=self.at(index),
            send_sem=self.send.at[number],
            recv_sem=self.recv.at[number],
            device_id=device,
            device_id_type=MESH,
        )

    def own_copy(self):
        g = self.g
        index = g.row_block(g.z, g.i2, g.i3, g.c)
        return pltpu.make_async_copy(self.shard, self.at(index), self.recv.at[self.n_own])

    def z_copy(self, other, k, src=None):
        g = self.g
        a2 = (1 - g.i2) if other else g.i2
        number = self.n_z + (k - 1) * 2 + int(other)
        return self.copy(g.row_block(g.z, a2, g.i3, g.c), number, g.at_z(g.above(k)), src)

    def p2_copy(self, z, src=None):
        g = self.g
        return self.copy(g.row_block(z, g.i2, g.i3, g.c), self.n_p2 + z, g.p2, src)

    def p3_copy(self, z, a2, src=None):
        g = self.g
        return self.copy(g.row_block(z, a2, g.i3, g.c), self.n_p3 + z * 2 + a2, g.p3, src)

    def sib_copy(self, z, a2, a3, src=None):
        g = self.g
        number = self.n_sib + g.block(z, a2, a3)
        return self.copy(g.row_block(z, a2, a3, g.c), number, g.sib, src)

    def wait(self, number, index):
        self.copy(index, number, self.g.sib).wait_recv()

    def start(self):
        g, src = self.g, self.shard
        self.p2_copy(g.z, src).start()
        self.p3_copy(g.z, g.i2, src).start()
        for k in range(1, g.Z):
            self.z_copy(False, k, src).start()
        self.sib_copy(g.z, g.i2, g.i3, src).start()
        self.own_copy().start()

    def first_p2(self):
        g = self.g
        o2 = 1 - g.i2
        self.wait(self.n_p2 + g.z, g.row_block(g.z, o2, g.i3, g.c))

        def along_z():
            for k in range(1, g.Z):
                self.z_copy(True, k).start()

        when(self.by_z, along_z)
        self.p3_copy(g.z, o2).start()
        self.sib_copy(g.z, o2, g.i3).start()

    def arrived_z(self, k):
        g = self.g
        z = g.below(k)
        self.wait(self.n_z + (k - 1) * 2, g.row_block(z, g.i2, g.i3, g.c))
        unless(self.by_z, lambda: self.p2_copy(z).start())
        self.p3_copy(z, g.i2).start()
        self.sib_copy(z, g.i2, g.i3).start()

    def later_p2(self, k):
        g = self.g
        z = g.below(k)
        o2 = 1 - g.i2
        number = pick(self.by_z, self.n_z + (k - 1) * 2 + 1, self.n_p2 + z)
        self.wait(number, g.row_block(z, o2, g.i3, g.c))
        self.p3_copy(z, o2).start()
        self.sib_copy(z, o2, g.i3).start()

    def all_z(self):
        for k in range(1, self.g.Z):
            self.arrived_z(k)

    def all_p2(self):
        for k in range(1, self.g.Z):
            self.later_p2(k)

    def arrived_p3(self, z):
        g = self.g
        for a2 in (0, 1):
            self.wait(self.n_p3 + z * 2 + a2, g.row_block(z, a2, 1 - g.i3, g.c))
            self.sib_copy(z, a2, 1 - g.i3).start()

    def all_p3(self):
        g = self.g
        for k in range(g.Z):
            self.arrived_p3(g.below(k))

    def arrived_sib(self, z):
        g = self.g
        for xx in (0, 1):
            for yy in (0, 1):
                number = self.n_sib + (z * 2 + xx) * 2 + yy
                self.wait(number, ((z * 2 + xx) * 2 + 1 - g.c) * 2 + yy)

    def complete(self):
        for z in range(self.g.Z):
            self.arrived_sib(z)
        self.own_copy().wait()

    def sent(self):
        g, src = self.g, self.shard
        self.p2_copy(g.z, src).wait_send()
        self.p3_copy(g.z, g.i2, src).wait_send()
        self.sib_copy(g.z, g.i2, g.i3, src).wait_send()
        for k in range(1, g.Z):
            self.z_copy(False, k, src).wait_send()
            z = g.above(k)
            when(self.by_z, lambda: self.z_copy(True, k).wait_send())
            unless(self.by_z, lambda: self.p2_copy(z).wait_send())
            self.p3_copy(z, g.i2).wait_send()
            self.sib_copy(z, g.i2, g.i3).wait_send()
        for z in range(g.Z):
            self.p3_copy(z, 1 - g.i2).wait_send()
            self.sib_copy(z, 1 - g.i2, g.i3).wait_send()
            for a2 in (0, 1):
                self.sib_copy(z, a2, 1 - g.i3).wait_send()


class Share:
    def __init__(self, place, part, first, landing, unit, n, send, recv, write, by_z):
        self.g, self.part, self.first = place, part, first
        self.rec3, self.rec = landing
        self.unit, self.n, self.send, self.recv, self.write = unit, n, send, recv, write
        self.kind, self.by_z = part.dtype, by_z

    @staticmethod
    def sems(Z):
        return 4 * Z - 1

    def copy(self, block, landing, slot, number, device):
        return pltpu.make_async_remote_copy(
            src_ref=self.part.at[pl.ds(self.first, self.n), block],
            dst_ref=landing.at[pl.ds(self.unit, self.n), slot],
            send_sem=self.send.at[number],
            recv_sem=self.recv.at[number],
            device_id=device,
            device_id_type=MESH,
        )

    def p3_copy(self, z, a2):
        g = self.g
        slot = z * 2 + a2
        return self.copy(g.block(z, a2, 1 - g.i3), self.rec3, slot, slot, g.p3)

    def p2_copy(self, z):
        g = self.g
        slot = pick(self.by_z, 0, z)
        block = g.block(z, 1 - g.i2, g.i3)
        return self.copy(block, self.rec, slot, 2 * g.Z + slot, g.p2)

    def z_copy(self, k, a2, by_z):
        g = self.g
        z = g.above(k)
        slot = 1 + (k - 1) * 2 + a2 if by_z else g.Z + k - 1
        return self.copy(g.block(z, a2, g.i3), self.rec, slot, 2 * g.Z + slot, g.at_z(z))

    def landed(self, ref, slot):
        return ref[pl.ds(self.unit, self.n), slot].astype(jnp.float32)

    def own(self, block):
        return self.part[pl.ds(self.first, self.n), block].astype(jnp.float32)

    def put(self, block, total):
        self.part[pl.ds(self.first, self.n), block] = total.astype(self.kind)

    def start(self, z):
        for a2 in (0, 1):
            self.p3_copy(z, a2).start()

    def start_all(self):
        g = self.g
        for k in range(1, g.Z + 1):
            self.start(g.above(k))

    def add3(self, z, a2):
        g = self.g
        self.p3_copy(z, a2).wait_recv()
        block = g.block(z, a2, g.i3)
        self.put(block, self.own(block) + self.landed(self.rec3, z * 2 + a2))

    def stage3(self, *ks):
        g = self.g
        for k in ks:
            z = g.above(k)
            o2 = 1 - g.i2
            self.add3(z, o2)
            if k > 0:
                when(self.by_z, lambda: self.z_copy(k, o2, True).start())
            unless(self.by_z, lambda: self.p2_copy(z).start())
            self.add3(z, g.i2)
            if k > 0:
                when(self.by_z, lambda: self.z_copy(k, g.i2, True).start())

    def stage2(self):
        g = self.g

        def with_p2():
            for k in range(1, g.Z):
                z = g.above(k)
                self.p2_copy(z).wait_recv()
                block = g.block(z, g.i2, g.i3)
                self.put(block, self.own(block) + self.landed(self.rec, z))
                self.z_copy(k, g.i2, False).start()

        def along_z():
            o2 = 1 - g.i2
            block = g.block(g.z, o2, g.i3)
            total = self.own(block)
            for k in range(1, g.Z):
                self.z_copy(k, o2, True).wait_recv()
                total += self.landed(self.rec, 1 + (k - 1) * 2 + o2)
            self.put(block, total)
            self.p2_copy(g.z).start()

        when(self.by_z, along_z)
        unless(self.by_z, with_p2)

    def last(self):
        g = self.g

        def finish(by_z):
            total = self.own(g.block(g.z, g.i2, g.i3))
            for k in range(1, g.Z):
                self.z_copy(k, g.i2, by_z).wait_recv()
                slot = 1 + (k - 1) * 2 + g.i2 if by_z else g.Z + k - 1
                total += self.landed(self.rec, slot)
            self.p2_copy(g.z).wait_recv()
            total += self.landed(self.rec, 0 if by_z else g.z)
            self.write(total)

        when(self.by_z, lambda: finish(True))
        unless(self.by_z, lambda: finish(False))

    def sent(self):
        g = self.g
        for z in range(g.Z):
            for a2 in (0, 1):
                self.p3_copy(z, a2).wait_send()

        def by_z():
            self.p2_copy(g.z).wait_send()
            for k in range(1, g.Z):
                for a2 in (0, 1):
                    self.z_copy(k, a2, True).wait_send()

        def by_p2():
            for z in range(g.Z):
                self.p2_copy(z).wait_send()
            for k in range(1, g.Z):
                self.z_copy(k, g.i2, False).wait_send()

        when(self.by_z, by_z)
        unless(self.by_z, by_p2)


def loop(count):
    def run(body):
        def step(i, carry):
            body(i)
            return carry

        lax.fori_loop(0, count, step, 0)

    return run


def run_at(t, events):
    for i, event in events.items():
        pl.when(t == i)(event)


def dot(a, b):
    return jnp.dot(a, b, preferred_element_type=jnp.float32)


def dot_nt(a, b):
    return lax.dot_general(a, b, (((1,), (1,)), ((), ())), preferred_element_type=jnp.float32)


def normed(v):
    center = v - jnp.mean(v, axis=-1, keepdims=True)
    r = lax.rsqrt(jnp.mean(center * center, axis=-1, keepdims=True) + epsilon)
    return center * r, r


def norm_pull(v, gain, e):
    z, r = normed(v)
    f = e * gain
    dv = r * (
        f
        - jnp.mean(f, axis=-1, keepdims=True)
        - z * jnp.mean(f * z, axis=-1, keepdims=True)
    )
    return dv, e * z


def turn(u, cosine, sine, half):
    lane = lax.broadcasted_iota(jnp.int32, u.shape, 1)
    swapped = jnp.where(
        lax.rem(lane, 2 * half) < half,
        pltpu.roll(u, u.shape[1] - half, 1),
        pltpu.roll(u, half, 1),
    )
    return u * cosine + swapped * sine


def turn_tables(row_len, head_dim):
    half = head_dim // 2
    inverse = 10000.0 ** (-2.0 * np.arange(half) / head_dim)
    angles = np.arange(row_len)[:, None] * inverse[None, :]
    cosine = np.tile(np.cos(angles), (1, 4))
    sine = np.tile(np.concatenate([-np.sin(angles), np.sin(angles)], axis=1), (1, 2))
    return cosine.astype(np.float32), sine.astype(np.float32)


def doc_ends(lens):
    ends = [lens[0, 0]]
    for d in range(1, DOCS):
        ends.append(ends[-1] + lens[0, d])
    return ends


def fill_bias(bias, lens, first, rows):
    ends = doc_ends(lens)
    block = 128
    blocks = bias.shape[1] // block

    @loop(bias.shape[0] * blocks)
    def _(i):
        shape = (block, rows)
        place = first + lax.broadcasted_iota(jnp.int32, shape, 1)
        key = i * block + lax.broadcasted_iota(jnp.int32, shape, 0)
        start = jnp.zeros(shape, jnp.int32)
        for d in range(DOCS):
            start = jnp.where(place >= ends[d], ends[d], start)
        fine = (key >= start) & (key <= place)
        spot = pl.ds(lax.rem(i, blocks) * block, block)
        bias[lax.div(i, blocks), spot, :] = jnp.where(fine, 0.0, masked_score)


def split_heads(v, axis=1):
    spot = lax.broadcasted_iota(jnp.int32, v.shape, axis)
    first = spot < v.shape[axis] // 2
    zero = jnp.zeros_like(v)
    return jnp.where(first, v, zero), jnp.where(first, zero, v)


class Tiles:
    def __init__(self, source, buffer, sems, ready=None):
        self.source, self.buffer, self.sems, self.ready = source, buffer, sems, ready
        self.depth = buffer.shape[0]

    def copy(self, t):
        slot = lax.rem(t, self.depth)
        return pltpu.make_async_copy(self.source(t), self.buffer.at[slot], self.sems.at[slot])

    def start(self, t):
        if self.ready is not None:
            self.ready(t)
        self.copy(t).start()

    def first(self, end, begin=0):
        for t in range(begin, min(begin + self.depth - 1, end)):
            self.start(jnp.int32(t))

    def get(self, t, end):
        later = t + self.depth - 1

        @pl.when(later < end)
        def _():
            self.start(later)

        self.copy(t).wait()
        return self.buffer[lax.rem(t, self.depth)]


def columns(t, size):
    return pl.ds(pl.multiple_of(t * size, size), size)


def forward_kernel(dp_size, head_dim, *refs):
    (tok, lens, gs, wq, wo, wu, wd, cosine, sine) = refs[:9]
    (out, wq_f, wo_f, wu_f, wd_f, gain_o, q_o, k_o, v_o, ob_o, lse_o) = refs[9:20]
    (araw_o, h_o, mraw_o, bt_o, gt_o, gp_o, at_o, atx_o) = refs[20:28]
    (g_full, gain, tokx, a, ax, at, atx, q, k, v, vt, bias, ob, lse) = refs[28:42]
    (araw, h, mraw, b, bt, act, actt, gp, wbuf, dbuf) = refs[42:52]
    sems = refs[52:62]
    wsem, dsem, xsem, osem = refs[62:66]
    g = Place(dp_size)
    y = g.y
    rows, width = tok.shape
    half = head_dim // 2
    pairs = width // 128
    scale = head_dim ** (-0.5)
    on_core = g.c == 0
    gg, gq, go, gu, gd = [
        Gather(g, s, f, sems[2 * i], sems[2 * i + 1], mode)
        for i, (s, f, mode) in enumerate(
            (
                (gs, g_full, False),
                (wq, wq_f, MODES[0] and on_core),
                (wo, wo_f, MODES[1] and on_core),
                (wu, wu_f, MODES[2] and on_core),
                (wd, wd_f, MODES[3] and on_core),
            )
        )
    ]
    Z = g.Z
    saves = []

    def save(src, dst):
        copy = pltpu.make_async_copy(src, dst, osem.at[len(saves)])
        copy.start()
        saves.append(copy)

    tok_copy = pltpu.make_async_remote_copy(
        src_ref=tok,
        dst_ref=tokx,
        send_sem=xsem.at[0],
        recv_sem=xsem.at[1],
        device_id=g.device(g.z, g.x, g.c, 1 - y),
        device_id_type=MESH,
    )
    g.barrier()
    gg.start()
    gq.start()
    go.start()
    gu.start()
    fill_bias(bias, lens, y * rows, rows)
    gg.first_p2()
    gg.all_z()
    gg.all_p2()
    gg.all_p3()
    gq.first_p2()
    gq.all_z()
    gg.complete()
    turned = jnp.transpose(g_full[...].astype(jnp.float32))
    gain[...] = turned[:8]
    save(gain, gain_o)

    def first_norm(src, dst, dst_t):
        @loop(rows // 128)
        def _(i):
            spot = pl.ds(i * 128, 128)
            z, _r = normed(src[spot, :].astype(jnp.float32))
            value = z * gain[0:1, :]
            dst[spot, :] = value.astype(jnp.bfloat16)
            dst_t[:, spot] = jnp.transpose(value).astype(jnp.bfloat16)

    gq.all_p2()

    @pl.when(y == 0)
    def _():
        tok_copy.start()

    gd.start()
    first_norm(tok, a, at)
    save(at, at_o)
    go.first_p2()
    go.all_z()
    gq.all_p3()
    go.all_p2()
    gq.complete()

    tiles = Tiles(lambda t: wq_f.at[:, columns(t, 512)], wbuf, wsem)
    per = width // 512
    first = pl.multiple_of(y * rows, rows)

    def turned_pair(u, start):
        return turn(u, cosine[pl.ds(start, rows), :], sine[pl.ds(start, rows), :], half)

    tiles.first(3 * per)

    @loop(per)
    def _(t):
        u = dot(a[...], tiles.get(t, 3 * per))
        for j in range(4):
            part = turned_pair(u[:, j * 128 : j * 128 + 128], first) * scale
            q[4 * t + j] = part.astype(jnp.bfloat16)

    gu.first_p2()
    go.all_p3()

    def keys(w, t, src, start):
        u = dot(src[...], w)
        for j in range(4):
            part = turned_pair(u[:, j * 128 : j * 128 + 128], start)
            k[4 * t + j, pl.ds(start, rows), :] = part.astype(jnp.bfloat16)

    def values(w, t, src, start):
        u = dot(src[...], w)
        ut = jnp.transpose(u).astype(jnp.bfloat16)
        for j in range(4):
            cols = slice(j * 128, j * 128 + 128)
            v[4 * t + j, pl.ds(start, rows), :] = u[:, cols].astype(jnp.bfloat16)
            vt[4 * t + j, :, pl.ds(start, rows)] = ut[cols]

    @loop(per)
    def _(t):
        keys(tiles.get(t + per, 3 * per), t, a, first)

    @loop(per)
    def _(t):
        values(tiles.get(t + 2 * per, 3 * per), t, a, first)

    gu.all_z()
    gd.first_p2()

    @pl.when(y == 1)
    def _():
        tok_copy.wait_recv()
        first_norm(tokx, ax, atx)
        tiles.first(3 * per, per)

        @loop(per)
        def _(t):
            keys(tiles.get(t + per, 3 * per), t, ax, 0)

        @loop(per)
        def _(t):
            values(tiles.get(t + 2 * per, 3 * per), t, ax, 0)

    save(atx, atx_o)
    save(q, q_o)
    save(k, k_o)
    save(v, v_o)

    def attend(p, block, count):
        spot = slice(block * 256, block * 256 + 256)
        heads = split_heads(q[p, spot, :])
        kk = k[p, :count, :]
        vv = vt[p, :, :count]
        parts = []
        for i in (0, 1):
            s = dot_nt(kk, heads[i]) + bias[0, :count, spot]
            m = jnp.max(s, axis=0, keepdims=True)
            e = jnp.exp(s - m)
            total = jnp.sum(e, axis=0, keepdims=True)
            lse[p, i : i + 1, spot] = m + jnp.log(total)
            parts.append(dot(vv, e.astype(jnp.bfloat16)) * (1.0 / total))
        upper = lax.broadcasted_iota(jnp.int32, parts[0].shape, 0) < head_dim
        ob[p, :, spot] = jnp.where(upper, parts[0], parts[1]).astype(jnp.bfloat16)

    events = {
        0: lambda: gu.all_p2(),
        2: lambda: gd.all_z(),
        4: lambda: gu.all_p3(),
        6: lambda: gd.all_p2(),
    }
    blocks = rows // 256

    @loop(pairs)
    def _(p):
        for half_row in (0, 1):

            @pl.when(y == half_row)
            def _():
                for block in range(blocks):
                    attend(p, block, (half_row * blocks + block + 1) * 256)

        run_at(p, events)

    save(ob, ob_o)
    save(lse, lse_o)

    go.complete()
    tiles = Tiles(lambda t: wo_f.at[:, columns(t, 512)], wbuf, wsem)
    tiles.first(per)
    a[...] = jnp.transpose(ob[...].reshape(width, rows))

    @loop(per)
    def _(t):
        w = tiles.get(t, per)
        araw[:, columns(t, 512)] = dot(a[...], w)

    save(araw, araw_o)

    @loop(rows // 128)
    def _(i):
        spot = pl.ds(i * 128, 128)
        z, _r = normed(araw[spot, :])
        hidden = tok[spot, :].astype(jnp.float32) + z * gain[1:2, :]
        h[spot, :] = hidden
        z, _r = normed(hidden)
        value = z * gain[2:3, :]
        b[spot, :] = value.astype(jnp.bfloat16)
        bt[:, spot] = jnp.transpose(value).astype(jnp.bfloat16)

    save(h, h_o)
    save(bt, bt_o)

    gu.complete()
    tiles = Tiles(lambda t: wu_f.at[:, columns(t, 512)], wbuf, wsem)
    ups = act.shape[0]
    tiles.first(ups)
    c0 = math.sqrt(2.0 / math.pi)

    @loop(ups)
    def _(t):
        u = dot(b[...], tiles.get(t, ups))
        square = u * u
        th = jnp.tanh(c0 * (u + 0.044715 * (square * u)))
        value = 0.5 * u * (1.0 + th)
        slope = 0.5 * (1.0 + th) + (0.5 * c0) * u * (1.0 - th * th) * (
            1.0 + (3 * 0.044715) * square
        )
        act[t] = value.astype(jnp.bfloat16)
        actt[t] = jnp.transpose(value).astype(jnp.bfloat16).reshape(2, 256, rows)
        gp[t] = slope.astype(jnp.bfloat16)

    save(actt, gt_o)
    save(gp, gp_o)

    gd.all_p3()
    gd.complete()
    tiles = Tiles(lambda t: wd_f.at[columns(t, 512), :], dbuf, dsem)
    tiles.first(ups)
    mraw[...] = jnp.zeros_like(mraw)

    @loop(ups)
    def _(t):
        mraw[...] += dot(act[t], tiles.get(t, ups))

    save(mraw, mraw_o)
    ends = doc_ends(lens)

    @loop(rows // 128)
    def _(i):
        spot = pl.ds(i * 128, 128)
        z, _r = normed(mraw[spot, :])
        result = h[spot, :] + z * gain[3:4, :]
        place = y * rows + i * 128 + lax.broadcasted_iota(jnp.int32, result.shape, 0)
        result = jnp.where(place < ends[DOCS - 2], result, 0.0)
        out[spot, :] = result.astype(jnp.bfloat16)

    for copy in saves:
        copy.wait()

    @pl.when(y == 0)
    def _():
        tok_copy.wait_send()

    for m in (gg, gq, go, gu, gd):
        m.sent()


def forward(tokens, lengths, gains_wide, w_qkv, w_out, w_up, w_down, tables):
    dp_size = lax.axis_size("dp")
    devices = dp_size * lax.axis_size("ctx")
    rows, width = tokens.shape
    row_len = rows * lax.axis_size("ctx")
    head_dim = width // HEADS
    pairs = width // 128
    ups = w_up.shape[1] // 512
    bf, f32 = jnp.bfloat16, jnp.float32
    any_spec = pl.BlockSpec(memory_space=pl.ANY)
    vm = pl.BlockSpec(memory_space=pltpu.VMEM)
    shape = jax.ShapeDtypeStruct

    def whole(w):
        return shape((w.shape[0] * devices, w.shape[1]), bf)

    outs = [
        shape((rows, width), bf),
        whole(w_qkv),
        whole(w_out),
        whole(w_up),
        whole(w_down),
        shape((8, width), f32),
        shape((pairs, rows, 128), bf),
        shape((pairs, row_len, 128), bf),
        shape((pairs, row_len, 128), bf),
        shape((pairs, 128, rows), bf),
        shape((pairs, 2, rows), f32),
        shape((rows, width), f32),
        shape((rows, width), f32),
        shape((rows, width), f32),
        shape((width, rows), bf),
        shape((ups, 2, 256, rows), bf),
        shape((ups, rows, 512), bf),
        shape((width, rows), bf),
        shape((width, rows), bf),
    ]
    scratch = [
        pltpu.VMEM((width, 128), bf),
        pltpu.VMEM((8, width), f32),
        pltpu.VMEM((rows, width), bf),
        pltpu.VMEM((rows, width), bf),
        pltpu.VMEM((rows, width), bf),
        pltpu.VMEM((width, rows), bf),
        pltpu.VMEM((width, rows), bf),
        pltpu.VMEM((pairs, rows, 128), bf),
        pltpu.VMEM((pairs, row_len, 128), bf),
        pltpu.VMEM((pairs, row_len, 128), bf),
        pltpu.VMEM((pairs, 128, row_len), bf),
        pltpu.VMEM((1, row_len, rows), f32),
        pltpu.VMEM((pairs, 128, rows), bf),
        pltpu.VMEM((pairs, 2, rows), f32),
        pltpu.VMEM((rows, width), f32),
        pltpu.VMEM((rows, width), f32),
        pltpu.VMEM((rows, width), f32),
        pltpu.VMEM((rows, width), bf),
        pltpu.VMEM((width, rows), bf),
        pltpu.VMEM((ups, rows, 512), bf),
        pltpu.VMEM((ups, 2, 256, rows), bf),
        pltpu.VMEM((ups, rows, 512), bf),
        pltpu.VMEM((3, width, 512), bf),
        pltpu.VMEM((3, 512, width), bf),
    ]
    scratch += [pltpu.SemaphoreType.DMA((Gather.sems(dp_size // 4),))] * 10
    scratch += [pltpu.SemaphoreType.DMA((3,))] * 3 + [pltpu.SemaphoreType.DMA((16,))]
    return pl.pallas_call(
        functools.partial(forward_kernel, dp_size, head_dim),
        out_shape=outs,
        in_specs=[vm, pl.BlockSpec(memory_space=pltpu.SMEM), vm]
        + [any_spec] * 4
        + [vm, vm],
        out_specs=[vm] + [any_spec] * (len(outs) - 1),
        scratch_shapes=scratch,
        compiler_params=pltpu.CompilerParams(
            collective_id=0, has_side_effects=True, vmem_limit_bytes=60 * 2**20
        ),
    )(tokens, lengths, gains_wide, w_qkv, w_out, w_up, w_down, *tables)


def backward_kernel(dp_size, head_dim, *refs):
    (tok, dout, lens, gain, cosine, sine, wq, wo, wu, wd) = refs[:10]
    (q_i, k_i, v_i, ob_i, lse_i, araw_i, h_i, mraw_i, bt_i, gt_i, gp_i, at_i, atx_i) = refs[10:23]
    (dtok, out_q, out_o, out_u, out_d, out_g) = refs[23:29]
    (gts, dus, dzs) = refs[29:32]
    (part, rec3, rec, gpart, grec3, grec) = refs[32:38]
    (f1, f2, acc, dm, dms, da, das, dz, bt, bts, obts, ats, atx, atxs) = refs[38:52]
    (q, ob, lse, dk, dv, dg, dgs, dgt, dnxs) = refs[52:61]
    (kbuf, vbuf, wbuf, dbuf, gbuf, gsbuf, gpbuf, sbuf) = refs[61:69]
    tsems = refs[69:79]
    usend, urecv, gsend, grecv, zsend, zrecv, osend, orecv, lsem = refs[79:88]
    dnsem = refs[88]
    gsems, rsems = refs[89:95], refs[95:101]
    at, xbuf, do, dnx = bt, gpbuf, dm, da
    g = Place(dp_size)
    Z, y, c = g.Z, g.y, g.c
    rows, width = tok.shape
    half = head_dim // 2
    pairs = width // 128
    scale = head_dim ** (-0.5)
    ups = gp_i.shape[0]
    per = width // 512
    bf, f32 = jnp.bfloat16, jnp.float32
    first = pl.multiple_of(y * rows, rows)

    def to_sib(src, dst, send, recv):
        return pltpu.make_async_remote_copy(
            src_ref=src,
            dst_ref=dst,
            send_sem=send,
            recv_sem=recv,
            device_id=g.sib,
            device_id_type=MESH,
        )

    def load(src, dst, i):
        return pltpu.make_async_copy(src, dst, lsem.at[i])

    h_load = load(h_i, f2, 0)
    bt_load = load(bt_i.at[:, c], bt, 1)
    atx_load = load(atx_i.at[:, c], atx, 2)
    q_load = load(q_i, q, 3)
    ob_load = load(ob_i, ob, 4)
    lse_load = load(lse_i, lse, 5)
    at_load = load(at_i.at[:, c], at, 6)

    def gt_send(i):
        return to_sib(gt_i.at[i, 1 - c], gts.at[i], gsend.at[i], grecv.at[i])

    bt_send = to_sib(bt_i.at[:, 1 - c], bts, osend.at[0], orecv.at[0])
    ob_send = to_sib(ob_i.at[:, 1 - c], obts, osend.at[1], orecv.at[1])
    at_send = to_sib(at_i.at[:, 1 - c], ats, osend.at[2], orecv.at[2])
    atx_send = to_sib(atx_i.at[:, 1 - c], atxs, osend.at[3], orecv.at[3])
    dm_send = to_sib(dm, dms, osend.at[4], orecv.at[4])
    da_send = to_sib(da, das, osend.at[5], orecv.at[5])
    dg_send = to_sib(dg, dgs, osend.at[6], orecv.at[6])
    dnx_send = pltpu.make_async_remote_copy(
        src_ref=dnx,
        dst_ref=dnxs,
        send_sem=dnsem.at[0],
        recv_sem=dnsem.at[1],
        device_id=g.device(g.z, g.x, c, 1 - y),
        device_id_type=MESH,
    )

    def du_send(t):
        return to_sib(dz.at[t], dus.at[t], usend.at[t], urecv.at[t])

    def dz_send(t):
        return to_sib(dz.at[t], dzs.at[t], zsend.at[t], zrecv.at[t])

    landing = (rec3, rec)

    def write_d(total):
        out_d[...] = total.reshape(out_d.shape)

    def write_into(out, column):
        def write(total):
            for i in range(total.shape[0]):
                out[:, column + i * width : column + (i + 1) * width] = total[i]

        return write

    def write_g(total):
        out_g[...] = total[0]

    on_core = c == 0
    s_d = Share(
        g, part, 0, landing, 0, 4, gsems[0], rsems[0], write_d, MODES[3] and on_core
    )
    s_u = [
        Share(
            g, part, 4 + 2 * i, landing, 4 + 2 * i, 2, gsems[1 + i], rsems[1 + i],
            write_into(out_u, 2 * i * width), MODES[2] and on_core,
        )
        for i in (0, 1)
    ]
    s_o = Share(
        g, part, 8, landing, 8, 1, gsems[3], rsems[3], write_into(out_o, 0),
        MODES[1] and on_core,
    )
    s_q = Share(
        g, part, 0, landing, 9, 3, gsems[4], rsems[4], write_into(out_q, 0),
        MODES[0] and on_core,
    )
    s_g = Share(g, gpart, 0, (grec3, grec), 0, 1, gsems[5], rsems[5], write_g, False)

    mraws = Tiles(lambda i: mraw_i.at[columns(i, 128), :], f1, tsems[9])
    araws = Tiles(lambda i: araw_i.at[columns(i, 128), :], f1, tsems[9])
    mraws.first(rows // 128)
    g.barrier()
    for k in range(1, Z + 1):
        for i in (0, 1):
            gt_send(g.above(k) * 2 + i).start()
    for copy in (bt_send, ob_send, at_send):
        copy.start()

    @pl.when(y == 1)
    def _():
        atx_send.start()

    def gt_ready(j):
        for i in (0, 1):
            gt_send(g.above(j + 1) * 2 + i).wait_recv()

    own_g = Tiles(lambda j: gt_i.at[pl.ds(g.above(j + 1) * 2, 2), c], gbuf, tsems[0])
    sib_g = Tiles(lambda j: gts.at[pl.ds(g.above(j + 1) * 2, 2)], gsbuf, tsems[1], gt_ready)
    own_g.first(Z)
    for copy in (h_load, bt_load, atx_load, q_load, ob_load, lse_load):
        copy.start()
    dg[...] = jnp.zeros_like(dg)
    ends = doc_ends(lens)

    def upstream(i):
        e = dout[pl.ds(i * 128, 128), :].astype(f32)
        place = y * rows + i * 128 + lax.broadcasted_iota(jnp.int32, e.shape, 0)
        return jnp.where(place < ends[DOCS - 2], e, 0.0)

    def gain_sum(index, term):
        dg[index : index + 1, :] += jnp.sum(term, axis=0, keepdims=True)

    @loop(rows // 128)
    def _(i):
        value, term = norm_pull(mraws.get(i, rows // 128), gain[3:4, :], upstream(i))
        dm[pl.ds(i * 128, 128), :] = value.astype(bf)
        gain_sum(3, term)

    dm_send.start()
    downs = Tiles(lambda t: wd.at[columns(t, 512), :], dbuf, tsems[2])
    upw = Tiles(lambda t: wu.at[:, columns(t, 512)], wbuf, tsems[3])
    slopes = Tiles(lambda t: gp_i.at[t], gpbuf, tsems[4])
    for tiles in (downs, upw, slopes):
        tiles.first(ups)
    sib_g.first(Z)
    dm_send.wait_recv()

    @loop(Z)
    def _(j):
        z = g.above(j + 1)
        total = dot(own_g.get(j, Z).reshape(512, rows), dm[...])
        total += dot(sib_g.get(j, Z).reshape(512, rows), dms[...])
        total = total.astype(bf).reshape(4, 4, 32, width)
        for a in range(4):
            for e in range(4):
                part[e, 4 * z + a] = total[a, e]
        s_d.start(z)

    def add_to(halves, value, weights):
        for j in (0, 1):
            halves[j] += dot_nt(value, weights[j * 512 : (j + 1) * 512])

    acc[...] = jnp.zeros_like(acc)

    @loop(ups)
    def _(t):
        du = dot_nt(dm[...], downs.get(t, ups)) * slopes.get(t, ups).astype(f32)
        du = du.astype(bf)
        dz[t] = du
        du_send(t).start()
        add_to(acc, du, upw.get(t, ups))
        run_at(t, {3: lambda: s_d.stage3(1), 7: lambda: s_d.stage3(2)})

    outs = Tiles(lambda t: wo.at[columns(t, 512), :], dbuf, tsems[2])
    outs.first(per)
    bt_load.wait()
    bt_send.wait_recv()
    sib_du = Tiles(lambda t: dus.at[t], sbuf, tsems[5], lambda t: du_send(t).wait_recv())
    sib_du.first(ups)
    for i in (0, 1):

        @loop(ups // 2)
        def _(t2):
            t = t2 + i * (ups // 2)
            total = dot(bt[...].reshape(-1, rows), dz[t])
            total += dot(bts[...].reshape(-1, rows), sib_du.get(t, ups))
            part[4 + lax.div(t, per), :, :, columns(lax.rem(t, per), 512)] = (
                total.astype(bf).reshape(4 * Z, 32, 512)
            )

        s_u[i].start_all()
        s_d.stage3(3 if i == 0 else 0)

    at_load.start()

    araws.first(rows // 128)
    h_load.wait()

    @loop(rows // 128)
    def _(i):
        spot = pl.ds(i * 128, 128)
        e = jnp.concatenate([acc[0, spot, :], acc[1, spot, :]], axis=1)
        value, term = norm_pull(f2[spot, :], gain[2:3, :], e)
        gain_sum(2, term)
        dh = upstream(i) + value
        f2[spot, :] = dh
        value, term = norm_pull(araws.get(i, rows // 128), gain[1:2, :], dh)
        gain_sum(1, term)
        da[spot, :] = value.astype(bf)

    da_send.start()
    dm_send.wait_send()
    s_d.stage2()

    @loop(per)
    def _(t):
        do[:, columns(t, 512)] = dot_nt(da[...], outs.get(t, per)).astype(bf)

    ob_load.wait()
    ob_send.wait_recv()
    da_send.wait_recv()

    @loop(per)
    def _(t):
        total = dot(ob[:, c].reshape(-1, rows), da[:, columns(t, 512)])
        total += dot(obts[...].reshape(-1, rows), das[:, columns(t, 512)])
        part[8, :, :, columns(t, 512)] = total.astype(bf).reshape(4 * Z, 32, 512)

    s_o.start_all()
    for t in range(ups):
        du_send(t).wait_send()

    keys = Tiles(lambda p: k_i.at[p], kbuf, tsems[6])
    values = Tiles(lambda p: v_i.at[p], vbuf, tsems[7])
    keys.first(pairs)
    values.first(pairs)
    fill_bias(acc, lens, y * rows, rows)
    q_load.wait()
    lse_load.wait()
    blocks = rows // 256

    def bias(count, spot):
        if count <= 512:
            return acc[0, :count, spot]
        return jnp.concatenate([acc[0, :, spot], acc[1, : count - 512, spot]], axis=0)

    def attend(p, block, count, fresh, kk, vv, kt):
        spot = slice(block * 256, block * 256 + 256)
        qs = split_heads(q[p, spot, :])
        do_pair = do[spot, columns(p, 128)]
        dos = split_heads(do_pair)
        ob_pair = ob[p, :, :, spot].astype(f32).reshape(128, -1)
        dot_o = jnp.transpose(do_pair.astype(f32)) * ob_pair
        mask = bias(count, spot)
        parts, dk_, dv_ = [], [], []
        for i in (0, 1):
            delta = jnp.sum(
                dot_o[i * head_dim : (i + 1) * head_dim], axis=0, keepdims=True
            )
            s = dot_nt(kk, qs[i]) + mask
            prob = jnp.exp(s - lse[p, i : i + 1, spot])
            ds = (prob * (dot_nt(vv, dos[i]) - delta)).astype(bf)
            dv_.append(dot(prob.astype(bf), dos[i]))
            dk_.append(dot(ds, qs[i]))
            parts.append(dot(kt, ds))
        if fresh:
            dk[:count, :] = dk_[0] + dk_[1]
            dv[:count, :] = dv_[0] + dv_[1]
        else:
            dk[:count, :] += dk_[0] + dk_[1]
            dv[:count, :] += dv_[0] + dv_[1]
        upper = lax.broadcasted_iota(jnp.int32, parts[0].shape, 0) < head_dim
        dq = jnp.transpose(jnp.where(upper, parts[0], parts[1]) * scale)
        start = pl.multiple_of(first + block * 256, 256)
        dq = turn(dq, cosine[pl.ds(start, 256), :], -sine[pl.ds(start, 256), :], half)
        dz[lax.div(p, 4), spot, lanes(p)] = dq.astype(bf)

    def lanes(p):
        return columns(lax.rem(p, 4), 128)

    def keep(p, start, base):
        spot = pl.ds(start, rows)
        u = turn(dk[spot, :], cosine[spot, :], -sine[spot, :], half)
        dz[base + lax.div(p, 4), :, lanes(p)] = u.astype(bf)
        dz[base + per + lax.div(p, 4), :, lanes(p)] = dv[spot, :].astype(bf)

    events = {
        0: lambda: s_u[0].stage3(1, 2),
        1: lambda: s_u[0].stage3(3, 0),
        2: lambda: s_d.last(),
        3: lambda: s_u[0].stage2(),
        4: lambda: s_u[1].stage3(1, 2, 3, 0),
        5: lambda: s_o.stage3(1, 2, 3, 0),
        6: lambda: (s_u[1].stage2(), s_u[0].last())[1],
        7: lambda: s_o.stage2(),
    }

    @loop(pairs)
    def _(p):
        kk = keys.get(p, pairs)
        vv = values.get(p, pairs)
        kt = jnp.transpose(kk.astype(f32)).astype(bf)
        for half_row in (0, 1):

            @pl.when(y == half_row)
            def _():
                for block in reversed(range(blocks)):
                    count = (half_row * blocks + block + 1) * 256
                    attend(p, block, count, block == blocks - 1, kk[:count], vv[:count], kt[:, :count])

        keep(p, first, per)

        @pl.when(y == 1)
        def _():
            keep(p, 0, 3 * per)

        @pl.when(lax.rem(p, 4) == 3)
        def _():
            for e in range(3):
                dz_send(e * per + lax.div(p, 4)).start()

            @pl.when(y == 1)
            def _():
                for e in (3, 4):
                    dz_send(e * per + lax.div(p, 4)).start()

        run_at(p, events)

    qkv_w = Tiles(lambda t: wq.at[:, columns(t, 512)], wbuf, tsems[3])

    @pl.when(y == 1)
    def _():
        qkv_w.first(3 * per, per)
        acc[...] = jnp.zeros_like(acc)
        da_send.wait_send()

        @loop(2 * per)
        def _(t):
            add_to(acc, dz[t + 3 * per], qkv_w.get(t + per, 3 * per))

        dnx[:, :512] = acc[0].astype(bf)
        dnx[:, 512:] = acc[1].astype(bf)
        dnx_send.start()

    qkv_w.first(3 * per)
    s_d.sent()
    atx_load.wait()
    at_load.wait()
    at_send.wait_recv()

    @pl.when(y == 1)
    def _():
        atx_send.wait_recv()

    def dz_ready(t):
        dz_send(t).wait_recv()

    sib_dz = Tiles(lambda t: dzs.at[t], sbuf, tsems[5], dz_ready)
    sib_dx = Tiles(lambda t: dzs.at[t], xbuf, tsems[8], dz_ready)
    sib_dz.first(3 * per)

    @pl.when(y == 1)
    def _():
        sib_dx.first(5 * per, 3 * per)

    @loop(3 * per)
    def _(t):
        acc[0] = dot(at[...].reshape(-1, rows), dz[t]) + dot(
            ats[...].reshape(-1, rows), sib_dz.get(t, 3 * per)
        )

        @pl.when((y == 1) & (t >= per))
        def _():
            tx = t + 2 * per
            acc[0] += dot(atx[...].reshape(-1, rows), dz[tx]) + dot(
                atxs[...].reshape(-1, rows), sib_dx.get(tx, 5 * per)
            )

        part[lax.div(t, per), :, :, columns(lax.rem(t, per), 512)] = (
            acc[0].astype(bf).reshape(4 * Z, 32, 512)
        )

    s_q.start_all()
    s_u[1].last()
    s_o.last()

    acc[...] = jnp.zeros_like(acc)

    @loop(3 * per)
    def _(t):
        add_to(acc, dz[t], qkv_w.get(t, 3 * per))

    @pl.when(y == 0)
    def _():
        dnx_send.wait_recv()
        acc[0] += dnxs[:, :512].astype(f32)
        acc[1] += dnxs[:, 512:].astype(f32)

    @loop(rows // 128)
    def _(i):
        spot = pl.ds(i * 128, 128)
        e = jnp.concatenate([acc[0, spot, :], acc[1, spot, :]], axis=1)
        value, term = norm_pull(tok[spot, :].astype(f32), gain[0:1, :], e)
        gain_sum(0, term)
        dtok[spot, :] = (f2[spot, :] + value).astype(bf)

    dg_send.start()
    s_q.stage3(1)
    dg_send.wait_recv()
    wide = jnp.concatenate([dg[...] + dgs[...], jnp.zeros((120, width), f32)], axis=0)
    dgt[...] = jnp.transpose(wide).reshape(dgt.shape)
    gpart[0] = dgt[:, c].reshape(gpart.shape[1:])
    s_g.start_all()
    s_q.stage3(2, 3, 0)
    s_g.stage3(1, 2, 3, 0)
    s_q.stage2()
    s_g.stage2()
    s_q.last()
    s_g.last()

    for i in range(2 * Z):
        gt_send(i).wait_send()
    for copy in (bt_send, ob_send, at_send, dg_send):
        copy.wait_send()
    for t in range(3 * per):
        dz_send(t).wait_send()

    @pl.when(y == 0)
    def _():
        da_send.wait_send()

    @pl.when(y == 1)
    def _():
        atx_send.wait_send()
        dnx_send.wait_send()
        for t in range(3 * per, 5 * per):
            dz_send(t).wait_send()

    for s in (s_u[0], s_u[1], s_o, s_q, s_g):
        s.sent()


def backward(tokens, d_out, lengths, gain_rows, tables, weights, saved, shards):
    dp_size = lax.axis_size("dp")
    Z = dp_size // 4
    rows, width = tokens.shape
    row_len = rows * lax.axis_size("ctx")
    head_dim = width // HEADS
    pairs = width // 128
    per = width // 512
    bf, f32 = jnp.bfloat16, jnp.float32
    ups = saved[10].shape[0]
    any_spec = pl.BlockSpec(memory_space=pl.ANY)
    vm = pl.BlockSpec(memory_space=pltpu.VMEM)
    smem = pl.BlockSpec(memory_space=pltpu.SMEM)
    shape = jax.ShapeDtypeStruct
    block = 32
    saved = list(saved)
    for i in (3, 8, 11, 12):
        saved[i] = saved[i].reshape(2 * Z, 2, width // (4 * Z), rows)
    outs = [
        shape((rows, width), bf),
        shape(shards[0].shape, f32),
        shape(shards[1].shape, f32),
        shape(shards[2].shape, f32),
        shape(shards[3].shape, f32),
        shape((block, 128), f32),
        shape((2 * Z, 256, rows), bf),
        shape((ups, rows, 512), bf),
        shape((5 * per, rows, 512), bf),
    ]
    core_rows = (2 * Z, width // (4 * Z), rows)
    scratch = [
        pltpu.VMEM((9, 4 * Z, block, width), bf),
        pltpu.VMEM((12, 2 * Z, block, width), bf),
        pltpu.VMEM((12, 2 * Z - 1, block, width), bf),
        pltpu.VMEM((1, 4 * Z, block, 128), f32),
        pltpu.VMEM((1, 2 * Z, block, 128), f32),
        pltpu.VMEM((1, 2 * Z - 1, block, 128), f32),
        pltpu.VMEM((2, 128, width), f32),
        pltpu.VMEM((rows, width), f32),
        pltpu.VMEM((2, rows, 512), f32),
        pltpu.VMEM((rows, width), bf),
        pltpu.VMEM((rows, width), bf),
        pltpu.VMEM((rows, width), bf),
        pltpu.VMEM((rows, width), bf),
        pltpu.VMEM((max(ups, 5 * per), rows, 512), bf),
    ]
    scratch += [pltpu.VMEM(core_rows, bf)] * 6
    scratch += [
        pltpu.VMEM((pairs, rows, 128), bf),
        pltpu.VMEM((2 * Z, 2, width // (4 * Z), rows), bf),
        pltpu.VMEM((pairs, 2, rows), f32),
        pltpu.VMEM((row_len, 128), f32),
        pltpu.VMEM((row_len, 128), f32),
        pltpu.VMEM((8, width), f32),
        pltpu.VMEM((8, width), f32),
        pltpu.VMEM((2 * Z, 2, width // (4 * Z), 128), f32),
        pltpu.VMEM((rows, width), bf),
        pltpu.VMEM((2, row_len, 128), bf),
        pltpu.VMEM((2, row_len, 128), bf),
        pltpu.VMEM((2, width, 512), bf),
        pltpu.VMEM((2, 512, width), bf),
        pltpu.VMEM((2, 2, 256, rows), bf),
        pltpu.VMEM((2, 2, 256, rows), bf),
        pltpu.VMEM((2, rows, 512), bf),
        pltpu.VMEM((2, rows, 512), bf),
    ]
    dma = pltpu.SemaphoreType.DMA
    scratch += [dma((3,))] * 10
    scratch += [dma((ups,))] * 2 + [dma((2 * Z,))] * 2 + [dma((5 * per,))] * 2
    scratch += [dma((7,))] * 2 + [dma((7,)), dma((2,))]
    scratch += [dma((Share.sems(Z),))] * 12
    return pl.pallas_call(
        functools.partial(backward_kernel, dp_size, head_dim),
        out_shape=outs,
        in_specs=[vm, vm, smem, vm, vm, vm] + [any_spec] * 17,
        out_specs=[vm] * 6 + [any_spec] * 3,
        scratch_shapes=scratch,
        compiler_params=pltpu.CompilerParams(
            collective_id=1, has_side_effects=True, vmem_limit_bytes=63 * 2**20
        ),
    )(tokens, d_out, lengths, gain_rows, *tables, *weights, *saved)


def layer_norm(values, gain_vec):
    center = values - jnp.mean(values, axis=-1, keepdims=True)
    spread = jnp.mean(center * center, axis=-1, keepdims=True)
    return center * lax.rsqrt(spread + epsilon) * gain_vec


def norm_back(values, gain_vec, upstream):
    unused, pullback = jax.vjp(layer_norm, values, gain_vec)
    return pullback(upstream)


def rotate(values, cosine_table, sine_table, direction):
    half_dim = values.shape[-1] // 2
    first_half = values[..., :half_dim]
    second_half = values[..., half_dim:]
    return jnp.concatenate(
        [
            first_half * cosine_table - direction * second_half * sine_table,
            second_half * cosine_table + direction * first_half * sine_table,
        ],
        axis=-1,
    )


def doc_layout(lengths, row_len):
    doc_ends = jnp.cumsum(lengths, axis=-1)
    places = jnp.arange(row_len, dtype=jnp.int32)
    passed = places[None, :, None] >= doc_ends[:, None, :]
    segment = jnp.sum(passed.astype(jnp.int32), axis=-1)
    starts = jnp.sum(jnp.where(passed, lengths[:, None, :], 0), axis=-1)
    position = places[None, :] - starts
    is_valid = places[None, :] < doc_ends[:, DOCS - 2][:, None]
    return (segment[0], position[0], is_valid[0])


def allowed_keys(own_seg, own_place, seg_full, first_key, block_rows):
    key_place = first_key + jnp.arange(block_rows, dtype=jnp.int32)
    key_seg = lax.dynamic_slice_in_dim(seg_full, first_key, block_rows)
    return (own_seg[:, None] == key_seg[None, :]) & (key_place[None, :] <= own_place[:, None])


def make_fold(queries, own_seg, own_place, seg_full, score_scale):

    def fold_piece(fold_state, piece, start):
        key_piece, value_piece = piece
        piece_rows = key_piece.shape[0]
        block_rows = math.gcd(piece_rows, 256)
        block_count = piece_rows // block_rows
        key_blocks = key_piece.reshape((block_count, block_rows) + key_piece.shape[1:])
        value_blocks = value_piece.reshape((block_count, block_rows) + value_piece.shape[1:])

        def step_block(carried, block_items):
            row_max, row_sum, weighted = carried
            key_block, value_block, block_id = block_items
            allowed = allowed_keys(own_seg, own_place, seg_full, block_id * block_rows, block_rows)
            scores = (
                jnp.einsum("qhd,khd->hqk", queries, key_block, preferred_element_type=jnp.float32)
                * score_scale
            )
            scores = jnp.where(allowed[None], scores, masked_score)
            new_max = jnp.maximum(row_max, jnp.max(scores, axis=-1))
            factor = jnp.exp(row_max - new_max)
            shifted = jnp.where(allowed[None], jnp.exp(scores - new_max[..., None]), 0.0)
            row_sum = row_sum * factor + jnp.sum(shifted, axis=-1)
            weighted = weighted * factor[..., None] + jnp.einsum(
                "hqk,khd->hqd",
                shifted.astype(jnp.bfloat16),
                value_block,
                preferred_element_type=jnp.float32,
            )
            return ((new_max, row_sum, weighted), None)

        block_ids = jnp.arange(block_count, dtype=jnp.int32)
        fold_state, unused = lax.scan(step_block, fold_state, (key_blocks, value_blocks, block_ids))
        return fold_state

    return fold_piece


def per_device(tokens, lengths, w_qkv, w_out, w_up, w_down, gains, d_out):
    tok_rows, model_width = tokens.shape
    row_len = tok_rows * lax.axis_size("ctx")
    head_count = HEADS
    head_dim = model_width // head_count
    score_scale = head_dim ** (-0.5)
    head_shape = (tok_rows, head_count, head_dim)
    seg_full, pos_full, valid_full = doc_layout(lengths, row_len)
    offset = lax.axis_index("ctx") * tok_rows
    own_seg = lax.dynamic_slice_in_dim(seg_full, offset, tok_rows)
    own_pos = lax.dynamic_slice_in_dim(pos_full, offset, tok_rows)
    own_valid = lax.dynamic_slice_in_dim(valid_full.astype(jnp.float32), offset, tok_rows)
    own_place = offset + jnp.arange(tok_rows, dtype=jnp.int32)
    freq_index = jnp.arange(head_dim // 2, dtype=jnp.float32)
    angles = own_pos.astype(jnp.float32)[:, None] * 10000.0 ** (-2.0 * freq_index / head_dim)
    cosine_table = jnp.cos(angles)[:, None, :]
    sine_table = jnp.sin(angles)[:, None, :]
    qkv_full, out_full, up_full, down_full, gain_full = (
        lax.all_gather(w_qkv, ("dp", "ctx"), axis=0, tiled=True),
        lax.all_gather(w_out, ("dp", "ctx"), axis=0, tiled=True),
        lax.all_gather(w_up, ("dp", "ctx"), axis=0, tiled=True),
        lax.all_gather(w_down, ("dp", "ctx"), axis=0, tiled=True),
        lax.all_gather(gains, ("dp", "ctx"), axis=0, tiled=True),
    )
    gain_f = gain_full.astype(jnp.float32)
    stream = tokens.astype(jnp.float32)
    normed = layer_norm(stream, gain_f[:, 0]).astype(jnp.bfloat16)
    qkv_raw = jnp.dot(normed, qkv_full, preferred_element_type=jnp.float32)
    queries = rotate(
        qkv_raw[:, :model_width].reshape(head_shape), cosine_table, sine_table, 1.0
    ).astype(jnp.bfloat16)
    key_heads = rotate(
        qkv_raw[:, model_width : 2 * model_width].reshape(head_shape), cosine_table, sine_table, 1.0
    ).astype(jnp.bfloat16)
    value_heads = qkv_raw[:, 2 * model_width :].reshape(head_shape).astype(jnp.bfloat16)
    start_state = (
        jnp.full((head_count, tok_rows), masked_score, jnp.float32),
        jnp.zeros((head_count, tok_rows), jnp.float32),
        jnp.zeros((head_count, tok_rows, head_dim), jnp.float32),
    )
    fold_piece = make_fold(queries, own_seg, own_place, seg_full, score_scale)
    row_max, row_sum, weighted = fold_piece(
        start_state,
        (
            lax.all_gather(key_heads, "ctx", axis=0, tiled=True),
            lax.all_gather(value_heads, "ctx", axis=0, tiled=True),
        ),
        jnp.int32(0),
    )
    attended = jnp.transpose(weighted / row_sum[..., None], (1, 0, 2))
    attended_b = attended.reshape(tok_rows, model_width).astype(jnp.bfloat16)
    attn_raw = jnp.dot(attended_b, out_full, preferred_element_type=jnp.float32)
    hidden = stream + layer_norm(attn_raw, gain_f[:, 1])
    mlp_in = layer_norm(hidden, gain_f[:, 2]).astype(jnp.bfloat16)
    up_proj = jnp.dot(mlp_in, up_full, preferred_element_type=jnp.float32)
    activated = jax.nn.gelu(up_proj).astype(jnp.bfloat16)
    mlp_raw = jnp.dot(activated, down_full, preferred_element_type=jnp.float32)
    result = hidden + layer_norm(mlp_raw, gain_f[:, 3])
    output = (result * own_valid[:, None]).astype(jnp.bfloat16)
    qkv_back, out_back, up_back, down_back = (
        lax.all_gather(w_qkv, ("dp", "ctx"), axis=0, tiled=True),
        lax.all_gather(w_out, ("dp", "ctx"), axis=0, tiled=True),
        lax.all_gather(w_up, ("dp", "ctx"), axis=0, tiled=True),
        lax.all_gather(w_down, ("dp", "ctx"), axis=0, tiled=True),
    )
    upstream = d_out.astype(jnp.float32) * own_valid[:, None]
    d_mlp, d_gain_four = norm_back(mlp_raw, gain_f[:, 3], upstream)
    d_mlp_b = d_mlp.astype(jnp.bfloat16)
    grad_down = jnp.einsum("tf,td->fd", activated, d_mlp_b, preferred_element_type=jnp.float32)
    d_activated = jnp.einsum("td,fd->tf", d_mlp_b, down_back, preferred_element_type=jnp.float32)
    unused, gelu_pull = jax.vjp(jax.nn.gelu, up_proj)
    d_up_b = gelu_pull(d_activated)[0].astype(jnp.bfloat16)
    grad_up = jnp.einsum("td,tf->df", mlp_in, d_up_b, preferred_element_type=jnp.float32)
    d_mlp_in = jnp.einsum("tf,df->td", d_up_b, up_back, preferred_element_type=jnp.float32)
    d_hidden_part, d_gain_three = norm_back(hidden, gain_f[:, 2], d_mlp_in)
    d_hidden = upstream + d_hidden_part
    d_attn, d_gain_two = norm_back(attn_raw, gain_f[:, 1], d_hidden)
    d_attn_b = d_attn.astype(jnp.bfloat16)
    grad_out = jnp.einsum("td,te->de", attended_b, d_attn_b, preferred_element_type=jnp.float32)
    d_attended = (
        jnp.einsum("te,de->td", d_attn_b, out_back, preferred_element_type=jnp.float32)
        .astype(jnp.bfloat16)
        .reshape(head_shape)
    )
    row_dot = jnp.einsum("qhd,qhd->hq", d_attended.astype(jnp.float32), attended)
    key_all, value_all = (
        lax.all_gather(key_heads, "ctx", axis=0, tiled=True),
        lax.all_gather(value_heads, "ctx", axis=0, tiled=True),
    )
    block_rows = math.gcd(row_len, 256)
    block_count = row_len // block_rows
    key_blocks = key_all.reshape((block_count, block_rows) + key_all.shape[1:])
    value_blocks = value_all.reshape((block_count, block_rows) + value_all.shape[1:])

    def back_block(d_queries, block_items):
        key_block, value_block, block_id = block_items
        allowed = allowed_keys(own_seg, own_place, seg_full, block_id * block_rows, block_rows)
        scores = (
            jnp.einsum("qhd,khd->hqk", queries, key_block, preferred_element_type=jnp.float32)
            * score_scale
        )
        attn_prob = jnp.where(
            allowed[None], jnp.exp(scores - row_max[..., None]) / row_sum[..., None], 0.0
        )
        d_prob = jnp.einsum(
            "qhd,khd->hqk", d_attended, value_block, preferred_element_type=jnp.float32
        )
        d_scores = (attn_prob * (d_prob - row_dot[..., None])).astype(jnp.bfloat16)
        d_queries = (
            d_queries
            + jnp.einsum("hqk,khd->qhd", d_scores, key_block, preferred_element_type=jnp.float32)
            * score_scale
        )
        d_keys = (
            jnp.einsum("hqk,qhd->khd", d_scores, queries, preferred_element_type=jnp.float32)
            * score_scale
        )
        d_values = jnp.einsum(
            "hqk,qhd->khd",
            attn_prob.astype(jnp.bfloat16),
            d_attended,
            preferred_element_type=jnp.float32,
        )
        return (d_queries, (d_keys, d_values))

    block_ids = jnp.arange(block_count, dtype=jnp.int32)
    d_queries, (d_keys_all, d_values_all) = lax.scan(
        back_block, jnp.zeros(head_shape, jnp.float32), (key_blocks, value_blocks, block_ids)
    )
    kv_terms = jnp.concatenate(
        [d_keys_all.reshape(row_len, model_width), d_values_all.reshape(row_len, model_width)],
        axis=-1,
    )
    kv_grad = lax.psum_scatter(
        kv_terms.astype(jnp.bfloat16), "ctx", scatter_dimension=0, tiled=True
    ).astype(jnp.float32)
    d_keys = kv_grad[:, :model_width].reshape(head_shape)
    d_qkv = jnp.concatenate(
        [
            rotate(d_queries, cosine_table, sine_table, -1.0).reshape(tok_rows, model_width),
            rotate(d_keys, cosine_table, sine_table, -1.0).reshape(tok_rows, model_width),
            kv_grad[:, model_width:],
        ],
        axis=-1,
    ).astype(jnp.bfloat16)
    grad_qkv = jnp.einsum("td,te->de", normed, d_qkv, preferred_element_type=jnp.float32)
    d_normed = jnp.einsum("te,de->td", d_qkv, qkv_back, preferred_element_type=jnp.float32)
    d_stream_part, d_gain_one = norm_back(stream, gain_f[:, 0], d_normed)
    d_tokens = (d_hidden + d_stream_part).astype(jnp.bfloat16)
    grad_gains = jnp.stack([d_gain_one, d_gain_two, d_gain_three, d_gain_four], axis=-1)
    shard_qkv, shard_out, shard_up, shard_down, shard_gains = (
        lax.psum_scatter(grad_qkv, ("dp", "ctx"), scatter_dimension=0, tiled=True),
        lax.psum_scatter(grad_out, ("dp", "ctx"), scatter_dimension=0, tiled=True),
        lax.psum_scatter(grad_up, ("dp", "ctx"), scatter_dimension=0, tiled=True),
        lax.psum_scatter(grad_down, ("dp", "ctx"), scatter_dimension=0, tiled=True),
        lax.psum_scatter(grad_gains, ("dp", "ctx"), scatter_dimension=0, tiled=True),
    )
    return (output, d_tokens, shard_qkv, shard_out, shard_up, shard_down, shard_gains)


def fused_device(tokens, lengths, w_qkv, w_out, w_up, w_down, gains, d_out):
    rows, width = tokens.shape
    row_len = rows * lax.axis_size("ctx")
    gains_wide = jnp.pad(gains, ((0, 0), (0, 128 - gains.shape[1])))
    tables = tuple(jnp.asarray(v) for v in turn_tables(row_len, width // HEADS))
    output, wq, wo, wu, wd, gain_rows, *saved = forward(
        tokens, lengths, gains_wide, w_qkv, w_out, w_up, w_down, tables
    )
    d_tokens, grad_qkv, grad_out, grad_up, grad_down, grad_gains = backward(
        tokens,
        d_out,
        lengths,
        gain_rows,
        tables,
        (wq, wo, wu, wd),
        saved,
        (w_qkv, w_out, w_up, w_down),
    )[:6]
    return (
        output,
        d_tokens,
        grad_qkv,
        grad_out,
        grad_up,
        grad_down,
        grad_gains[:, : gains.shape[1]],
    )


def layer(mesh):
    if mesh.shape["dp"] == 16 and mesh.shape["ctx"] == 2:
        return fused_device
    return per_device


def solution(mesh):
    return jax.shard_map(
        layer(mesh),
        mesh=mesh,
        in_specs=(
            P(("dp", "ctx"), None),
            P("dp", None),
            P(("dp", "ctx"), None),
            P(("dp", "ctx"), None),
            P(("dp", "ctx"), None),
            P(("dp", "ctx"), None),
            P(("dp", "ctx"), None),
            P(("dp", "ctx"), None),
        ),
        out_specs=(
            P(("dp", "ctx"), None),
            P(("dp", "ctx"), None),
            P(("dp", "ctx"), None),
            P(("dp", "ctx"), None),
            P(("dp", "ctx"), None),
            P(("dp", "ctx"), None),
            P(("dp", "ctx"), None),
        ),
        check_vma=False,
    )
```

time: 394 us -> 355 us (0.901)
  Pallas kernels: 381 us -> 343 us
    pallas_call x1, Pallas kernels: 186 us -> 160 us  [forward(): pl.pallas_call(functools.partial(forward_kernel, dp_size, head_dim), out_...]
    pallas_call x1, Pallas kernels: 195 us -> 183 us  [backward(): pl.pallas_call(functools.partial(backward_kernel, dp_size, head_dim), out...]
where the time goes in v4:
time: 355 us; the launch traced here: 354 us
  Pallas kernels  343 us (97%)
  local copies, waits for them, and re-layouts  10.4 us (3%)
    pallas_call x1, Pallas kernels, backward(): pl.pallas_call(functools.partial(backward_kernel, dp_size, head_dim), out...  183 us
    pallas_call x1, Pallas kernels, forward(): pl.pallas_call(functools.partial(forward_kernel, dp_size, head_dim), out_...  160 us
    unnamed x16, local copies, waits for them, and re-layouts  9.78 us

profile of v4, /device:TPU:1, one launch (start us, length us, event | category | flops | bytes accessed | tf_op | source)
XLA Modules:
  0.0 354.1 jit_solution(9414412636657485399)
XLA Ops:
  0.6 0.8 copy.17
  1.4 0.6 pad.4.refs_2_
  2.0 159.9 %shard_map.153 = (bf16[512,1024]{1,0:T(8,128)(2,1)}, bf16[1024,3072]{1,0:T(8,128)(2,1)}, bf16[1024,1024]{1,0:T(8,128)(2,1)}, bf16[1024,4096]{1,0:T(8,128)(2,1)},...) custom-call(bf16[512,1024]{1,0:T(8,128)(2,1)} %refs_0_.3, ...), custom_call_target="tpu_custom_call" | custom-call | tf_op jit(solution)/shard_map/pallas_call | solution.py:832
  161.9 183.2 %shard_map.154 = (bf16[512,1024]{1,0:T(8,128)(2,1)}, f32[32,3072]{1,0:T(8,128)}, f32[32,1024]{1,0:T(8,128)}, f32[32,4096]{1,0:T(8,128)}, f32[128,1024]{1,0:T(8,1...) custom-call(bf16[512,1024]{1,0:T(8,128)(2,1)} %refs_0_.3, ...), custom_call_target="tpu_custom_call" | custom-call | tf_op jit(solution)/shard_map/pallas_call | solution.py:1368
  345.1 0.0 copy-start.2
  345.1 0.0 copy-start.3
  345.1 0.0 copy-start.1
  345.1 0.0 copy-start
  345.1 1.5 copy.18
  346.6 2.3 copy.25
  348.9 2.3 copy.26
  351.1 0.0 copy-done.2
  351.1 0.7 copy.27
  351.9 0.0 copy-done.3
  351.9 0.7 copy.28
  352.5 0.0 copy-done.1
  352.5 0.8 copy.29
  353.3 0.0 copy-done
  353.3 0.8 copy.30
Async XLA Ops:
  345.1 6.0 %copy-start.2 = (f32[32,3072]{1,0:T(8,128)S(1)}, f32[32,3072]{1,0:T(8,128)}, u32[]{:S(2)}) copy-start(f32[32,3072]{1,0:T(8,128)} %get-tuple-element.73) | copy-start | bytes 1179652
  345.1 6.8 %copy-start.3 = (f32[32,1024]{1,0:T(8,128)S(1)}, f32[32,1024]{1,0:T(8,128)}, u32[]{:S(2)}) copy-start(f32[32,1024]{1,0:T(8,128)} %get-tuple-element.74) | copy-start | bytes 393220
  345.1 7.4 %copy-start.1 = (f32[32,4096]{1,0:T(8,128)S(1)}, f32[32,4096]{1,0:T(8,128)}, u32[]{:S(2)}) copy-start(f32[32,4096]{1,0:T(8,128)} %get-tuple-element.75) | copy-start | bytes 1572868
  345.1 8.2 %copy-start = (f32[128,1024]{1,0:T(8,128)S(1)}, f32[128,1024]{1,0:T(8,128)}, u32[]{:S(2)}) copy-start(f32[128,1024]{1,0:T(8,128)} %get-tuple-element.76) | copy-start | bytes 1572868

commit v5 on v4

--- a/solution.py
+++ b/solution.py
@@ -11,7 +11,58 @@
 
 HEADS = 16
 DOCS = 7
-MODES = (False, False, False, False)
+
+GATHER_BY_Z = (False, None, None, True)
+SHARE_BY_Z = (None, True, False, None)
+
+GATHER_PLAN = {
+    "start": ("gsz", "gsp2", "gsp3", "gssib", "qsz", "qsp3",),
+    "norm": ("gF", "gZ0", "ussib", "dsp2", "qsp2", "gZ1", "usp2", "osp3", "qF", "osz", "osp2", "qZ0", "qZ1", "gZ2", "usp3", "gP0", "oF", "dssib", "qZ2", "gT0", "usz", "qP0", "qP2", "uF", "qT0", "qT1", "gP2", "qP1", "gP1", "qT3", "oZ2", "gT1", "oZ0", "qssib", "ossib", "uT0", "oP0", "gT3", "token", "gT2", "oZ1", "qT2",),
+    "qkv": ("uZ2", "uZ0",),
+    ("k", 1): ("oP2", "oP1",),
+    ("v", 0): ("dF",),
+    ("v", 1): ("oT1",),
+    ("pair", 5): ("dsz",),
+    ("pair", 6): ("uP0",),
+    "other": ("oT0",),
+    ("more", 0): ("uZ1", "uP2", "oT3",),
+    ("more", 1): ("uP1", "oT2",),
+    ("more", 3): ("dsp3",),
+    ("more", 4): ("uT1",),
+    ("more", 5): ("dP1",),
+    ("more", 6): ("dZ0",),
+    "out": ("uT2", "dP0", "dZ2",),
+    "up": ("uT3",),
+    ("up", 0): ("dZ1",),
+    ("up", 1): ("dP2",),
+    ("up", 2): ("dT1",),
+    ("up", 4): ("dT0",),
+    ("up", 6): ("dT2",),
+    ("up", 7): ("dT3",),
+}
+
+NEAR = ((1, 2, 3), (0, 2, 3), (1, 3, 0), (2, 1, 0))
+FAR = ((3, 2, 1), (3, 0, 2), (0, 1, 3), (0, 1, 2))
+
+SHARE_PLAN = {
+    ("du", 6): ("d31",),
+    ("up", 4): ("d30",),
+    ("up", 6): ("d21",),
+    "out": ("d32",),
+    ("more", 1): ("d20",),
+    ("more", 2): ("v30",),
+    ("more", 6): ("u31", "v20", "v31", "u32", "v32", "u30", "u21",),
+    ("more", 7): ("d22",),
+    "other": ("o30",),
+    ("pair", 1): ("o32",),
+    ("pair", 2): ("v22",),
+    ("pair", 3): ("v21", "u22",),
+    "half": ("u20",),
+    ("pair", 6): ("o31",),
+    "input": ("a30",),
+    "gains": ("a32", "a31", "a20", "o21", "a33", "b31",),
+    "end": ("a22", "a21", "b32", "b22", "b30", "d33", "o33", "b21", "b20", "o22", "dE", "g31", "u33", "o20", "oE", "aE", "b33", "g30", "g32", "g33", "g21", "dL", "uE", "v33", "oL", "aL", "bE", "g20", "g22", "uL", "vE", "bL", "gE", "vL", "gL",),
+}
 
 epsilon = 1e-05
 masked_score = -1e30
@@ -69,6 +120,25 @@
     def at_z(self, z):
         return self.device(z, self.x, self.c, self.y)
 
+    def near(self, j):
+        if self.Z != 4:
+            return self.below(j + 1)
+        return sum(jnp.where(self.z == z, row[j], 0) for z, row in enumerate(NEAR))
+
+    def order(self, j):
+        if j == self.Z - 1:
+            return self.z
+        if self.Z != 4:
+            return self.above(j + 1)
+        return sum(jnp.where(self.z == z, row[j], 0) for z, row in enumerate(FAR))
+
+    def far(self, z):
+        return jnp.abs(z - self.z) == self.Z - 1
+
+    def between(self, z):
+        last = self.Z - 1
+        return ((z == 0) & (self.z == last - 1)) | ((z == last) & (self.z == 1))
+
     def block(self, z, a2, a3):
         c = self.c
         return (z * 2 + a3 * (1 - c) + a2 * c) * 2 + a2 * (1 - c) + a3 * c
@@ -98,24 +168,25 @@
         self.by_z = by_z
         Z = place.Z
         self.n_z = 0
-        self.n_p2 = 2 * (Z - 1)
+        self.n_pass = 2 * Z
+        self.n_p2 = 2 * Z + 2
         self.n_p3 = self.n_p2 + Z
         self.n_sib = self.n_p3 + 2 * Z
         self.n_own = self.n_sib + 4 * Z
 
     @staticmethod
     def sems(Z):
-        return 2 * (Z - 1) + Z + 2 * Z + 4 * Z + 1
+        return 9 * Z + 3
 
     def at(self, index):
         return self.full.at[pl.ds(pl.multiple_of(index * self.rows, self.rows), self.rows)]
 
-    def copy(self, index, number, device, src=None):
+    def copy(self, index, send, recv, device, src=None):
         return pltpu.make_async_remote_copy(
             src_ref=self.at(index) if src is None else src,
             dst_ref=self.at(index),
-            send_sem=self.send.at[number],
-            recv_sem=self.recv.at[number],
+            send_sem=self.send.at[send],
+            recv_sem=self.recv.at[recv],
             device_id=device,
             device_id_type=MESH,
         )
@@ -125,96 +196,109 @@
         index = g.row_block(g.z, g.i2, g.i3, g.c)
         return pltpu.make_async_copy(self.shard, self.at(index), self.recv.at[self.n_own])
 
-    def z_copy(self, other, k, src=None):
+    def z_copy(self, other, z, src=None):
         g = self.g
         a2 = (1 - g.i2) if other else g.i2
-        number = self.n_z + (k - 1) * 2 + int(other)
-        return self.copy(g.row_block(g.z, a2, g.i3, g.c), number, g.at_z(g.above(k)), src)
+        return self.copy(
+            g.row_block(g.z, a2, g.i3, g.c),
+            self.n_z + z * 2 + int(other),
+            self.n_z + g.z * 2 + int(other),
+            g.at_z(z),
+            src,
+        )
+
+    def pass_copy(self, other, z):
+        g = self.g
+        a2 = (1 - g.i2) if other else g.i2
+        return self.copy(
+            g.row_block(z, a2, g.i3, g.c),
+            self.n_pass + int(other),
+            self.n_z + z * 2 + int(other),
+            g.at_z(g.Z - 1 - z),
+        )
 
     def p2_copy(self, z, src=None):
         g = self.g
-        return self.copy(g.row_block(z, g.i2, g.i3, g.c), self.n_p2 + z, g.p2, src)
+        number = self.n_p2 + z
+        return self.copy(g.row_block(z, g.i2, g.i3, g.c), number, number, g.p2, src)
 
     def p3_copy(self, z, a2, src=None):
         g = self.g
-        return self.copy(g.row_block(z, a2, g.i3, g.c), self.n_p3 + z * 2 + a2, g.p3, src)
+        number = self.n_p3 + z * 2 + a2
+        return self.copy(g.row_block(z, a2, g.i3, g.c), number, number, g.p3, src)
 
     def sib_copy(self, z, a2, a3, src=None):
         g = self.g
         number = self.n_sib + g.block(z, a2, a3)
-        return self.copy(g.row_block(z, a2, a3, g.c), number, g.sib, src)
+        return self.copy(g.row_block(z, a2, a3, g.c), number, number, g.sib, src)
 
     def wait(self, number, index):
-        self.copy(index, number, self.g.sib).wait_recv()
-
-    def start(self):
-        g, src = self.g, self.shard
-        self.p2_copy(g.z, src).start()
-        self.p3_copy(g.z, g.i2, src).start()
+        self.copy(index, number, number, self.g.sib).wait_recv()
+
+    def each_z(self, act):
+        g = self.g
         for k in range(1, g.Z):
-            self.z_copy(False, k, src).start()
-        self.sib_copy(g.z, g.i2, g.i3, src).start()
+            z = g.above(k)
+            unless(g.far(z), lambda: act(z))
+
+    def start_z(self):
+        self.each_z(lambda z: self.z_copy(False, z, self.shard).start())
+
+    def start_p2(self):
+        self.p2_copy(self.g.z, self.shard).start()
+
+    def start_p3(self):
+        self.p3_copy(self.g.z, self.g.i2, self.shard).start()
+
+    def start_sib(self):
+        self.sib_copy(self.g.z, self.g.i2, self.g.i3, self.shard).start()
         self.own_copy().start()
 
-    def first_p2(self):
+    def first(self):
         g = self.g
         o2 = 1 - g.i2
         self.wait(self.n_p2 + g.z, g.row_block(g.z, o2, g.i3, g.c))
-
-        def along_z():
-            for k in range(1, g.Z):
-                self.z_copy(True, k).start()
-
-        when(self.by_z, along_z)
+        when(self.by_z, lambda: self.each_z(lambda z: self.z_copy(True, z).start()))
         self.p3_copy(g.z, o2).start()
         self.sib_copy(g.z, o2, g.i3).start()
 
-    def arrived_z(self, k):
-        g = self.g
-        z = g.below(k)
-        self.wait(self.n_z + (k - 1) * 2, g.row_block(z, g.i2, g.i3, g.c))
+    def relay(self, j, z, other):
+        if j == self.g.Z - 2:
+            pl.when(self.g.between(z))(lambda: self.pass_copy(other, z).start())
+
+    def from_z(self, j):
+        g = self.g
+        z = g.near(j)
+        self.wait(self.n_z + z * 2, g.row_block(z, g.i2, g.i3, g.c))
+        self.relay(j, z, False)
         unless(self.by_z, lambda: self.p2_copy(z).start())
         self.p3_copy(z, g.i2).start()
         self.sib_copy(z, g.i2, g.i3).start()
 
-    def later_p2(self, k):
-        g = self.g
-        z = g.below(k)
+    def from_p2(self, j):
+        g = self.g
+        z = g.near(j)
         o2 = 1 - g.i2
-        number = pick(self.by_z, self.n_z + (k - 1) * 2 + 1, self.n_p2 + z)
+        number = pick(self.by_z, self.n_z + z * 2 + 1, self.n_p2 + z)
         self.wait(number, g.row_block(z, o2, g.i3, g.c))
+        when(self.by_z, lambda: self.relay(j, z, True))
         self.p3_copy(z, o2).start()
         self.sib_copy(z, o2, g.i3).start()
 
-    def all_z(self):
-        for k in range(1, self.g.Z):
-            self.arrived_z(k)
-
-    def all_p2(self):
-        for k in range(1, self.g.Z):
-            self.later_p2(k)
-
-    def arrived_p3(self, z):
-        g = self.g
+    def from_p3(self, j):
+        g = self.g
+        z = g.near(j - 1) if j else g.z
         for a2 in (0, 1):
             self.wait(self.n_p3 + z * 2 + a2, g.row_block(z, a2, 1 - g.i3, g.c))
             self.sib_copy(z, a2, 1 - g.i3).start()
 
-    def all_p3(self):
-        g = self.g
-        for k in range(g.Z):
-            self.arrived_p3(g.below(k))
-
-    def arrived_sib(self, z):
-        g = self.g
-        for xx in (0, 1):
-            for yy in (0, 1):
-                number = self.n_sib + (z * 2 + xx) * 2 + yy
-                self.wait(number, ((z * 2 + xx) * 2 + 1 - g.c) * 2 + yy)
-
     def complete(self):
-        for z in range(self.g.Z):
-            self.arrived_sib(z)
+        g = self.g
+        for z in range(g.Z):
+            for xx in (0, 1):
+                for yy in (0, 1):
+                    number = self.n_sib + (z * 2 + xx) * 2 + yy
+                    self.wait(number, ((z * 2 + xx) * 2 + 1 - g.c) * 2 + yy)
         self.own_copy().wait()
 
     def sent(self):
@@ -222,10 +306,17 @@
         self.p2_copy(g.z, src).wait_send()
         self.p3_copy(g.z, g.i2, src).wait_send()
         self.sib_copy(g.z, g.i2, g.i3, src).wait_send()
+        self.each_z(lambda z: self.z_copy(False, z, src).wait_send())
+        when(self.by_z, lambda: self.each_z(lambda z: self.z_copy(True, z).wait_send()))
+        end = g.near(g.Z - 2)
+
+        def passed():
+            self.pass_copy(False, end).wait_send()
+            when(self.by_z, lambda: self.pass_copy(True, end).wait_send())
+
+        pl.when(g.between(end))(passed)
         for k in range(1, g.Z):
-            self.z_copy(False, k, src).wait_send()
             z = g.above(k)
-            when(self.by_z, lambda: self.z_copy(True, k).wait_send())
             unless(self.by_z, lambda: self.p2_copy(z).wait_send())
             self.p3_copy(z, g.i2).wait_send()
             self.sib_copy(z, g.i2, g.i3).wait_send()
@@ -237,20 +328,22 @@
 
 
 class Share:
-    def __init__(self, place, part, first, landing, unit, n, send, recv, write, by_z):
+    def __init__(self, place, part, first, landing, unit, n, send, recv, write, by_z, cols=None):
         self.g, self.part, self.first = place, part, first
         self.rec3, self.rec = landing
         self.unit, self.n, self.send, self.recv, self.write = unit, n, send, recv, write
         self.kind, self.by_z = part.dtype, by_z
+        self.cols = pl.ds(0, part.shape[-1]) if cols is None else cols
 
     @staticmethod
     def sems(Z):
         return 4 * Z - 1
 
     def copy(self, block, landing, slot, number, device):
+        rows = slice(None)
         return pltpu.make_async_remote_copy(
-            src_ref=self.part.at[pl.ds(self.first, self.n), block],
-            dst_ref=landing.at[pl.ds(self.unit, self.n), slot],
+            src_ref=self.part.at[pl.ds(self.first, self.n), block, rows, self.cols],
+            dst_ref=landing.at[pl.ds(self.unit, self.n), slot, rows, self.cols],
             send_sem=self.send.at[number],
             recv_sem=self.recv.at[number],
             device_id=device,
@@ -268,72 +361,84 @@
         block = g.block(z, 1 - g.i2, g.i3)
         return self.copy(block, self.rec, slot, 2 * g.Z + slot, g.p2)
 
-    def z_copy(self, k, a2, by_z):
-        g = self.g
-        z = g.above(k)
-        slot = 1 + (k - 1) * 2 + a2 if by_z else g.Z + k - 1
+    def z_slot(self, k, a2, by_z):
+        return 1 + (k - 1) * 2 + a2 if by_z else self.g.Z + k - 1
+
+    def z_copy(self, z, a2, by_z):
+        g = self.g
+        slot = self.z_slot(lax.rem(z - g.z + g.Z, g.Z), a2, by_z)
         return self.copy(g.block(z, a2, g.i3), self.rec, slot, 2 * g.Z + slot, g.at_z(z))
 
+    def z_wait(self, k, a2, by_z):
+        g = self.g
+        slot = self.z_slot(k, a2, by_z)
+        block = g.block(g.z, a2, g.i3)
+        self.copy(block, self.rec, slot, 2 * g.Z + slot, g.sib).wait_recv()
+        return self.landed(self.rec, slot)
+
     def landed(self, ref, slot):
-        return ref[pl.ds(self.unit, self.n), slot].astype(jnp.float32)
+        return ref[pl.ds(self.unit, self.n), slot, :, self.cols].astype(jnp.float32)
 
     def own(self, block):
-        return self.part[pl.ds(self.first, self.n), block].astype(jnp.float32)
+        return self.part[pl.ds(self.first, self.n), block, :, self.cols].astype(jnp.float32)
+
+    def add_to(self, block, ref, slot):
+        spot = (pl.ds(self.first, self.n), block, slice(None), self.cols)
+        self.part[spot] += ref[pl.ds(self.unit, self.n), slot, :, self.cols]
 
     def put(self, block, total):
-        self.part[pl.ds(self.first, self.n), block] = total.astype(self.kind)
+        self.part[pl.ds(self.first, self.n), block, :, self.cols] = total.astype(self.kind)
 
     def start(self, z):
         for a2 in (0, 1):
             self.p3_copy(z, a2).start()
 
     def start_all(self):
-        g = self.g
-        for k in range(1, g.Z + 1):
-            self.start(g.above(k))
+        for j in range(self.g.Z):
+            self.start(self.g.order(j))
 
     def add3(self, z, a2):
         g = self.g
         self.p3_copy(z, a2).wait_recv()
-        block = g.block(z, a2, g.i3)
-        self.put(block, self.own(block) + self.landed(self.rec3, z * 2 + a2))
-
-    def stage3(self, *ks):
-        g = self.g
-        for k in ks:
-            z = g.above(k)
-            o2 = 1 - g.i2
-            self.add3(z, o2)
-            if k > 0:
-                when(self.by_z, lambda: self.z_copy(k, o2, True).start())
-            unless(self.by_z, lambda: self.p2_copy(z).start())
-            self.add3(z, g.i2)
-            if k > 0:
-                when(self.by_z, lambda: self.z_copy(k, g.i2, True).start())
-
-    def stage2(self):
+        self.add_to(g.block(z, a2, g.i3), self.rec3, z * 2 + a2)
+
+    def stage3(self, j):
+        g = self.g
+        z = g.order(j)
+        o2 = 1 - g.i2
+        own = j == g.Z - 1
+        self.add3(z, o2)
+        if not own:
+            when(self.by_z, lambda: self.z_copy(z, o2, True).start())
+        unless(self.by_z, lambda: self.p2_copy(z).start())
+        self.add3(z, g.i2)
+        if not own:
+            when(self.by_z, lambda: self.z_copy(z, g.i2, True).start())
+
+    def stage2(self, j):
         g = self.g
 
         def with_p2():
-            for k in range(1, g.Z):
-                z = g.above(k)
-                self.p2_copy(z).wait_recv()
-                block = g.block(z, g.i2, g.i3)
-                self.put(block, self.own(block) + self.landed(self.rec, z))
-                self.z_copy(k, g.i2, False).start()
+            z = g.order(j)
+            self.p2_copy(z).wait_recv()
+            self.add_to(g.block(z, g.i2, g.i3), self.rec, z)
+            self.z_copy(z, g.i2, False).start()
+
+        unless(self.by_z, with_p2)
+
+    def sum_z(self):
+        g = self.g
 
         def along_z():
             o2 = 1 - g.i2
             block = g.block(g.z, o2, g.i3)
             total = self.own(block)
             for k in range(1, g.Z):
-                self.z_copy(k, o2, True).wait_recv()
-                total += self.landed(self.rec, 1 + (k - 1) * 2 + o2)
+                total += self.z_wait(k, o2, True)
             self.put(block, total)
             self.p2_copy(g.z).start()
 
         when(self.by_z, along_z)
-        unless(self.by_z, with_p2)
 
     def last(self):
         g = self.g
@@ -341,9 +446,7 @@
         def finish(by_z):
             total = self.own(g.block(g.z, g.i2, g.i3))
             for k in range(1, g.Z):
-                self.z_copy(k, g.i2, by_z).wait_recv()
-                slot = 1 + (k - 1) * 2 + g.i2 if by_z else g.Z + k - 1
-                total += self.landed(self.rec, slot)
+                total += self.z_wait(k, g.i2, by_z)
             self.p2_copy(g.z).wait_recv()
             total += self.landed(self.rec, 0 if by_z else g.z)
             self.write(total)
@@ -361,13 +464,13 @@
             self.p2_copy(g.z).wait_send()
             for k in range(1, g.Z):
                 for a2 in (0, 1):
-                    self.z_copy(k, a2, True).wait_send()
+                    self.z_copy(g.above(k), a2, True).wait_send()
 
         def by_p2():
             for z in range(g.Z):
                 self.p2_copy(z).wait_send()
             for k in range(1, g.Z):
-                self.z_copy(k, g.i2, False).wait_send()
+                self.z_copy(g.above(k), g.i2, False).wait_send()
 
         when(self.by_z, by_z)
         unless(self.by_z, by_p2)
@@ -447,10 +550,9 @@
 
     @loop(bias.shape[0] * blocks)
     def _(i):
-        shape = (block, rows)
-        place = first + lax.broadcasted_iota(jnp.int32, shape, 1)
-        key = i * block + lax.broadcasted_iota(jnp.int32, shape, 0)
-        start = jnp.zeros(shape, jnp.int32)
+        place = first + lax.broadcasted_iota(jnp.int32, (1, rows), 1)
+        key = i * block + lax.broadcasted_iota(jnp.int32, (block, rows), 0)
+        start = jnp.zeros((1, rows), jnp.int32)
         for d in range(DOCS):
             start = jnp.where(place >= ends[d], ends[d], start)
         fine = (key >= start) & (key <= place)
@@ -501,27 +603,28 @@
 def forward_kernel(dp_size, head_dim, *refs):
     (tok, lens, gs, wq, wo, wu, wd, cosine, sine) = refs[:9]
     (out, wq_f, wo_f, wu_f, wd_f, gain_o, q_o, k_o, v_o, ob_o, lse_o) = refs[9:20]
-    (araw_o, h_o, mraw_o, bt_o, gt_o, gp_o, at_o, atx_o) = refs[20:28]
-    (g_full, gain, tokx, a, ax, at, atx, q, k, v, vt, bias, ob, lse) = refs[28:42]
-    (araw, h, mraw, b, bt, act, actt, gp, wbuf, dbuf) = refs[42:52]
-    sems = refs[52:62]
-    wsem, dsem, xsem, osem = refs[62:66]
+    (araw_o, h_o, mraw_o, bt_o, gt_o, gp_o, at_o, atx_o, tokx_o) = refs[20:29]
+    (g_full, gain, tokx, a, ax, at, atx, q, k, v, vt, bias, ob, lse) = refs[29:43]
+    (araw, h, mraw, b, bt, act, actt, gp, wbuf, dbuf) = refs[43:53]
+    sems = refs[53:63]
+    wsem, dsem, xsem, osem = refs[63:67]
+    o_own = refs[67]
     g = Place(dp_size)
     y = g.y
     rows, width = tok.shape
     half = head_dim // 2
     pairs = width // 128
     scale = head_dim ** (-0.5)
-    on_core = g.c == 0
+    modes = [g.c == 0 if m is None else m for m in GATHER_BY_Z]
     gg, gq, go, gu, gd = [
         Gather(g, s, f, sems[2 * i], sems[2 * i + 1], mode)
         for i, (s, f, mode) in enumerate(
             (
                 (gs, g_full, False),
-                (wq, wq_f, MODES[0] and on_core),
-                (wo, wo_f, MODES[1] and on_core),
-                (wu, wu_f, MODES[2] and on_core),
-                (wd, wd_f, MODES[3] and on_core),
+                (wq, wq_f, modes[0]),
+                (wo, wo_f, modes[1]),
+                (wu, wu_f, modes[2]),
+                (wd, wd_f, modes[3]),
             )
         )
     ]
@@ -541,18 +644,30 @@
         device_id=g.device(g.z, g.x, g.c, 1 - y),
         device_id_type=MESH,
     )
+    named = {"g": gg, "q": gq, "o": go, "u": gu, "d": gd}
+
+    def serve(slot):
+        for step in GATHER_PLAN.get(slot, ()):
+            m, kind = named.get(step[0]), step[1]
+            if step == "token":
+                pl.when(y == 0)(lambda: tok_copy.start())
+            elif kind == "s":
+                getattr(m, "start_" + step[2:])()
+            elif kind == "F":
+                m.first()
+            else:
+                act = {"Z": m.from_z, "P": m.from_p2, "T": m.from_p3}[kind]
+                act(int(step[2:]))
+
+    def serve_at(name, t, count):
+        for i in range(count):
+            if (name, i) in GATHER_PLAN:
+                pl.when(t == i)(functools.partial(serve, (name, i)))
+
     g.barrier()
-    gg.start()
-    gq.start()
-    go.start()
-    gu.start()
+    serve("start")
     fill_bias(bias, lens, y * rows, rows)
-    gg.first_p2()
-    gg.all_z()
-    gg.all_p2()
-    gg.all_p3()
-    gq.first_p2()
-    gq.all_z()
+    serve("norm")
     gg.complete()
     turned = jnp.transpose(g_full[...].astype(jnp.float32))
     gain[...] = turned[:8]
@@ -567,19 +682,9 @@
             dst[spot, :] = value.astype(jnp.bfloat16)
             dst_t[:, spot] = jnp.transpose(value).astype(jnp.bfloat16)
 
-    gq.all_p2()
-
-    @pl.when(y == 0)
-    def _():
-        tok_copy.start()
-
-    gd.start()
     first_norm(tok, a, at)
     save(at, at_o)
-    go.first_p2()
-    go.all_z()
-    gq.all_p3()
-    go.all_p2()
+    serve("qkv")
     gq.complete()
 
     tiles = Tiles(lambda t: wq_f.at[:, columns(t, 512)], wbuf, wsem)
@@ -593,13 +698,11 @@
 
     @loop(per)
     def _(t):
+        serve_at("q", t, per)
         u = dot(a[...], tiles.get(t, 3 * per))
         for j in range(4):
             part = turned_pair(u[:, j * 128 : j * 128 + 128], first) * scale
             q[4 * t + j] = part.astype(jnp.bfloat16)
-
-    gu.first_p2()
-    go.all_p3()
 
     def keys(w, t, src, start):
         u = dot(src[...], w)
@@ -617,14 +720,43 @@
 
     @loop(per)
     def _(t):
+        serve_at("k", t, per)
         keys(tiles.get(t + per, 3 * per), t, a, first)
 
     @loop(per)
     def _(t):
+        serve_at("v", t, per)
         values(tiles.get(t + 2 * per, 3 * per), t, a, first)
 
-    gu.all_z()
-    gd.first_p2()
+    def attend(p, block, keys_at):
+        spot = slice(block * 256, block * 256 + 256)
+        heads = split_heads(q[p, spot, :])
+        kk = k[p, keys_at, :]
+        vv = vt[p, :, keys_at]
+        mask = bias[0, keys_at, spot]
+        parts, logs = [], []
+        for i in (0, 1):
+            s = dot_nt(kk, heads[i]) + mask
+            m = jnp.max(s, axis=0, keepdims=True)
+            e = jnp.exp(s - m)
+            total = jnp.sum(e, axis=0, keepdims=True)
+            logs.append(m + jnp.log(total))
+            parts.append(dot(vv, e.astype(jnp.bfloat16)) * (1.0 / total))
+        return spot, parts, logs
+
+    upper = lax.broadcasted_iota(jnp.int32, (128, 256), 0) < head_dim
+    blocks = rows // 256
+
+    @loop(pairs)
+    def _(p):
+        serve_at("pair", p, pairs)
+        for block in range(blocks):
+            spot, parts, logs = attend(p, block, pl.ds(first, (block + 1) * 256))
+            for i in (0, 1):
+                lse[p, i : i + 1, spot] = logs[i]
+            o_own[p, :, spot] = jnp.where(upper, parts[0], parts[1])
+
+    serve("other")
 
     @pl.when(y == 1)
     def _():
@@ -641,48 +773,41 @@
             values(tiles.get(t + 2 * per, 3 * per), t, ax, 0)
 
     save(atx, atx_o)
+    save(tokx, tokx_o)
     save(q, q_o)
     save(k, k_o)
     save(v, v_o)
 
-    def attend(p, block, count):
-        spot = slice(block * 256, block * 256 + 256)
-        heads = split_heads(q[p, spot, :])
-        kk = k[p, :count, :]
-        vv = vt[p, :, :count]
-        parts = []
-        for i in (0, 1):
-            s = dot_nt(kk, heads[i]) + bias[0, :count, spot]
-            m = jnp.max(s, axis=0, keepdims=True)
-            e = jnp.exp(s - m)
-            total = jnp.sum(e, axis=0, keepdims=True)
-            lse[p, i : i + 1, spot] = m + jnp.log(total)
-            parts.append(dot(vv, e.astype(jnp.bfloat16)) * (1.0 / total))
-        upper = lax.broadcasted_iota(jnp.int32, parts[0].shape, 0) < head_dim
-        ob[p, :, spot] = jnp.where(upper, parts[0], parts[1]).astype(jnp.bfloat16)
-
-    events = {
-        0: lambda: gu.all_p2(),
-        2: lambda: gd.all_z(),
-        4: lambda: gu.all_p3(),
-        6: lambda: gd.all_p2(),
-    }
-    blocks = rows // 256
-
-    @loop(pairs)
-    def _(p):
-        for half_row in (0, 1):
-
-            @pl.when(y == half_row)
-            def _():
-                for block in range(blocks):
-                    attend(p, block, (half_row * blocks + block + 1) * 256)
-
-        run_at(p, events)
+    @pl.when(y == 0)
+    def _():
+        @loop(pairs)
+        def _(p):
+            serve_at("more", p, pairs)
+            ob[p] = o_own[p].astype(jnp.bfloat16)
+
+    @pl.when(y == 1)
+    def _():
+        @loop(pairs)
+        def _(p):
+            serve_at("more", p, pairs)
+            for block in range(blocks):
+                spot, parts, logs = attend(p, block, pl.ds(0, rows))
+                shares = []
+                for i in (0, 1):
+                    old = lse[p, i : i + 1, spot]
+                    top = jnp.maximum(old, logs[i])
+                    both = top + jnp.log(jnp.exp(old - top) + jnp.exp(logs[i] - top))
+                    lse[p, i : i + 1, spot] = both
+                    shares.append((jnp.exp(old - both), jnp.exp(logs[i] - both)))
+                own = o_own[p, :, spot]
+                first_head = own * shares[0][0] + parts[0] * shares[0][1]
+                second_head = own * shares[1][0] + parts[1] * shares[1][1]
+                ob[p, :, spot] = jnp.where(upper, first_head, second_head).astype(jnp.bfloat16)
 
     save(ob, ob_o)
     save(lse, lse_o)
 
+    serve("out")
     go.complete()
     tiles = Tiles(lambda t: wo_f.at[:, columns(t, 512)], wbuf, wsem)
     tiles.first(per)
@@ -709,6 +834,7 @@
     save(h, h_o)
     save(bt, bt_o)
 
+    serve("up")
     gu.complete()
     tiles = Tiles(lambda t: wu_f.at[:, columns(t, 512)], wbuf, wsem)
     ups = act.shape[0]
@@ -717,6 +843,7 @@
 
     @loop(ups)
     def _(t):
+        serve_at("up", t, ups)
         u = dot(b[...], tiles.get(t, ups))
         square = u * u
         th = jnp.tanh(c0 * (u + 0.044715 * (square * u)))
@@ -731,7 +858,7 @@
     save(actt, gt_o)
     save(gp, gp_o)
 
-    gd.all_p3()
+    serve("down")
     gd.complete()
     tiles = Tiles(lambda t: wd_f.at[columns(t, 512), :], dbuf, dsem)
     tiles.first(ups)
@@ -800,6 +927,7 @@
         shape((ups, rows, 512), bf),
         shape((width, rows), bf),
         shape((width, rows), bf),
+        shape((rows, width), bf),
     ]
     scratch = [
         pltpu.VMEM((width, 128), bf),
@@ -829,6 +957,7 @@
     ]
     scratch += [pltpu.SemaphoreType.DMA((Gather.sems(dp_size // 4),))] * 10
     scratch += [pltpu.SemaphoreType.DMA((3,))] * 3 + [pltpu.SemaphoreType.DMA((16,))]
+    scratch += [pltpu.VMEM((pairs, 128, rows), f32)]
     return pl.pallas_call(
         functools.partial(forward_kernel, dp_size, head_dim),
         out_shape=outs,
@@ -844,22 +973,23 @@
 
 
 def backward_kernel(dp_size, head_dim, *refs):
-    (tok, dout, lens, gain, cosine, sine, wq, wo, wu, wd) = refs[:10]
-    (q_i, k_i, v_i, ob_i, lse_i, araw_i, h_i, mraw_i, bt_i, gt_i, gp_i, at_i, atx_i) = refs[10:23]
-    (dtok, out_q, out_o, out_u, out_d, out_g) = refs[23:29]
-    (gts, dus, dzs) = refs[29:32]
-    (part, rec3, rec, gpart, grec3, grec) = refs[32:38]
-    (f1, f2, acc, dm, dms, da, das, dz, bt, bts, obts, ats, atx, atxs) = refs[38:52]
-    (q, ob, lse, dk, dv, dg, dgs, dgt, dnxs) = refs[52:61]
-    (kbuf, vbuf, wbuf, dbuf, gbuf, gsbuf, gpbuf, sbuf) = refs[61:69]
+    (tok_i, dout, lens, gain, cosine_i, sine_i, wq, wo, wu, wd) = refs[:10]
+    (q_i, k_i, v_i, ob_i, lse_i, araw_i, h_i, mraw_i, bt_i, gt_i, gp_i, at_i, atx_i, tokx_i) = refs[10:24]
+    (dtok, out_q, out_o, out_u, out_d, out_g) = refs[24:30]
+    (gts, dus, dzs) = refs[30:33]
+    (part, rec3, rec, gpart, grec3, grec) = refs[33:39]
+    (f1, f2, acc, dm, dms, da, das, dz, bt, bts, obts, ats, atx, atxs) = refs[39:53]
+    (q, ob, lse, dk, dv, dg, dgs, dgt, dnxs) = refs[53:62]
+    (kbuf, vbuf, wbuf, dbuf, gbuf, gpbuf, sbuf) = refs[62:69]
     tsems = refs[69:79]
     usend, urecv, gsend, grecv, zsend, zrecv, osend, orecv, lsem = refs[79:88]
     dnsem = refs[88]
-    gsems, rsems = refs[89:95], refs[95:101]
-    at, xbuf, do, dnx = bt, gpbuf, dm, da
+    gsems, rsems = refs[89:96], refs[96:103]
+    tok, cosine, sine = refs[103:106]
+    at, xbuf, do, dnx, tokx = bt, gpbuf, dm, da, das
     g = Place(dp_size)
     Z, y, c = g.Z, g.y, g.c
-    rows, width = tok.shape
+    rows, width = dout.shape
     half = head_dim // 2
     pairs = width // 128
     scale = head_dim ** (-0.5)
@@ -888,15 +1018,26 @@
     ob_load = load(ob_i, ob, 4)
     lse_load = load(lse_i, lse, 5)
     at_load = load(at_i.at[:, c], at, 6)
+    tokx_load = load(tokx_i, tokx, 7)
+    tok_load = load(tok_i, tok, 8)
+    cosine_load = load(cosine_i, cosine, 9)
+    sine_load = load(sine_i, sine, 10)
 
     def gt_send(i):
-        return to_sib(gt_i.at[i, 1 - c], gts.at[i], gsend.at[i], grecv.at[i])
+        half_z = pl.ds(pl.multiple_of(lax.rem(i, 2) * 256, 256), 256)
+        return to_sib(
+            gt_i.at[i, 1 - c], gts.at[lax.div(i, 2), half_z], gsend.at[i], grecv.at[i]
+        )
 
     bt_send = to_sib(bt_i.at[:, 1 - c], bts, osend.at[0], orecv.at[0])
     ob_send = to_sib(ob_i.at[:, 1 - c], obts, osend.at[1], orecv.at[1])
     at_send = to_sib(at_i.at[:, 1 - c], ats, osend.at[2], orecv.at[2])
     atx_send = to_sib(atx_i.at[:, 1 - c], atxs, osend.at[3], orecv.at[3])
-    dm_send = to_sib(dm, dms, osend.at[4], orecv.at[4])
+
+    def dm_send(i):
+        spot = columns(i, 128)
+        return to_sib(dm.at[spot, :], dms.at[spot, :], osend.at[7 + i], orecv.at[7 + i])
+
     da_send = to_sib(da, das, osend.at[5], orecv.at[5])
     dg_send = to_sib(dg, dgs, osend.at[6], orecv.at[6])
     dnx_send = pltpu.make_async_remote_copy(
@@ -911,8 +1052,11 @@
     def du_send(t):
         return to_sib(dz.at[t], dus.at[t], usend.at[t], urecv.at[t])
 
-    def dz_send(t):
-        return to_sib(dz.at[t], dzs.at[t], zsend.at[t], zrecv.at[t])
+    def dz_send(e, p):
+        t = e * per + lax.div(p, 4)
+        spot = columns(lax.rem(p, 4), 128)
+        n = e * pairs + p
+        return to_sib(dz.at[t, :, spot], dzs.at[t, :, spot], zsend.at[n], zrecv.at[n])
 
     landing = (rec3, rec)
 
@@ -922,41 +1066,61 @@
     def write_into(out, column):
         def write(total):
             for i in range(total.shape[0]):
-                out[:, column + i * width : column + (i + 1) * width] = total[i]
+                begin = column + i * width
+                out[:, begin : begin + total.shape[2]] = total[i]
 
         return write
 
     def write_g(total):
         out_g[...] = total[0]
 
-    on_core = c == 0
+    modes = [c == 0 if m is None else m for m in SHARE_BY_Z]
     s_d = Share(
-        g, part, 0, landing, 0, 4, gsems[0], rsems[0], write_d, MODES[3] and on_core
+        g, part, 0, landing, 0, 4, gsems[0], rsems[0], write_d, modes[3]
     )
     s_u = [
         Share(
             g, part, 4 + 2 * i, landing, 4 + 2 * i, 2, gsems[1 + i], rsems[1 + i],
-            write_into(out_u, 2 * i * width), MODES[2] and on_core,
+            write_into(out_u, 2 * i * width), modes[2],
         )
         for i in (0, 1)
     ]
     s_o = Share(
         g, part, 8, landing, 8, 1, gsems[3], rsems[3], write_into(out_o, 0),
-        MODES[1] and on_core,
+        modes[1],
     )
-    s_q = Share(
-        g, part, 0, landing, 9, 3, gsems[4], rsems[4], write_into(out_q, 0),
-        MODES[0] and on_core,
-    )
-    s_g = Share(g, gpart, 0, (grec3, grec), 0, 1, gsems[5], rsems[5], write_g, False)
+    s_q = [
+        Share(
+            g, part, 9, landing, 9, 3, gsems[4 + i], rsems[4 + i],
+            write_into(out_q, i * 512), modes[0], pl.ds(i * 512, 512),
+        )
+        for i in (0, 1)
+    ]
+    s_g = Share(g, gpart, 0, (grec3, grec), 0, 1, gsems[6], rsems[6], write_g, False)
+    named = {"d": s_d, "u": s_u[0], "v": s_u[1], "o": s_o, "a": s_q[0], "b": s_q[1], "g": s_g}
+
+    def serve(slot):
+        for step in SHARE_PLAN.get(slot, ()):
+            s = named[step[0]]
+            if step[1] == "L":
+                s.last()
+            elif step[1] == "E":
+                s.sum_z()
+            else:
+                (s.stage3 if step[1] == "3" else s.stage2)(int(step[2]))
+
+    def serve_at(name, t, count):
+        for i in range(count):
+            if (name, i) in SHARE_PLAN:
+                pl.when(t == i)(functools.partial(serve, (name, i)))
 
     mraws = Tiles(lambda i: mraw_i.at[columns(i, 128), :], f1, tsems[9])
     araws = Tiles(lambda i: araw_i.at[columns(i, 128), :], f1, tsems[9])
     mraws.first(rows // 128)
     g.barrier()
-    for k in range(1, Z + 1):
+    for j in range(Z):
         for i in (0, 1):
-            gt_send(g.above(k) * 2 + i).start()
+            gt_send(g.order(j) * 2 + i).start()
     for copy in (bt_send, ob_send, at_send):
         copy.start()
 
@@ -964,14 +1128,19 @@
     def _():
         atx_send.start()
 
+    def z_of(j):
+        return sum(jnp.where(j == i, g.order(i), 0) for i in range(Z))
+
     def gt_ready(j):
         for i in (0, 1):
-            gt_send(g.above(j + 1) * 2 + i).wait_recv()
-
-    own_g = Tiles(lambda j: gt_i.at[pl.ds(g.above(j + 1) * 2, 2), c], gbuf, tsems[0])
-    sib_g = Tiles(lambda j: gts.at[pl.ds(g.above(j + 1) * 2, 2)], gsbuf, tsems[1], gt_ready)
+            gt_send(z_of(j) * 2 + i).wait_recv()
+
+    own_g = Tiles(lambda j: gt_i.at[pl.ds(z_of(j) * 2, 2), c], gbuf, tsems[0])
+    sib_g = Tiles(lambda j: gts.at[z_of(j)], sbuf, tsems[1], gt_ready)
     own_g.first(Z)
-    for copy in (h_load, bt_load, atx_load, q_load, ob_load, lse_load):
+    for copy in (
+        h_load, bt_load, atx_load, q_load, ob_load, lse_load, cosine_load, sine_load, tok_load
+    ):
         copy.start()
     dg[...] = jnp.zeros_like(dg)
     ends = doc_ends(lens)
@@ -989,21 +1158,27 @@
         value, term = norm_pull(mraws.get(i, rows // 128), gain[3:4, :], upstream(i))
         dm[pl.ds(i * 128, 128), :] = value.astype(bf)
         gain_sum(3, term)
-
-    dm_send.start()
+        dm_send(i).start()
+
     downs = Tiles(lambda t: wd.at[columns(t, 512), :], dbuf, tsems[2])
     upw = Tiles(lambda t: wu.at[:, columns(t, 512)], wbuf, tsems[3])
     slopes = Tiles(lambda t: gp_i.at[t], gpbuf, tsems[4])
     for tiles in (downs, upw, slopes):
         tiles.first(ups)
+    araws.first(rows // 128)
+    keys = Tiles(lambda p: k_i.at[p], kbuf, tsems[6])
+    values = Tiles(lambda p: v_i.at[p], vbuf, tsems[7])
+    keys.first(pairs)
+    values.first(pairs)
     sib_g.first(Z)
-    dm_send.wait_recv()
+    for i in range(rows // 128):
+        dm_send(i).wait_recv()
 
     @loop(Z)
     def _(j):
-        z = g.above(j + 1)
+        z = z_of(j)
         total = dot(own_g.get(j, Z).reshape(512, rows), dm[...])
-        total += dot(sib_g.get(j, Z).reshape(512, rows), dms[...])
+        total += dot(sib_g.get(j, Z), dms[...])
         total = total.astype(bf).reshape(4, 4, 32, width)
         for a in range(4):
             for e in range(4):
@@ -1014,28 +1189,29 @@
         for j in (0, 1):
             halves[j] += dot_nt(value, weights[j * 512 : (j + 1) * 512])
 
+    sib_du = Tiles(lambda t: dus.at[t], sbuf, tsems[5], lambda t: du_send(t).wait_recv())
     acc[...] = jnp.zeros_like(acc)
 
     @loop(ups)
     def _(t):
+        serve_at("du", t, ups)
         du = dot_nt(dm[...], downs.get(t, ups)) * slopes.get(t, ups).astype(f32)
         du = du.astype(bf)
         dz[t] = du
         du_send(t).start()
         add_to(acc, du, upw.get(t, ups))
-        run_at(t, {3: lambda: s_d.stage3(1), 7: lambda: s_d.stage3(2)})
+        pl.when(t == 3)(lambda: sib_du.first(ups))
 
     outs = Tiles(lambda t: wo.at[columns(t, 512), :], dbuf, tsems[2])
     outs.first(per)
     bt_load.wait()
     bt_send.wait_recv()
-    sib_du = Tiles(lambda t: dus.at[t], sbuf, tsems[5], lambda t: du_send(t).wait_recv())
-    sib_du.first(ups)
     for i in (0, 1):
 
         @loop(ups // 2)
         def _(t2):
             t = t2 + i * (ups // 2)
+            serve_at("up", t, ups)
             total = dot(bt[...].reshape(-1, rows), dz[t])
             total += dot(bts[...].reshape(-1, rows), sib_du.get(t, ups))
             part[4 + lax.div(t, per), :, :, columns(lax.rem(t, per), 512)] = (
@@ -1043,11 +1219,10 @@
             )
 
         s_u[i].start_all()
-        s_d.stage3(3 if i == 0 else 0)
 
     at_load.start()
 
-    araws.first(rows // 128)
+    serve("norm")
     h_load.wait()
 
     @loop(rows // 128)
@@ -1063,13 +1238,15 @@
         da[spot, :] = value.astype(bf)
 
     da_send.start()
-    dm_send.wait_send()
-    s_d.stage2()
+    for i in range(rows // 128):
+        dm_send(i).wait_send()
+    serve("do")
 
     @loop(per)
     def _(t):
         do[:, columns(t, 512)] = dot_nt(da[...], outs.get(t, per)).astype(bf)
 
+    serve("out")
     ob_load.wait()
     ob_send.wait_recv()
     da_send.wait_recv()
@@ -1084,28 +1261,27 @@
     for t in range(ups):
         du_send(t).wait_send()
 
-    keys = Tiles(lambda p: k_i.at[p], kbuf, tsems[6])
-    values = Tiles(lambda p: v_i.at[p], vbuf, tsems[7])
-    keys.first(pairs)
-    values.first(pairs)
+    qkv_w = Tiles(lambda t: wq.at[:, columns(t, 512)], wbuf, tsems[3])
+    pl.when(y == 1)(lambda: qkv_w.first(3 * per, per))
+    serve("mask")
     fill_bias(acc, lens, y * rows, rows)
-    q_load.wait()
-    lse_load.wait()
+    pl.when(y == 1)(lambda: tokx_load.start())
+    for copy in (q_load, lse_load, cosine_load, sine_load, tok_load):
+        copy.wait()
     blocks = rows // 256
 
-    def bias(count, spot):
-        if count <= 512:
-            return acc[0, :count, spot]
-        return jnp.concatenate([acc[0, :, spot], acc[1, : count - 512, spot]], axis=0)
-
-    def attend(p, block, count, fresh, kk, vv, kt):
+    def attend(p, block, base, count, fresh):
         spot = slice(block * 256, block * 256 + 256)
+        slot = lax.rem(p, 2)
+        kk = kbuf[slot, pl.ds(base, count), :]
+        vv = vbuf[slot, pl.ds(base, count), :]
+        kt = jnp.transpose(kk.astype(f32)).astype(bf)
         qs = split_heads(q[p, spot, :])
         do_pair = do[spot, columns(p, 128)]
         dos = split_heads(do_pair)
         ob_pair = ob[p, :, :, spot].astype(f32).reshape(128, -1)
         dot_o = jnp.transpose(do_pair.astype(f32)) * ob_pair
-        mask = bias(count, spot)
+        mask = acc[lax.div(base, 512), :count, spot]
         parts, dk_, dv_ = [], [], []
         for i in (0, 1):
             delta = jnp.sum(
@@ -1126,129 +1302,134 @@
         upper = lax.broadcasted_iota(jnp.int32, parts[0].shape, 0) < head_dim
         dq = jnp.transpose(jnp.where(upper, parts[0], parts[1]) * scale)
         start = pl.multiple_of(first + block * 256, 256)
-        dq = turn(dq, cosine[pl.ds(start, 256), :], -sine[pl.ds(start, 256), :], half)
-        dz[lax.div(p, 4), spot, lanes(p)] = dq.astype(bf)
+        return spot, turn(dq, cosine[pl.ds(start, 256), :], -sine[pl.ds(start, 256), :], half)
 
     def lanes(p):
         return columns(lax.rem(p, 4), 128)
 
     def keep(p, start, base):
         spot = pl.ds(start, rows)
-        u = turn(dk[spot, :], cosine[spot, :], -sine[spot, :], half)
+        u = turn(dk[...], cosine[spot, :], -sine[spot, :], half)
         dz[base + lax.div(p, 4), :, lanes(p)] = u.astype(bf)
-        dz[base + per + lax.div(p, 4), :, lanes(p)] = dv[spot, :].astype(bf)
-
-    events = {
-        0: lambda: s_u[0].stage3(1, 2),
-        1: lambda: s_u[0].stage3(3, 0),
-        2: lambda: s_d.last(),
-        3: lambda: s_u[0].stage2(),
-        4: lambda: s_u[1].stage3(1, 2, 3, 0),
-        5: lambda: s_o.stage3(1, 2, 3, 0),
-        6: lambda: (s_u[1].stage2(), s_u[0].last())[1],
-        7: lambda: s_o.stage2(),
-    }
-
-    @loop(pairs)
-    def _(p):
-        kk = keys.get(p, pairs)
-        vv = values.get(p, pairs)
-        kt = jnp.transpose(kk.astype(f32)).astype(bf)
-        for half_row in (0, 1):
-
-            @pl.when(y == half_row)
-            def _():
-                for block in reversed(range(blocks)):
-                    count = (half_row * blocks + block + 1) * 256
-                    attend(p, block, count, block == blocks - 1, kk[:count], vv[:count], kt[:, :count])
-
-        keep(p, first, per)
-
-        @pl.when(y == 1)
-        def _():
-            keep(p, 0, 3 * per)
-
-        @pl.when(lax.rem(p, 4) == 3)
-        def _():
-            for e in range(3):
-                dz_send(e * per + lax.div(p, 4)).start()
-
-            @pl.when(y == 1)
-            def _():
-                for e in (3, 4):
-                    dz_send(e * per + lax.div(p, 4)).start()
-
-        run_at(p, events)
-
-    qkv_w = Tiles(lambda t: wq.at[:, columns(t, 512)], wbuf, tsems[3])
-
-    @pl.when(y == 1)
-    def _():
-        qkv_w.first(3 * per, per)
+        dz[base + per + lax.div(p, 4), :, lanes(p)] = dv[...].astype(bf)
+
+    def other_half():
         acc[...] = jnp.zeros_like(acc)
         da_send.wait_send()
+        tokx_load.wait()
 
         @loop(2 * per)
         def _(t):
             add_to(acc, dz[t + 3 * per], qkv_w.get(t + per, 3 * per))
 
-        dnx[:, :512] = acc[0].astype(bf)
-        dnx[:, 512:] = acc[1].astype(bf)
+        @loop(rows // 128)
+        def _(i):
+            spot = pl.ds(i * 128, 128)
+            e = jnp.concatenate([acc[0, spot, :], acc[1, spot, :]], axis=1)
+            value, term = norm_pull(tokx[spot, :].astype(f32), gain[0:1, :], e)
+            gain_sum(0, term)
+            dnx[spot, :] = value.astype(bf)
+
         dnx_send.start()
 
-    qkv_w.first(3 * per)
-    s_d.sent()
-    atx_load.wait()
-    at_load.wait()
-    at_send.wait_recv()
+    def qkv_gradient(h):
+        at_both = (at[...].reshape(-1, rows), ats[...].reshape(-1, rows))
+
+        def ready(i):
+            for j in range(4):
+                dz_send(i, h * 4 + j).wait_recv()
+
+        sib_dz = Tiles(lambda i: dzs.at[i * per + h], sbuf, tsems[5], ready)
+        sib_dx = Tiles(lambda i: dzs.at[i * per + h], xbuf, tsems[8], ready)
+        sib_dz.first(3)
+        pl.when(y == 1)(lambda: sib_dx.first(5, 3))
+
+        @loop(3)
+        def _(e):
+            def total():
+                return dot(at_both[0], dz[e * per + h]) + dot(at_both[1], sib_dz.get(e, 3))
+
+            def keep_total(value):
+                part[9 + e, :, :, columns(h, 512)] = value.astype(bf).reshape(4 * Z, 32, 512)
+
+            both = (y == 1) & (e > 0)
+
+            @pl.when(jnp.logical_not(both))
+            def _():
+                keep_total(total())
+
+            @pl.when(both)
+            def _():
+                value = total() + dot(atx[...].reshape(-1, rows), dz[(e + 2) * per + h])
+                keep_total(value + dot(atxs[...].reshape(-1, rows), sib_dx.get(e + 2, 5)))
+
+        for i in (0, 1):
+            pl.when(h == i)(lambda: s_q[i].start_all())
+
+    @pl.when(y == 0)
+    def _():
+        for p in range(pairs):
+            serve(("more", p))
+        serve("other")
 
     @pl.when(y == 1)
     def _():
-        atx_send.wait_recv()
-
-    def dz_ready(t):
-        dz_send(t).wait_recv()
-
-    sib_dz = Tiles(lambda t: dzs.at[t], sbuf, tsems[5], dz_ready)
-    sib_dx = Tiles(lambda t: dzs.at[t], xbuf, tsems[8], dz_ready)
-    sib_dz.first(3 * per)
-
-    @pl.when(y == 1)
-    def _():
-        sib_dx.first(5 * per, 3 * per)
-
-    @loop(3 * per)
-    def _(t):
-        acc[0] = dot(at[...].reshape(-1, rows), dz[t]) + dot(
-            ats[...].reshape(-1, rows), sib_dz.get(t, 3 * per)
-        )
-
-        @pl.when((y == 1) & (t >= per))
+        @loop(pairs)
+        def _(p):
+            serve_at("more", p, pairs)
+            keys.get(p, pairs)
+            values.get(p, pairs)
+            for block in range(blocks):
+                spot, dq = attend(p, block, 0, rows, block == 0)
+                dz[lax.div(p, 4), spot, lanes(p)] = dq.astype(bf)
+            keep(p, 0, 3 * per)
+            for e in (3, 4):
+                dz_send(e, p).start()
+
+        serve("other")
+        keys.first(pairs)
+        values.first(pairs)
+        other_half()
+        fill_bias(acc, lens, y * rows, rows)
+
+    @loop(pairs)
+    def _(p):
+        serve_at("pair", p, pairs)
+        keys.get(p, pairs)
+        values.get(p, pairs)
+        for block in reversed(range(blocks)):
+            spot, dq = attend(p, block, first, (block + 1) * 256, block == blocks - 1)
+            before = dz[lax.div(p, 4), spot, lanes(p)].astype(f32)
+            dq += jnp.where(y == 1, before, 0.0)
+            dz[lax.div(p, 4), spot, lanes(p)] = dq.astype(bf)
+        keep(p, first, per)
+        for e in range(3):
+            dz_send(e, p).start()
+
+        @pl.when(p == pairs // 2 - 1)
         def _():
-            tx = t + 2 * per
-            acc[0] += dot(atx[...].reshape(-1, rows), dz[tx]) + dot(
-                atxs[...].reshape(-1, rows), sib_dx.get(tx, 5 * per)
-            )
-
-        part[lax.div(t, per), :, :, columns(lax.rem(t, per), 512)] = (
-            acc[0].astype(bf).reshape(4 * Z, 32, 512)
-        )
-
-    s_q.start_all()
-    s_u[1].last()
-    s_o.last()
+            serve("half")
+            at_load.wait()
+            at_send.wait_recv()
+            atx_load.wait()
+            pl.when(y == 1)(lambda: atx_send.wait_recv())
+
+        @pl.when(p == pairs - 1)
+        def _():
+            serve("rest")
+
+        @pl.when(lax.rem(p, 4) == 3)
+        def _():
+            qkv_gradient(lax.div(p, 4))
+
+    serve("input")
+    qkv_w.first(3 * per)
 
     acc[...] = jnp.zeros_like(acc)
 
     @loop(3 * per)
     def _(t):
         add_to(acc, dz[t], qkv_w.get(t, 3 * per))
-
-    @pl.when(y == 0)
-    def _():
-        dnx_send.wait_recv()
-        acc[0] += dnxs[:, :512].astype(f32)
-        acc[1] += dnxs[:, 512:].astype(f32)
 
     @loop(rows // 128)
     def _(i):
@@ -1256,28 +1437,34 @@
         e = jnp.concatenate([acc[0, spot, :], acc[1, spot, :]], axis=1)
         value, term = norm_pull(tok[spot, :].astype(f32), gain[0:1, :], e)
         gain_sum(0, term)
-        dtok[spot, :] = (f2[spot, :] + value).astype(bf)
+        f2[spot, :] += value
 
     dg_send.start()
-    s_q.stage3(1)
+    serve("gains")
     dg_send.wait_recv()
     wide = jnp.concatenate([dg[...] + dgs[...], jnp.zeros((120, width), f32)], axis=0)
     dgt[...] = jnp.transpose(wide).reshape(dgt.shape)
     gpart[0] = dgt[:, c].reshape(gpart.shape[1:])
     s_g.start_all()
-    s_q.stage3(2, 3, 0)
-    s_g.stage3(1, 2, 3, 0)
-    s_q.stage2()
-    s_g.stage2()
-    s_q.last()
-    s_g.last()
+    serve("end")
+
+    @pl.when(y == 0)
+    def _():
+        dnx_send.wait_recv()
+        dtok[...] = (f2[...] + dnxs[...].astype(f32)).astype(bf)
+
+    @pl.when(y == 1)
+    def _():
+        dtok[...] = f2[...].astype(bf)
 
     for i in range(2 * Z):
-        gt_send(i).wait_send()
+        gt_send(jnp.int32(i)).wait_send()
     for copy in (bt_send, ob_send, at_send, dg_send):
         copy.wait_send()
-    for t in range(3 * per):
-        dz_send(t).wait_send()
+    @loop(pairs)
+    def _(p):
+        for e in range(3):
+            dz_send(e, p).wait_send()
 
     @pl.when(y == 0)
     def _():
@@ -1287,10 +1474,13 @@
     def _():
         atx_send.wait_send()
         dnx_send.wait_send()
-        for t in range(3 * per, 5 * per):
-            dz_send(t).wait_send()
-
-    for s in (s_u[0], s_u[1], s_o, s_q, s_g):
+
+        @loop(pairs)
+        def _(p):
+            for e in (3, 4):
+                dz_send(e, p).wait_send()
+
+    for s in (s_d, s_u[0], s_u[1], s_o, s_q[0], s_q[1], s_g):
         s.sent()
 
 
@@ -1319,13 +1509,13 @@
         shape(shards[2].shape, f32),
         shape(shards[3].shape, f32),
         shape((block, 128), f32),
-        shape((2 * Z, 256, rows), bf),
+        shape((Z, 512, rows), bf),
         shape((ups, rows, 512), bf),
         shape((5 * per, rows, 512), bf),
     ]
     core_rows = (2 * Z, width // (4 * Z), rows)
     scratch = [
-        pltpu.VMEM((9, 4 * Z, block, width), bf),
+        pltpu.VMEM((12, 4 * Z, block, width), bf),
         pltpu.VMEM((12, 2 * Z, block, width), bf),
         pltpu.VMEM((12, 2 * Z - 1, block, width), bf),
         pltpu.VMEM((1, 4 * Z, block, 128), f32),
@@ -1345,8 +1535,8 @@
         pltpu.VMEM((pairs, rows, 128), bf),
         pltpu.VMEM((2 * Z, 2, width // (4 * Z), rows), bf),
         pltpu.VMEM((pairs, 2, rows), f32),
-        pltpu.VMEM((row_len, 128), f32),
-        pltpu.VMEM((row_len, 128), f32),
+        pltpu.VMEM((rows, 128), f32),
+        pltpu.VMEM((rows, 128), f32),
         pltpu.VMEM((8, width), f32),
         pltpu.VMEM((8, width), f32),
         pltpu.VMEM((2 * Z, 2, width // (4 * Z), 128), f32),
@@ -1356,25 +1546,52 @@
         pltpu.VMEM((2, width, 512), bf),
         pltpu.VMEM((2, 512, width), bf),
         pltpu.VMEM((2, 2, 256, rows), bf),
-        pltpu.VMEM((2, 2, 256, rows), bf),
         pltpu.VMEM((2, rows, 512), bf),
         pltpu.VMEM((2, rows, 512), bf),
     ]
     dma = pltpu.SemaphoreType.DMA
     scratch += [dma((3,))] * 10
-    scratch += [dma((ups,))] * 2 + [dma((2 * Z,))] * 2 + [dma((5 * per,))] * 2
-    scratch += [dma((7,))] * 2 + [dma((7,)), dma((2,))]
-    scratch += [dma((Share.sems(Z),))] * 12
+    scratch += [dma((ups,))] * 2 + [dma((2 * Z,))] * 2 + [dma((5 * pairs,))] * 2
+    scratch += [dma((11,))] * 2 + [dma((11,)), dma((2,))]
+    scratch += [dma((Share.sems(Z),))] * 14
+    scratch += [pltpu.VMEM((rows, width), bf)] + [pltpu.VMEM((row_len, 128), f32)] * 2
     return pl.pallas_call(
         functools.partial(backward_kernel, dp_size, head_dim),
         out_shape=outs,
-        in_specs=[vm, vm, smem, vm, vm, vm] + [any_spec] * 17,
+        in_specs=[any_spec, vm, smem, vm] + [any_spec] * 20,
         out_specs=[vm] * 6 + [any_spec] * 3,
         scratch_shapes=scratch,
         compiler_params=pltpu.CompilerParams(
             collective_id=1, has_side_effects=True, vmem_limit_bytes=63 * 2**20
         ),
     )(tokens, d_out, lengths, gain_rows, *tables, *weights, *saved)
+
+
+def hand_on(*arrays):
+    n = len(arrays) - 1
+
+    def kernel(*refs):
+        sources, targets, sems = refs[: n + 1], refs[n + 1 : 2 * n + 2], refs[-1]
+        copies = [
+            pltpu.make_async_copy(sources[i], targets[i], sems.at[i]) for i in range(n)
+        ]
+        for copy in copies:
+            copy.start()
+        targets[n][...] = sources[n][:, : targets[n].shape[1]]
+        for copy in copies:
+            copy.wait()
+
+    any_spec = pl.BlockSpec(memory_space=pl.ANY)
+    vm = pl.BlockSpec(memory_space=pltpu.VMEM)
+    shapes = [jax.ShapeDtypeStruct(a.shape, a.dtype) for a in arrays[:n]]
+    shapes.append(jax.ShapeDtypeStruct((arrays[n].shape[0], 4), arrays[n].dtype))
+    return pl.pallas_call(
+        kernel,
+        out_shape=shapes,
+        in_specs=[vm] * (n + 1),
+        out_specs=[any_spec] * n + [vm],
+        scratch_shapes=[pltpu.SemaphoreType.DMA((n,))],
+    )(*arrays)
 
 
 def layer_norm(values, gain_vec):
@@ -1634,14 +1851,8 @@
         saved,
         (w_qkv, w_out, w_up, w_down),
     )[:6]
-    return (
-        output,
-        d_tokens,
-        grad_qkv,
-        grad_out,
-        grad_up,
-        grad_down,
-        grad_gains[:, : gains.shape[1]],
+    return tuple(
+        hand_on(output, d_tokens, grad_qkv, grad_out, grad_up, grad_down, grad_gains)
     )
 
 

time: 355 us -> 303 us (0.85)
  the two profiles are of different devices: /device:TPU:1 before, /device:TPU:0 now
where the time goes in v5:
time: 303 us
  Pallas kernels  299 us (99%)
    pallas_call x1, Pallas kernels, backward(): pl.pallas_call(functools.partial(backward_kernel, dp_size, head_dim), out...  156 us
    pallas_call x1, Pallas kernels, forward(): pl.pallas_call(functools.partial(forward_kernel, dp_size, head_dim), out_...  139 us

profile of v5, /device:TPU:0, one launch (start us, length us, event | category | flops | bytes accessed | tf_op | source)
XLA Modules:
  0.0 302.6 jit_solution(799516379405275665)
XLA Ops:
  0.6 0.8 copy.17
  1.4 0.6 pad.4.refs_2_
  2.0 138.6 %shard_map.153 = (bf16[512,1024]{1,0:T(8,128)(2,1)}, bf16[1024,3072]{1,0:T(8,128)(2,1)}, bf16[1024,1024]{1,0:T(8,128)(2,1)}, bf16[1024,4096]{1,0:T(8,128)(2,1)},...) custom-call(bf16[512,1024]{1,0:T(8,128)(2,1)} %refs_0_.3, ...), custom_call_target="tpu_custom_call" | custom-call | tf_op jit(solution)/shard_map/pallas_call | solution.py:961
  140.6 156.1 %shard_map.154 = (bf16[512,1024]{1,0:T(8,128)(2,1)}, f32[32,3072]{1,0:T(8,128)}, f32[32,1024]{1,0:T(8,128)}, f32[32,4096]{1,0:T(8,128)}, f32[128,1024]{1,0:T(8,1...) custom-call(bf16[512,1024]{1,0:T(8,128)(2,1)} %refs_0_.3, ...), custom_call_target="tpu_custom_call" | custom-call | tf_op jit(solution)/shard_map/pallas_call | solution.py:1558
  296.7 4.5 %shard_map.155 = (bf16[512,1024]{1,0:T(8,128)(2,1)}, bf16[512,1024]{1,0:T(8,128)(2,1)}, f32[32,3072]{1,0:T(8,128)}, f32[32,1024]{1,0:T(8,128)}, f32[32,4096]{1,0...) custom-call(bf16[512,1024]{1,0:T(8,128)(2,1)} %get-tuple-element.33.refs_0_, ...), custom_call_target="tpu_custom_call" | custom-call | tf_op jit(solution)/shard_map/pallas_call | solution.py:1588
  301.2 1.4 copy.18

commit v6 on v5

--- a/solution.py
+++ b/solution.py
@@ -13,55 +13,98 @@
 DOCS = 7
 
 GATHER_BY_Z = (False, None, None, True)
-SHARE_BY_Z = (None, True, False, None)
-
+SHARE_BY_Z = (None, None, None, None)
+
+TOKENS = 999
 GATHER_PLAN = {
-    "start": ("gsz", "gsp2", "gsp3", "gssib", "qsz", "qsp3",),
-    "norm": ("gF", "gZ0", "ussib", "dsp2", "qsp2", "gZ1", "usp2", "osp3", "qF", "osz", "osp2", "qZ0", "qZ1", "gZ2", "usp3", "gP0", "oF", "dssib", "qZ2", "gT0", "usz", "qP0", "qP2", "uF", "qT0", "qT1", "gP2", "qP1", "gP1", "qT3", "oZ2", "gT1", "oZ0", "qssib", "ossib", "uT0", "oP0", "gT3", "token", "gT2", "oZ1", "qT2",),
-    "qkv": ("uZ2", "uZ0",),
-    ("k", 1): ("oP2", "oP1",),
-    ("v", 0): ("dF",),
-    ("v", 1): ("oT1",),
-    ("pair", 5): ("dsz",),
-    ("pair", 6): ("uP0",),
-    "other": ("oT0",),
-    ("more", 0): ("uZ1", "uP2", "oT3",),
-    ("more", 1): ("uP1", "oT2",),
-    ("more", 3): ("dsp3",),
-    ("more", 4): ("uT1",),
-    ("more", 5): ("dP1",),
-    ("more", 6): ("dZ0",),
-    "out": ("uT2", "dP0", "dZ2",),
-    "up": ("uT3",),
-    ("up", 0): ("dZ1",),
-    ("up", 1): ("dP2",),
-    ("up", 2): ("dT1",),
-    ("up", 4): ("dT0",),
-    ("up", 6): ("dT2",),
-    ("up", 7): ("dT3",),
+    "norm": {
+        0: (41, 110, 230, 100, 320, 140, 330, 0, 400, 51, 141, 10, 130, 150, 40, 42, 142, 62, 52, 50, 30, 151, 160, 60, 152, 999, 410, 63, 61, 430, 162, 161, 340,),
+    },
+    "qkv": {
+        0: (241, 163, 420, 240,),
+    },
+    "k": {
+        0: (210,),
+    },
+    "v": {
+        1: (350,),
+    },
+    "pair": {
+        2: (250, 342,),
+        6: (242, 251, 341,),
+        7: (352,),
+    },
+    "other": {
+        0: (252,),
+    },
+    "more": {
+        0: (351, 450,),
+        1: (360, 452, 260,),
+        2: (460,),
+        3: (261,),
+        4: (361, 262, 442,),
+        5: (440,),
+        6: (451, 263, 441,),
+    },
+    "out": {
+        0: (362,),
+    },
+    "to up": {
+        0: (363, 463,),
+    },
+    "up": {
+        0: (461,),
+        5: (462,),
+    },
+    "start": {
+        0: (300, 20, 120, 200, 310, 220,),
+    },
 }
 
 NEAR = ((1, 2, 3), (0, 2, 3), (1, 3, 0), (2, 1, 0))
 FAR = ((3, 2, 1), (3, 0, 2), (0, 1, 3), (0, 1, 2))
 
 SHARE_PLAN = {
-    ("du", 6): ("d31",),
-    ("up", 4): ("d30",),
-    ("up", 6): ("d21",),
-    "out": ("d32",),
-    ("more", 1): ("d20",),
-    ("more", 2): ("v30",),
-    ("more", 6): ("u31", "v20", "v31", "u32", "v32", "u30", "u21",),
-    ("more", 7): ("d22",),
-    "other": ("o30",),
-    ("pair", 1): ("o32",),
-    ("pair", 2): ("v22",),
-    ("pair", 3): ("v21", "u22",),
-    "half": ("u20",),
-    ("pair", 6): ("o31",),
-    "input": ("a30",),
-    "gains": ("a32", "a31", "a20", "o21", "a33", "b31",),
-    "end": ("a22", "a21", "b32", "b22", "b30", "d33", "o33", "b21", "b20", "o22", "dE", "g31", "u33", "o20", "oE", "aE", "b33", "g30", "g32", "g33", "g21", "dL", "uE", "v33", "oL", "aL", "bE", "g20", "g22", "uL", "vE", "bL", "gE", "vL", "gL",),
+    "du": {
+        4: (0,),
+    },
+    "up": {
+        0: (10,),
+    },
+    "norm": {
+        0: (1,),
+    },
+    "do": {
+        0: (2,),
+    },
+    "out": {
+        0: (100,),
+    },
+    "more": {
+        1: (101,),
+        5: (12,),
+        6: (111, 11,),
+    },
+    "pair": {
+        0: (110, 200,),
+        1: (202,),
+        3: (102,),
+        4: (212,),
+        5: (201, 211,),
+        6: (112,),
+    },
+    "half": {
+        0: (210,),
+    },
+    "input": {
+        0: (300, 302, 301, 3,),
+    },
+    "gains": {
+        0: (401, 103, 120, 312, 311, 402,),
+    },
+    "end": {
+        0: (310, 400, 500, 501, 502, 503, 411, 403, 303, 320, 412, 512, 410, 510, 203, 511, 20, 130, 220, 330, 420, 520, 30, 230, 430, 530,),
+    },
 }
 
 epsilon = 1e-05
@@ -172,11 +215,11 @@
         self.n_p2 = 2 * Z + 2
         self.n_p3 = self.n_p2 + Z
         self.n_sib = self.n_p3 + 2 * Z
-        self.n_own = self.n_sib + 4 * Z
+        self.n_own = self.n_sib + 2 * Z
 
     @staticmethod
     def sems(Z):
-        return 9 * Z + 3
+        return 7 * Z + 3
 
     def at(self, index):
         return self.full.at[pl.ds(pl.multiple_of(index * self.rows, self.rows), self.rows)]
@@ -227,10 +270,18 @@
         number = self.n_p3 + z * 2 + a2
         return self.copy(g.row_block(z, a2, g.i3, g.c), number, number, g.p3, src)
 
-    def sib_copy(self, z, a2, a3, src=None):
-        g = self.g
-        number = self.n_sib + g.block(z, a2, a3)
-        return self.copy(g.row_block(z, a2, a3, g.c), number, number, g.sib, src)
+    def sib_copy(self, z, xx, core):
+        rows = 2 * self.rows
+        spot = pl.ds(pl.multiple_of(((z * 2 + xx) * 2 + core) * rows, rows), rows)
+        number = self.n_sib + z * 2 + xx
+        return pltpu.make_async_remote_copy(
+            src_ref=self.full.at[spot],
+            dst_ref=self.full.at[spot],
+            send_sem=self.send.at[number],
+            recv_sem=self.recv.at[number],
+            device_id=self.g.sib,
+            device_id_type=MESH,
+        )
 
     def wait(self, number, index):
         self.copy(index, number, number, self.g.sib).wait_recv()
@@ -249,9 +300,6 @@
 
     def start_p3(self):
         self.p3_copy(self.g.z, self.g.i2, self.shard).start()
-
-    def start_sib(self):
-        self.sib_copy(self.g.z, self.g.i2, self.g.i3, self.shard).start()
         self.own_copy().start()
 
     def first(self):
@@ -260,7 +308,6 @@
         self.wait(self.n_p2 + g.z, g.row_block(g.z, o2, g.i3, g.c))
         when(self.by_z, lambda: self.each_z(lambda z: self.z_copy(True, z).start()))
         self.p3_copy(g.z, o2).start()
-        self.sib_copy(g.z, o2, g.i3).start()
 
     def relay(self, j, z, other):
         if j == self.g.Z - 2:
@@ -273,7 +320,6 @@
         self.relay(j, z, False)
         unless(self.by_z, lambda: self.p2_copy(z).start())
         self.p3_copy(z, g.i2).start()
-        self.sib_copy(z, g.i2, g.i3).start()
 
     def from_p2(self, j):
         g = self.g
@@ -283,29 +329,27 @@
         self.wait(number, g.row_block(z, o2, g.i3, g.c))
         when(self.by_z, lambda: self.relay(j, z, True))
         self.p3_copy(z, o2).start()
-        self.sib_copy(z, o2, g.i3).start()
 
     def from_p3(self, j):
         g = self.g
         z = g.near(j - 1) if j else g.z
         for a2 in (0, 1):
             self.wait(self.n_p3 + z * 2 + a2, g.row_block(z, a2, 1 - g.i3, g.c))
-            self.sib_copy(z, a2, 1 - g.i3).start()
+        if j == 0:
+            self.own_copy().wait()
+        for xx in (0, 1):
+            self.sib_copy(z, xx, g.c).start()
 
     def complete(self):
         g = self.g
         for z in range(g.Z):
             for xx in (0, 1):
-                for yy in (0, 1):
-                    number = self.n_sib + (z * 2 + xx) * 2 + yy
-                    self.wait(number, ((z * 2 + xx) * 2 + 1 - g.c) * 2 + yy)
-        self.own_copy().wait()
+                self.sib_copy(z, xx, 1 - g.c).wait_recv()
 
     def sent(self):
         g, src = self.g, self.shard
         self.p2_copy(g.z, src).wait_send()
         self.p3_copy(g.z, g.i2, src).wait_send()
-        self.sib_copy(g.z, g.i2, g.i3, src).wait_send()
         self.each_z(lambda z: self.z_copy(False, z, src).wait_send())
         when(self.by_z, lambda: self.each_z(lambda z: self.z_copy(True, z).wait_send()))
         end = g.near(g.Z - 2)
@@ -319,12 +363,10 @@
             z = g.above(k)
             unless(self.by_z, lambda: self.p2_copy(z).wait_send())
             self.p3_copy(z, g.i2).wait_send()
-            self.sib_copy(z, g.i2, g.i3).wait_send()
         for z in range(g.Z):
             self.p3_copy(z, 1 - g.i2).wait_send()
-            self.sib_copy(z, 1 - g.i2, g.i3).wait_send()
-            for a2 in (0, 1):
-                self.sib_copy(z, a2, 1 - g.i3).wait_send()
+            for xx in (0, 1):
+                self.sib_copy(z, xx, g.c).wait_send()
 
 
 class Share:
@@ -644,25 +686,23 @@
         device_id=g.device(g.z, g.x, g.c, 1 - y),
         device_id_type=MESH,
     )
-    named = {"g": gg, "q": gq, "o": go, "u": gu, "d": gd}
-
-    def serve(slot):
-        for step in GATHER_PLAN.get(slot, ()):
-            m, kind = named.get(step[0]), step[1]
-            if step == "token":
+    matrices = (gg, gq, go, gu, gd)
+
+    def serve(name, i=0):
+        for step in GATHER_PLAN.get(name, {}).get(i, ()):
+            if step == TOKENS:
                 pl.when(y == 0)(lambda: tok_copy.start())
-            elif kind == "s":
-                getattr(m, "start_" + step[2:])()
-            elif kind == "F":
-                m.first()
+                continue
+            m, kind, j = matrices[step // 100], step // 10 % 10, step % 10
+            if kind < 4:
+                (m.start_p2, m.start_p3, m.start_z, m.first)[kind]()
             else:
-                act = {"Z": m.from_z, "P": m.from_p2, "T": m.from_p3}[kind]
-                act(int(step[2:]))
+                (m.from_z, m.from_p2, m.from_p3)[kind - 4](j)
 
     def serve_at(name, t, count):
         for i in range(count):
-            if (name, i) in GATHER_PLAN:
-                pl.when(t == i)(functools.partial(serve, (name, i)))
+            if i in GATHER_PLAN.get(name, {}):
+                pl.when(t == i)(functools.partial(serve, name, i))
 
     g.barrier()
     serve("start")
@@ -834,7 +874,7 @@
     save(h, h_o)
     save(bt, bt_o)
 
-    serve("up")
+    serve("to up")
     gu.complete()
     tiles = Tiles(lambda t: wu_f.at[:, columns(t, 512)], wbuf, wsem)
     ups = act.shape[0]
@@ -1054,8 +1094,8 @@
 
     def dz_send(e, p):
         t = e * per + lax.div(p, 4)
-        spot = columns(lax.rem(p, 4), 128)
-        n = e * pairs + p
+        spot = columns(lax.div(lax.rem(p, 4), 2), 256)
+        n = e * (pairs // 2) + lax.div(p, 2)
         return to_sib(dz.at[t, :, spot], dzs.at[t, :, spot], zsend.at[n], zrecv.at[n])
 
     landing = (rec3, rec)
@@ -1078,13 +1118,9 @@
     s_d = Share(
         g, part, 0, landing, 0, 4, gsems[0], rsems[0], write_d, modes[3]
     )
-    s_u = [
-        Share(
-            g, part, 4 + 2 * i, landing, 4 + 2 * i, 2, gsems[1 + i], rsems[1 + i],
-            write_into(out_u, 2 * i * width), modes[2],
-        )
-        for i in (0, 1)
-    ]
+    s_u = Share(
+        g, part, 4, landing, 4, 4, gsems[1], rsems[1], write_into(out_u, 0), modes[2]
+    )
     s_o = Share(
         g, part, 8, landing, 8, 1, gsems[3], rsems[3], write_into(out_o, 0),
         modes[1],
@@ -1097,22 +1133,20 @@
         for i in (0, 1)
     ]
     s_g = Share(g, gpart, 0, (grec3, grec), 0, 1, gsems[6], rsems[6], write_g, False)
-    named = {"d": s_d, "u": s_u[0], "v": s_u[1], "o": s_o, "a": s_q[0], "b": s_q[1], "g": s_g}
-
-    def serve(slot):
-        for step in SHARE_PLAN.get(slot, ()):
-            s = named[step[0]]
-            if step[1] == "L":
-                s.last()
-            elif step[1] == "E":
-                s.sum_z()
+    groups = (s_d, s_u, s_o, s_q[0], s_q[1], s_g)
+
+    def serve(name, i=0):
+        for step in SHARE_PLAN.get(name, {}).get(i, ()):
+            s, kind, j = groups[step // 100], step // 10 % 10, step % 10
+            if kind < 2:
+                (s.stage3, s.stage2)[kind](j)
             else:
-                (s.stage3 if step[1] == "3" else s.stage2)(int(step[2]))
+                (s.sum_z, s.last)[kind - 2]()
 
     def serve_at(name, t, count):
         for i in range(count):
-            if (name, i) in SHARE_PLAN:
-                pl.when(t == i)(functools.partial(serve, (name, i)))
+            if i in SHARE_PLAN.get(name, {}):
+                pl.when(t == i)(functools.partial(serve, name, i))
 
     mraws = Tiles(lambda i: mraw_i.at[columns(i, 128), :], f1, tsems[9])
     araws = Tiles(lambda i: araw_i.at[columns(i, 128), :], f1, tsems[9])
@@ -1206,20 +1240,16 @@
     outs.first(per)
     bt_load.wait()
     bt_send.wait_recv()
-    for i in (0, 1):
-
-        @loop(ups // 2)
-        def _(t2):
-            t = t2 + i * (ups // 2)
-            serve_at("up", t, ups)
-            total = dot(bt[...].reshape(-1, rows), dz[t])
-            total += dot(bts[...].reshape(-1, rows), sib_du.get(t, ups))
-            part[4 + lax.div(t, per), :, :, columns(lax.rem(t, per), 512)] = (
-                total.astype(bf).reshape(4 * Z, 32, 512)
-            )
-
-        s_u[i].start_all()
-
+    @loop(ups)
+    def _(t):
+        serve_at("up", t, ups)
+        total = dot(bt[...].reshape(-1, rows), dz[t])
+        total += dot(bts[...].reshape(-1, rows), sib_du.get(t, ups))
+        part[4 + lax.div(t, per), :, :, columns(lax.rem(t, per), 512)] = (
+            total.astype(bf).reshape(4 * Z, 32, 512)
+        )
+
+    s_u.start_all()
     at_load.start()
 
     serve("norm")
@@ -1336,7 +1366,7 @@
         at_both = (at[...].reshape(-1, rows), ats[...].reshape(-1, rows))
 
         def ready(i):
-            for j in range(4):
+            for j in (1, 3):
                 dz_send(i, h * 4 + j).wait_recv()
 
         sib_dz = Tiles(lambda i: dzs.at[i * per + h], sbuf, tsems[5], ready)
@@ -1369,7 +1399,7 @@
     @pl.when(y == 0)
     def _():
         for p in range(pairs):
-            serve(("more", p))
+            serve("more", p)
         serve("other")
 
     @pl.when(y == 1)
@@ -1383,8 +1413,11 @@
                 spot, dq = attend(p, block, 0, rows, block == 0)
                 dz[lax.div(p, 4), spot, lanes(p)] = dq.astype(bf)
             keep(p, 0, 3 * per)
-            for e in (3, 4):
-                dz_send(e, p).start()
+
+            @pl.when(lax.rem(p, 2) == 1)
+            def _():
+                for e in (3, 4):
+                    dz_send(e, p).start()
 
         serve("other")
         keys.first(pairs)
@@ -1403,8 +1436,11 @@
             dq += jnp.where(y == 1, before, 0.0)
             dz[lax.div(p, 4), spot, lanes(p)] = dq.astype(bf)
         keep(p, first, per)
-        for e in range(3):
-            dz_send(e, p).start()
+
+        @pl.when(lax.rem(p, 2) == 1)
+        def _():
+            for e in range(3):
+                dz_send(e, p).start()
 
         @pl.when(p == pairs // 2 - 1)
         def _():
@@ -1461,10 +1497,10 @@
         gt_send(jnp.int32(i)).wait_send()
     for copy in (bt_send, ob_send, at_send, dg_send):
         copy.wait_send()
-    @loop(pairs)
-    def _(p):
+    @loop(pairs // 2)
+    def _(i):
         for e in range(3):
-            dz_send(e, p).wait_send()
+            dz_send(e, 2 * i + 1).wait_send()
 
     @pl.when(y == 0)
     def _():
@@ -1475,12 +1511,12 @@
         atx_send.wait_send()
         dnx_send.wait_send()
 
-        @loop(pairs)
-        def _(p):
+        @loop(pairs // 2)
+        def _(i):
             for e in (3, 4):
-                dz_send(e, p).wait_send()
-
-    for s in (s_d, s_u[0], s_u[1], s_o, s_q[0], s_q[1], s_g):
+                dz_send(e, 2 * i + 1).wait_send()
+
+    for s in (s_d, s_u, s_o, s_q[0], s_q[1], s_g):
         s.sent()
 
 

time: 303 us -> 303 us (level)
  no operation moved by 1% of the time
where the time goes in v6:
time: 303 us; the launch traced here: 302 us
  Pallas kernels  298 us (98%)
    pallas_call x1, Pallas kernels, backward(): pl.pallas_call(functools.partial(backward_kernel, dp_size, head_dim), out...  158 us
    pallas_call x1, Pallas kernels, forward(): pl.pallas_call(functools.partial(forward_kernel, dp_size, head_dim), out_...  136 us

profile of v6, /device:TPU:0, one launch (start us, length us, event | category | flops | bytes accessed | tf_op | source)
XLA Modules:
  0.0 301.7 jit_solution(3666762946673200642)
XLA Ops:
  0.6 0.8 copy.17
  1.4 0.6 pad.4.refs_2_
  2.0 136.3 %shard_map.153 = (bf16[512,1024]{1,0:T(8,128)(2,1)}, bf16[1024,3072]{1,0:T(8,128)(2,1)}, bf16[1024,1024]{1,0:T(8,128)(2,1)}, bf16[1024,4096]{1,0:T(8,128)(2,1)},...) custom-call(bf16[512,1024]{1,0:T(8,128)(2,1)} %refs_0_.3, ...), custom_call_target="tpu_custom_call" | custom-call | tf_op jit(solution)/shard_map/pallas_call | solution.py:1001
  138.3 157.6 %shard_map.154 = (bf16[512,1024]{1,0:T(8,128)(2,1)}, f32[32,3072]{1,0:T(8,128)}, f32[32,1024]{1,0:T(8,128)}, f32[32,4096]{1,0:T(8,128)}, f32[128,1024]{1,0:T(8,1...) custom-call(bf16[512,1024]{1,0:T(8,128)(2,1)} %refs_0_.3, ...), custom_call_target="tpu_custom_call" | custom-call | tf_op jit(solution)/shard_map/pallas_call | solution.py:1594
  295.8 4.5 %shard_map.155 = (bf16[512,1024]{1,0:T(8,128)(2,1)}, bf16[512,1024]{1,0:T(8,128)(2,1)}, f32[32,3072]{1,0:T(8,128)}, f32[32,1024]{1,0:T(8,128)}, f32[32,4096]{1,0...) custom-call(bf16[512,1024]{1,0:T(8,128)(2,1)} %get-tuple-element.33.refs_0_, ...), custom_call_target="tpu_custom_call" | custom-call | tf_op jit(solution)/shard_map/pallas_call | solution.py:1624
  300.3 1.4 copy.18

commit v7 on v6

--- a/solution.py
+++ b/solution.py
@@ -18,46 +18,44 @@
 TOKENS = 999
 GATHER_PLAN = {
     "norm": {
-        0: (41, 110, 230, 100, 320, 140, 330, 0, 400, 51, 141, 10, 130, 150, 40, 42, 142, 62, 52, 50, 30, 151, 160, 60, 152, 999, 410, 63, 61, 430, 162, 161, 340,),
+        0: (230, 210, 320, 10, 330, 110, 30, 130, 140, 141, 41, 150, 40, 142, 151, 152, 42, 52, 242, 50, 51, 420, 161, 310, 252, 240, 162, 60, 163, 999, 160, 61, 250, 63, 62, 340, 241, 342,),
     },
     "qkv": {
-        0: (241, 163, 420, 240,),
-    },
-    "k": {
-        0: (210,),
+        0: (430, 410,),
+    },
+    "q": {
+        1: (263,),
     },
     "v": {
+        0: (251,),
         1: (350,),
     },
     "pair": {
-        2: (250, 342,),
-        6: (242, 251, 341,),
-        7: (352,),
+        3: (360,),
+        4: (260,),
+        5: (352, 341,),
     },
     "other": {
-        0: (252,),
+        0: (440,),
     },
     "more": {
-        0: (351, 450,),
-        1: (360, 452, 260,),
-        2: (460,),
-        3: (261,),
-        4: (361, 262, 442,),
-        5: (440,),
-        6: (451, 263, 441,),
-    },
-    "out": {
-        0: (362,),
+        0: (351,),
+        2: (450, 261,),
+        3: (441, 460,),
+        4: (452,),
+        5: (262,),
+        7: (363, 442,),
     },
     "to up": {
-        0: (363, 463,),
+        0: (361, 451, 362,),
     },
     "up": {
-        0: (461,),
+        1: (461,),
+        3: (463,),
         5: (462,),
     },
     "start": {
-        0: (300, 20, 120, 200, 310, 220,),
+        0: (300, 400, 120, 20, 220, 200, 100, 0,),
     },
 }
 
@@ -66,44 +64,43 @@
 
 SHARE_PLAN = {
     "du": {
-        4: (0,),
+        3: (0,),
     },
     "up": {
-        0: (10,),
-    },
-    "norm": {
-        0: (1,),
-    },
-    "do": {
-        0: (2,),
+        3: (10,),
+        4: (1, 2,),
     },
     "out": {
         0: (100,),
     },
+    "mask": {
+        0: (12,),
+    },
     "more": {
         1: (101,),
-        5: (12,),
-        6: (111, 11,),
+    },
+    "other": {
+        0: (110,),
     },
     "pair": {
-        0: (110, 200,),
-        1: (202,),
-        3: (102,),
-        4: (212,),
-        5: (201, 211,),
-        6: (112,),
+        0: (200, 11,),
+        1: (102,),
+        2: (201,),
+        3: (210, 112, 202, 212,),
+        4: (111,),
+        6: (3,),
     },
     "half": {
-        0: (210,),
+        0: (211,),
     },
     "input": {
-        0: (300, 302, 301, 3,),
+        0: (301, 300,),
     },
     "gains": {
-        0: (401, 103, 120, 312, 311, 402,),
+        0: (302, 400, 312, 311, 401, 310,),
     },
     "end": {
-        0: (310, 400, 500, 501, 502, 503, 411, 403, 303, 320, 412, 512, 410, 510, 203, 511, 20, 130, 220, 330, 420, 520, 30, 230, 430, 530,),
+        0: (402, 303, 203, 412, 410, 500, 501, 502, 103, 220, 320, 403, 411, 510, 511, 512, 20, 120, 230, 330, 420, 503, 30, 130, 430, 520, 530,),
     },
 }
 
@@ -643,14 +640,14 @@
 
 
 def forward_kernel(dp_size, head_dim, *refs):
-    (tok, lens, gs, wq, wo, wu, wd, cosine, sine) = refs[:9]
+    (tok_i, lens, gs, wq, wo, wu, wd, cosine_i, sine_i) = refs[:9]
     (out, wq_f, wo_f, wu_f, wd_f, gain_o, q_o, k_o, v_o, ob_o, lse_o) = refs[9:20]
     (araw_o, h_o, mraw_o, bt_o, gt_o, gp_o, at_o, atx_o, tokx_o) = refs[20:29]
     (g_full, gain, tokx, a, ax, at, atx, q, k, v, vt, bias, ob, lse) = refs[29:43]
     (araw, h, mraw, b, bt, act, actt, gp, wbuf, dbuf) = refs[43:53]
     sems = refs[53:63]
     wsem, dsem, xsem, osem = refs[63:67]
-    o_own = refs[67]
+    o_own, tok, cosine, sine = refs[67:71]
     g = Place(dp_size)
     y = g.y
     rows, width = tok.shape
@@ -679,7 +676,7 @@
         saves.append(copy)
 
     tok_copy = pltpu.make_async_remote_copy(
-        src_ref=tok,
+        src_ref=tok_i,
         dst_ref=tokx,
         send_sem=xsem.at[0],
         recv_sem=xsem.at[1],
@@ -704,8 +701,14 @@
             if i in GATHER_PLAN.get(name, {}):
                 pl.when(t == i)(functools.partial(serve, name, i))
 
+    loads = [
+        pltpu.make_async_copy(src, dst, osem.at[16 + i])
+        for i, (src, dst) in enumerate(((tok_i, tok), (cosine_i, cosine), (sine_i, sine)))
+    ]
     g.barrier()
     serve("start")
+    for copy in loads:
+        copy.start()
     fill_bias(bias, lens, y * rows, rows)
     serve("norm")
     gg.complete()
@@ -722,11 +725,14 @@
             dst[spot, :] = value.astype(jnp.bfloat16)
             dst_t[:, spot] = jnp.transpose(value).astype(jnp.bfloat16)
 
+    loads[0].wait()
     first_norm(tok, a, at)
     save(at, at_o)
     serve("qkv")
     gq.complete()
 
+    loads[1].wait()
+    loads[2].wait()
     tiles = Tiles(lambda t: wq_f.at[:, columns(t, 512)], wbuf, wsem)
     per = width // 512
     first = pl.multiple_of(y * rows, rows)
@@ -996,14 +1002,15 @@
         pltpu.VMEM((3, 512, width), bf),
     ]
     scratch += [pltpu.SemaphoreType.DMA((Gather.sems(dp_size // 4),))] * 10
-    scratch += [pltpu.SemaphoreType.DMA((3,))] * 3 + [pltpu.SemaphoreType.DMA((16,))]
-    scratch += [pltpu.VMEM((pairs, 128, rows), f32)]
+    scratch += [pltpu.SemaphoreType.DMA((3,))] * 3 + [pltpu.SemaphoreType.DMA((19,))]
+    scratch += [pltpu.VMEM((pairs, 128, rows), f32), pltpu.VMEM((rows, width), bf)]
+    scratch += [pltpu.VMEM((row_len, 128), f32)] * 2
     return pl.pallas_call(
         functools.partial(forward_kernel, dp_size, head_dim),
         out_shape=outs,
-        in_specs=[vm, pl.BlockSpec(memory_space=pltpu.SMEM), vm]
+        in_specs=[any_spec, pl.BlockSpec(memory_space=pltpu.SMEM), vm]
         + [any_spec] * 4
-        + [vm, vm],
+        + [any_spec] * 2,
         out_specs=[vm] + [any_spec] * (len(outs) - 1),
         scratch_shapes=scratch,
         compiler_params=pltpu.CompilerParams(
@@ -1013,7 +1020,7 @@
 
 
 def backward_kernel(dp_size, head_dim, *refs):
-    (tok_i, dout, lens, gain, cosine_i, sine_i, wq, wo, wu, wd) = refs[:10]
+    (tok_i, dout_i, lens, gain, cosine_i, sine_i, wq, wo, wu, wd) = refs[:10]
     (q_i, k_i, v_i, ob_i, lse_i, araw_i, h_i, mraw_i, bt_i, gt_i, gp_i, at_i, atx_i, tokx_i) = refs[10:24]
     (dtok, out_q, out_o, out_u, out_d, out_g) = refs[24:30]
     (gts, dus, dzs) = refs[30:33]
@@ -1025,11 +1032,11 @@
     usend, urecv, gsend, grecv, zsend, zrecv, osend, orecv, lsem = refs[79:88]
     dnsem = refs[88]
     gsems, rsems = refs[89:96], refs[96:103]
-    tok, cosine, sine = refs[103:106]
+    tok, cosine, sine, dout = refs[103:107]
     at, xbuf, do, dnx, tokx = bt, gpbuf, dm, da, das
     g = Place(dp_size)
     Z, y, c = g.Z, g.y, g.c
-    rows, width = dout.shape
+    rows, width = dout_i.shape
     half = head_dim // 2
     pairs = width // 128
     scale = head_dim ** (-0.5)
@@ -1062,6 +1069,7 @@
     tok_load = load(tok_i, tok, 8)
     cosine_load = load(cosine_i, cosine, 9)
     sine_load = load(sine_i, sine, 10)
+    dout_load = load(dout_i, dout, 11)
 
     def gt_send(i):
         half_z = pl.ds(pl.multiple_of(lax.rem(i, 2) * 256, 256), 256)
@@ -1150,6 +1158,7 @@
 
     mraws = Tiles(lambda i: mraw_i.at[columns(i, 128), :], f1, tsems[9])
     araws = Tiles(lambda i: araw_i.at[columns(i, 128), :], f1, tsems[9])
+    dout_load.start()
     mraws.first(rows // 128)
     g.barrier()
     for j in range(Z):
@@ -1186,6 +1195,8 @@
 
     def gain_sum(index, term):
         dg[index : index + 1, :] += jnp.sum(term, axis=0, keepdims=True)
+
+    dout_load.wait()
 
     @loop(rows // 128)
     def _(i):
@@ -1300,12 +1311,16 @@
         copy.wait()
     blocks = rows // 256
 
-    def attend(p, block, base, count, fresh):
+    def turned_keys(p, base):
+        kk = kbuf[lax.rem(p, 2), pl.ds(base, rows), :]
+        return jnp.transpose(kk.astype(f32)).astype(bf)
+
+    def attend(p, block, base, count, fresh, kt):
         spot = slice(block * 256, block * 256 + 256)
         slot = lax.rem(p, 2)
         kk = kbuf[slot, pl.ds(base, count), :]
         vv = vbuf[slot, pl.ds(base, count), :]
-        kt = jnp.transpose(kk.astype(f32)).astype(bf)
+        kt = kt[:, :count]
         qs = split_heads(q[p, spot, :])
         do_pair = do[spot, columns(p, 128)]
         dos = split_heads(do_pair)
@@ -1409,8 +1424,9 @@
             serve_at("more", p, pairs)
             keys.get(p, pairs)
             values.get(p, pairs)
+            kt = turned_keys(p, 0)
             for block in range(blocks):
-                spot, dq = attend(p, block, 0, rows, block == 0)
+                spot, dq = attend(p, block, 0, rows, block == 0, kt)
                 dz[lax.div(p, 4), spot, lanes(p)] = dq.astype(bf)
             keep(p, 0, 3 * per)
 
@@ -1430,8 +1446,10 @@
         serve_at("pair", p, pairs)
         keys.get(p, pairs)
         values.get(p, pairs)
+        kt = turned_keys(p, first)
         for block in reversed(range(blocks)):
-            spot, dq = attend(p, block, first, (block + 1) * 256, block == blocks - 1)
+            count = (block + 1) * 256
+            spot, dq = attend(p, block, first, count, block == blocks - 1, kt)
             before = dz[lax.div(p, 4), spot, lanes(p)].astype(f32)
             dq += jnp.where(y == 1, before, 0.0)
             dz[lax.div(p, 4), spot, lanes(p)] = dq.astype(bf)
@@ -1588,13 +1606,14 @@
     dma = pltpu.SemaphoreType.DMA
     scratch += [dma((3,))] * 10
     scratch += [dma((ups,))] * 2 + [dma((2 * Z,))] * 2 + [dma((5 * pairs,))] * 2
-    scratch += [dma((11,))] * 2 + [dma((11,)), dma((2,))]
+    scratch += [dma((11,))] * 2 + [dma((12,)), dma((2,))]
     scratch += [dma((Share.sems(Z),))] * 14
     scratch += [pltpu.VMEM((rows, width), bf)] + [pltpu.VMEM((row_len, 128), f32)] * 2
+    scratch += [pltpu.VMEM((rows, width), bf)]
     return pl.pallas_call(
         functools.partial(backward_kernel, dp_size, head_dim),
         out_shape=outs,
-        in_specs=[any_spec, vm, smem, vm] + [any_spec] * 20,
+        in_specs=[any_spec, any_spec, smem, vm] + [any_spec] * 20,
         out_specs=[vm] * 6 + [any_spec] * 3,
         scratch_shapes=scratch,
         compiler_params=pltpu.CompilerParams(

time: 303 us -> 297 us (0.980); the launches traced: 302 us -> 293 us
  Pallas kernels: 298 us -> 289 us
    pallas_call x1, Pallas kernels: 136 us -> 131 us  [forward(): pl.pallas_call(functools.partial(forward_kernel, dp_size, head_dim), out_...]
    pallas_call x1, Pallas kernels: 158 us -> 154 us  [backward(): pl.pallas_call(functools.partial(backward_kernel, dp_size, head_dim), out...]
where the time goes in v7:
time: 297 us; the launch traced here: 293 us
  Pallas kernels  289 us (97%)
    pallas_call x1, Pallas kernels, backward(): pl.pallas_call(functools.partial(backward_kernel, dp_size, head_dim), out...  154 us
    pallas_call x1, Pallas kernels, forward(): pl.pallas_call(functools.partial(forward_kernel, dp_size, head_dim), out_...  131 us

profile of v7, /device:TPU:0, one launch (start us, length us, event | category | flops | bytes accessed | tf_op | source)
XLA Modules:
  0.0 292.5 jit_solution(9450629510512425612)
XLA Ops:
  0.6 0.8 copy.17
  1.4 0.6 pad.4.refs_2_
  2.0 130.5 %shard_map.153 = (bf16[512,1024]{1,0:T(8,128)(2,1)}, bf16[1024,3072]{1,0:T(8,128)(2,1)}, bf16[1024,1024]{1,0:T(8,128)(2,1)}, bf16[1024,4096]{1,0:T(8,128)(2,1)},...) custom-call(bf16[512,1024]{1,0:T(8,128)(2,1)} %refs_0_.3, ...), custom_call_target="tpu_custom_call" | custom-call | tf_op jit(solution)/shard_map/pallas_call | solution.py:1008
  132.5 154.1 %shard_map.154 = (bf16[512,1024]{1,0:T(8,128)(2,1)}, f32[32,3072]{1,0:T(8,128)}, f32[32,1024]{1,0:T(8,128)}, f32[32,4096]{1,0:T(8,128)}, f32[128,1024]{1,0:T(8,1...) custom-call(bf16[512,1024]{1,0:T(8,128)(2,1)} %refs_0_.3, ...), custom_call_target="tpu_custom_call" | custom-call | tf_op jit(solution)/shard_map/pallas_call | solution.py:1613
  286.7 4.5 %shard_map.155 = (bf16[512,1024]{1,0:T(8,128)(2,1)}, bf16[512,1024]{1,0:T(8,128)(2,1)}, f32[32,3072]{1,0:T(8,128)}, f32[32,1024]{1,0:T(8,128)}, f32[32,4096]{1,0...) custom-call(bf16[512,1024]{1,0:T(8,128)(2,1)} %get-tuple-element.33.refs_0_, ...), custom_call_target="tpu_custom_call" | custom-call | tf_op jit(solution)/shard_map/pallas_call | solution.py:1643
  291.2 1.4 copy.18

commit v8 on v7

--- a/solution.py
+++ b/solution.py
@@ -1626,26 +1626,35 @@
     n = len(arrays) - 1
 
     def kernel(*refs):
-        sources, targets, sems = refs[: n + 1], refs[n + 1 : 2 * n + 2], refs[-1]
-        copies = [
-            pltpu.make_async_copy(sources[i], targets[i], sems.at[i]) for i in range(n)
+        sources, targets = refs[: n + 1], refs[n + 1 : 2 * n + 2]
+        held, loaded, stored = refs[2 * n + 2 : 3 * n + 2], refs[-2], refs[-1]
+        loads = [
+            pltpu.make_async_copy(sources[i], held[i], loaded.at[i]) for i in range(n)
         ]
-        for copy in copies:
+        stores = [
+            pltpu.make_async_copy(held[i], targets[i], stored.at[i]) for i in range(n)
+        ]
+        for copy in loads:
             copy.start()
-        targets[n][...] = sources[n][:, : targets[n].shape[1]]
-        for copy in copies:
+        targets[n][...] = jnp.transpose(sources[n][...])[: targets[n].shape[0]]
+        for load, store in zip(loads, stores):
+            load.wait()
+            store.start()
+        for copy in stores:
             copy.wait()
 
     any_spec = pl.BlockSpec(memory_space=pl.ANY)
     vm = pl.BlockSpec(memory_space=pltpu.VMEM)
     shapes = [jax.ShapeDtypeStruct(a.shape, a.dtype) for a in arrays[:n]]
-    shapes.append(jax.ShapeDtypeStruct((arrays[n].shape[0], 4), arrays[n].dtype))
+    shapes.append(jax.ShapeDtypeStruct((4, arrays[n].shape[0]), arrays[n].dtype))
     return pl.pallas_call(
         kernel,
         out_shape=shapes,
-        in_specs=[vm] * (n + 1),
+        in_specs=[any_spec] * n + [vm],
         out_specs=[any_spec] * n + [vm],
-        scratch_shapes=[pltpu.SemaphoreType.DMA((n,))],
+        scratch_shapes=[pltpu.VMEM(a.shape, a.dtype) for a in arrays[:n]]
+        + [pltpu.SemaphoreType.DMA((n,))] * 2,
+        compiler_params=pltpu.CompilerParams(vmem_limit_bytes=16 * 2**20),
     )(*arrays)
 
 
@@ -1906,9 +1915,10 @@
         saved,
         (w_qkv, w_out, w_up, w_down),
     )[:6]
-    return tuple(
-        hand_on(output, d_tokens, grad_qkv, grad_out, grad_up, grad_down, grad_gains)
+    *results, gains_turned = hand_on(
+        output, d_tokens, grad_qkv, grad_out, grad_up, grad_down, grad_gains
     )
+    return (*results, gains_turned.T)
 
 
 def layer(mesh):

time: 297 us -> 302 us (1.017)
  local copies, waits for them, and re-layouts: 2.75 us -> 8.52 us
    unnamed x1 -> x15, local copies, waits for them, and re-layouts: 0.77 us -> 7.91 us
where the time goes in v8:
time: 302 us; the launch traced here: 297 us
  Pallas kernels  288 us (95%)
  local copies, waits for them, and re-layouts  8.52 us (3%)
    pallas_call x1, Pallas kernels, backward(): pl.pallas_call(functools.partial(backward_kernel, dp_size, head_dim), out...  154 us
    pallas_call x1, Pallas kernels, forward(): pl.pallas_call(functools.partial(forward_kernel, dp_size, head_dim), out_...  131 us
    unnamed x15, local copies, waits for them, and re-layouts  7.91 us

profile of v8, /device:TPU:0, one launch (start us, length us, event | category | flops | bytes accessed | tf_op | source)
XLA Modules:
  0.0 297.1 jit_solution(10546909007433112132)
XLA Ops:
  0.6 0.8 copy.17
  1.4 0.6 pad.4.refs_2_
  2.0 130.5 %shard_map.153 = (bf16[512,1024]{1,0:T(8,128)(2,1)}, bf16[1024,3072]{1,0:T(8,128)(2,1)}, bf16[1024,1024]{1,0:T(8,128)(2,1)}, bf16[1024,4096]{1,0:T(8,128)(2,1)},...) custom-call(bf16[512,1024]{1,0:T(8,128)(2,1)} %refs_0_.3, ...), custom_call_target="tpu_custom_call" | custom-call | tf_op jit(solution)/shard_map/pallas_call | solution.py:1008
  132.5 154.1 %shard_map.154 = (bf16[512,1024]{1,0:T(8,128)(2,1)}, f32[32,3072]{1,0:T(8,128)}, f32[32,1024]{1,0:T(8,128)}, f32[32,4096]{1,0:T(8,128)}, f32[128,1024]{1,0:T(8,1...) custom-call(bf16[512,1024]{1,0:T(8,128)(2,1)} %refs_0_.3, ...), custom_call_target="tpu_custom_call" | custom-call | tf_op jit(solution)/shard_map/pallas_call | solution.py:1613
  286.7 0.0 copy-start
  286.7 1.2 copy-done
  287.9 0.0 copy-start.1
  287.9 1.2 copy-done.1
  289.1 0.0 copy-start.2
  289.1 1.0 copy-done.2
  290.1 0.0 copy-start.3
  290.1 1.0 copy-done.3
  291.2 0.0 copy-start.4
  291.2 1.0 copy-done.4
  292.2 0.0 copy-start.5
  292.2 0.9 copy-done.5
  293.1 0.0 copy-start.6
  293.1 0.7 copy-done.6
  293.8 3.1 %shard_map.155 = (bf16[512,1024]{1,0:T(8,128)(2,1)}, bf16[512,1024]{1,0:T(8,128)(2,1)}, f32[32,3072]{1,0:T(8,128)}, f32[32,1024]{1,0:T(8,128)}, f32[32,4096]{1,0...) custom-call(bf16[512,1024]{1,0:T(8,128)(2,1)S(1)} %copy-done, bf16[512,1024]{1,0:T(8,128)(2,1)S(1)} %copy-done.1, ...), custom_call_target="tpu_custom_call" | custom-call | tf_op jit(solution)/shard_map/pallas_call | solution.py:1650
Async XLA Ops:
  286.7 1.2 copy-start
  287.9 1.2 copy-start.1
  289.1 1.0 copy-start.2
  290.1 1.0 copy-start.3
  291.2 1.0 copy-start.4
  292.2 0.9 copy-start.5
  293.1 0.7 copy-start.6
